TPU v7x, 32 devices: a whole 2x2x4 slice. The times are simulated.
32 devices in a mesh: expert: 4 (over y, x), dp: 8 (over z, core).
Axes of the slice: x: 2, y: 2, z: 4, core: 2. Of those that a mesh axis runs over, the one named last changes fastest.
Arguments:
- residual_in: bfloat16 [4096, 2048], P(('expert', 'dp')), may hold values from -6 to 6
- cotangent: bfloat16 [4096, 2048], P(('expert', 'dp')), may hold values from -6 to 6
- lengths: int32 [4], P('expert'), may hold values from 512 to 1024, as said below
- routes: int32 [4096, 8], P(('expert', 'dp')), may hold values from 0 to 15, all different within a row; in each aligned block of 128 rows (0 to 127, 128 to 255, ...) at most 128 rows name the same one
- attn_qkv: float32 [3, 2048, 2048], P(None, ('expert', 'dp')), may hold values from -0.125 to 0.125
- attn_out: float32 [2048, 2048], P(('expert', 'dp')), may hold values from -2 to 2
- gains: float32 [4, 2048], P(None, ('expert', 'dp')), may hold values from 0.5 to 1.5
- router: float32 [2048, 16], P(('expert', 'dp')), may hold values from -0.0625 to 0.0625
- expert_in: float32 [2048, 16, 2, 1024], P('dp', 'expert'), may hold values from -0.125 to 0.125
- expert_down: float32 [2048, 16, 1024], P('dp', 'expert'), may hold values from -0.5 to 0.5
Outputs:
- output: float32 [4096, 2048], P(('expert', 'dp'))
- grad_input: float32 [4096, 2048], P(('expert', 'dp'))
- grad_qkv: float32 [3, 2048, 2048], P(None, ('expert', 'dp'))
- grad_out: float32 [2048, 2048], P(('expert', 'dp'))
- grad_gains: float32 [4, 2048], P(None, ('expert', 'dp'))
- grad_router: float32 [2048, 16], P(('expert', 'dp'))
- grad_expert_in: float32 [2048, 16, 2, 1024], P('dp', 'expert')
- grad_expert_down: float32 [2048, 16, 1024], P('dp', 'expert')
Inputs may be any that keep to these rules, and one draw needn't show every extreme that they name: `routes`: each token names 8 different experts. Among the 128 tokens of one device no expert is named by more than 128 tokens, and in every draw some expert is named by exactly 128 tokens of some device. `lengths`: in every draw some sequence is full.
All inputs are finite; a program needn't handle non-finite values.
Results may differ from a plain program's by a relative error of at most 0.019.
The roundings to bfloat16 on the way count: a program that leaves them out, or rounds other values in their place, can miss the bound.
Values may be sent and summed in bfloat16 or wider, within the bound.
A program may use at most 512 MiB of HBM per device.

v0:
```python
import jax
import jax.numpy as jnp
from jax import lax
from jax.sharding import PartitionSpec as P

HEADS = 16
HD = 128


epsilon = 1e-05
rope_base = 10000.0
masked_score = -1000000000.0


def rms_scale(values):
    return lax.rsqrt(jnp.mean(values * values, axis=-1, keepdims=True) + epsilon)


def angle_tables(positions):
    frequency = rope_base ** (-2.0 * jnp.arange(HD // 2, dtype=jnp.float32) / HD)
    angles = positions.astype(jnp.float32)[:, None] * frequency[None, :]
    return (jnp.cos(angles), jnp.sin(angles))


def rotate(values, cosine, sine_table):
    row_count = values.shape[0]
    shaped = values.reshape(row_count, HEADS, 2, HD // 2)
    first_half = shaped[:, :, 0, :]
    second_half = shaped[:, :, 1, :]
    cos_rows = cosine[:, None, :]
    sin_rows = sine_table[:, None, :]
    turned = jnp.stack(
        [
            first_half * cos_rows - second_half * sin_rows,
            second_half * cos_rows + first_half * sin_rows,
        ],
        axis=2,
    )
    return turned.reshape(row_count, HEADS * HD)


def rms_back(grad_rows, normed, scale, gain):
    grad_normed = grad_rows * gain
    inner = jnp.mean(grad_normed * normed, axis=-1, keepdims=True)
    return (scale * grad_normed - normed * scale * inner, jnp.sum(grad_rows * normed, axis=0))


def slot_index(route_rows, experts, capacity):
    flat_routes = route_rows.reshape(-1)
    onehot = (flat_routes[:, None] == jnp.arange(experts, dtype=jnp.int32)[None, :]).astype(
        jnp.int32
    )
    rank_rows = jnp.sum((jnp.cumsum(onehot, axis=0) - onehot) * onehot, axis=1)
    return flat_routes * capacity + rank_rows


def head_scores(query_rot, key_all, key_live):
    row_count = query_rot.shape[0]
    query_heads = query_rot.reshape(row_count, HEADS, HD)
    key_heads = key_all.reshape(key_all.shape[0], HEADS, HD)
    raw_scores = jnp.einsum(
        "qhd,khd->hqk", query_heads, key_heads, preferred_element_type=jnp.float32
    ) * HD ** (-0.5)
    return jnp.where(key_live[None, None, :], raw_scores, masked_score)


def to_owners(buffer):
    return lax.all_to_all(buffer, "expert", split_axis=0, concat_axis=0, tiled=True)


def from_owners(buffer):
    return lax.all_to_all(buffer, "expert", split_axis=0, concat_axis=0, tiled=True)


def shards(
    residual_in,
    cotangent,
    lengths,
    routes,
    attn_qkv,
    attn_out,
    gains,
    router,
    expert_in,
    expert_down,
):
    tok_rows, model_width = residual_in.shape
    top_count = routes.shape[1]
    owners = lax.axis_size("expert")
    local_experts = expert_in.shape[1]
    experts = local_experts * owners
    capacity = tok_rows * top_count * 2 // experts
    local_slots = local_experts * capacity
    seq_rows = tok_rows * lax.axis_size("dp")
    low_type = jnp.bfloat16
    high_type = jnp.float32
    score_scale = HD ** (-0.5)
    qkv_weights, out_weight, gain_low, router_weight = (
        lax.all_gather(attn_qkv.astype(low_type), ("expert", "dp"), axis=1, tiled=True),
        lax.all_gather(attn_out.astype(low_type), ("expert", "dp"), axis=0, tiled=True),
        lax.all_gather(gains.astype(low_type), ("expert", "dp"), axis=1, tiled=True),
        lax.all_gather(router.astype(low_type), ("expert", "dp"), axis=0, tiled=True),
    )
    gain_rows = gain_low.astype(high_type)
    input_rows = residual_in.astype(high_type)
    scale_in = rms_scale(input_rows)
    normed_in_f = input_rows * scale_in
    normed_in = (normed_in_f * gain_rows[0]).astype(low_type)
    query_raw = jnp.dot(normed_in, qkv_weights[0], preferred_element_type=high_type)
    key_raw = jnp.dot(normed_in, qkv_weights[1], preferred_element_type=high_type)
    value_rows = jnp.dot(normed_in, qkv_weights[2], preferred_element_type=high_type).astype(
        low_type
    )
    positions = lax.axis_index("dp") * tok_rows + jnp.arange(tok_rows, dtype=jnp.int32)
    length_now = lengths[0]
    live_rows = (positions < length_now).astype(high_type)[:, None]
    key_live = jnp.arange(seq_rows, dtype=jnp.int32) < length_now
    cosine, sine_table = angle_tables(positions)
    query_scale = rms_scale(query_raw)
    query_normed = query_raw * query_scale
    query_rot = rotate(query_normed * gain_rows[1], cosine, sine_table).astype(low_type)
    key_scale = rms_scale(key_raw)
    key_normed = key_raw * key_scale
    key_rot = rotate(key_normed * gain_rows[2], cosine, sine_table).astype(low_type)
    key_all = lax.all_gather(key_rot, "dp", axis=0, tiled=True)
    value_all = lax.all_gather(value_rows, "dp", axis=0, tiled=True)
    scores = head_scores(query_rot, key_all, key_live)
    top_score = jnp.max(scores, axis=-1, keepdims=True)
    exp_scores = jnp.exp(scores - top_score)
    row_total = jnp.sum(exp_scores, axis=-1, keepdims=True)
    weights_low = (exp_scores / row_total).astype(low_type)
    log_total = top_score + jnp.log(row_total)
    value_heads = value_all.reshape(seq_rows, HEADS, HD)
    attended = jnp.einsum(
        "hqk,khd->qhd", weights_low, value_heads, preferred_element_type=high_type
    )
    attended = attended.reshape(tok_rows, model_width).astype(low_type)
    branch = jnp.dot(attended, out_weight, preferred_element_type=high_type)
    middle = input_rows + live_rows * branch
    scale_mid = rms_scale(middle)
    normed_mid_f = middle * scale_mid
    normed_mid = (normed_mid_f * gain_rows[3]).astype(low_type)
    logits = jnp.dot(normed_mid, router_weight, preferred_element_type=high_type)
    selector = (routes[:, :, None] == jnp.arange(experts, dtype=jnp.int32)[None, None, :]).astype(
        high_type
    )
    chosen = jnp.einsum("te,tje->tj", logits, selector)
    gate_weights = jax.nn.softmax(chosen, axis=-1)
    slot_rows = slot_index(routes, experts, capacity)
    token_of = jnp.arange(slot_rows.shape[0], dtype=jnp.int32) // top_count
    send_rows = (
        jnp.zeros((experts * capacity, model_width), low_type)
        .at[slot_rows]
        .set(normed_mid[token_of])
    )
    rows_recv = lax.all_to_all(
        send_rows.reshape(owners, local_slots, model_width),
        "expert",
        split_axis=0,
        concat_axis=0,
        tiled=True,
    )
    rows_recv = rows_recv.reshape(owners, local_experts, capacity, model_width)
    weights_in, weights_down = (
        lax.all_gather(expert_in.astype(low_type), "dp", axis=0, tiled=True),
        lax.all_gather(expert_down.astype(low_type), "dp", axis=0, tiled=True),
    )
    both_parts = jnp.einsum(
        "sxmd,dxkf->sxmkf", rows_recv, weights_in, preferred_element_type=high_type
    )
    gate_part = both_parts[:, :, :, 0, :]
    up_part = both_parts[:, :, :, 1, :]
    hidden = (jax.nn.silu(gate_part) * up_part).astype(low_type)
    produced = jnp.einsum(
        "sxmf,dxf->sxmd", hidden, weights_down, preferred_element_type=high_type
    ).astype(low_type)
    returned = from_owners(produced.reshape(owners, local_slots, model_width))
    returned = returned.reshape(experts * capacity, model_width)
    picked = returned[slot_rows].reshape(tok_rows, top_count, model_width).astype(high_type)
    combined = jnp.sum(gate_weights[:, :, None] * picked, axis=1)
    output = middle + live_rows * combined
    grad_rows = cotangent.astype(high_type)
    grad_comb = live_rows * grad_rows
    grad_gates = jnp.einsum("tjd,td->tj", picked, grad_comb)
    grad_chosen = gate_weights * (
        grad_gates - jnp.sum(gate_weights * grad_gates, axis=-1, keepdims=True)
    )
    grad_logits = jnp.einsum("tj,tje->te", grad_chosen, selector).astype(low_type)
    grad_send = (
        (gate_weights[:, :, None] * grad_comb[:, None, :]).astype(low_type).reshape(-1, model_width)
    )
    grad_buffer = (
        jnp.zeros((experts * capacity, model_width), low_type).at[slot_rows].set(grad_send)
    )
    grad_recv = to_owners(grad_buffer.reshape(owners, local_slots, model_width))
    grad_recv = grad_recv.reshape(owners, local_experts, capacity, model_width)
    grad_hidden = jnp.einsum(
        "sxmd,dxf->sxmf", grad_recv, weights_down, preferred_element_type=high_type
    )
    sigma_gate = jax.nn.sigmoid(gate_part)
    grad_gate = grad_hidden * up_part * sigma_gate * (1.0 + gate_part * (1.0 - sigma_gate))
    grad_up = grad_hidden * gate_part * sigma_gate
    grad_both = jnp.stack([grad_gate, grad_up], axis=3).astype(low_type)
    grad_rows_out = jnp.einsum(
        "sxmkf,dxkf->sxmd", grad_both, weights_in, preferred_element_type=high_type
    ).astype(low_type)
    grad_back = from_owners(grad_rows_out.reshape(owners, local_slots, model_width))
    grad_back = grad_back.reshape(experts * capacity, model_width)
    grad_mid_norm = jnp.sum(
        grad_back[slot_rows].reshape(tok_rows, top_count, model_width).astype(high_type), axis=1
    )
    grad_mid_norm = grad_mid_norm + jnp.dot(
        grad_logits, router_weight.T, preferred_element_type=high_type
    )
    grad_router = jnp.dot(normed_mid.T, grad_logits, preferred_element_type=high_type)
    row_piece = rows_recv
    grad_expert_in = lax.psum_scatter(
        jnp.einsum(
            "sxmd,sxmkf->dxkf", row_piece, grad_both, preferred_element_type=high_type
        ).astype(jnp.bfloat16),
        "dp",
        scatter_dimension=0,
        tiled=True,
    ).astype(jnp.float32)
    row_piece = grad_recv
    grad_expert_down = lax.psum_scatter(
        jnp.einsum("sxmd,sxmf->dxf", row_piece, hidden, preferred_element_type=high_type).astype(
            jnp.bfloat16
        ),
        "dp",
        scatter_dimension=0,
        tiled=True,
    ).astype(jnp.float32)
    grad_mid_rows, grad_gain_mid = rms_back(grad_mid_norm, normed_mid_f, scale_mid, gain_rows[3])
    grad_middle = grad_rows + grad_mid_rows
    grad_branch = (live_rows * grad_middle).astype(low_type)
    grad_out_weight = jnp.dot(attended.T, grad_branch, preferred_element_type=high_type)
    grad_attended = jnp.dot(grad_branch, out_weight.T, preferred_element_type=high_type).astype(
        low_type
    )
    scores = head_scores(query_rot, key_all, key_live)
    probs_full = jnp.exp(scores - log_total)
    grad_heads = grad_attended.reshape(tok_rows, HEADS, HD)
    value_heads = value_all.reshape(seq_rows, HEADS, HD)
    key_heads = key_all.reshape(seq_rows, HEADS, HD)
    query_heads = query_rot.reshape(tok_rows, HEADS, HD)
    grad_probs = jnp.einsum(
        "qhd,khd->hqk", grad_heads, value_heads, preferred_element_type=high_type
    )
    inner_rows = jnp.sum(probs_full * grad_probs, axis=-1, keepdims=True)
    grad_scores = (probs_full * (grad_probs - inner_rows)).astype(low_type)
    grad_query = (
        jnp.einsum(
            "hqk,khd->qhd", grad_scores, key_heads, preferred_element_type=high_type
        ).reshape(tok_rows, model_width)
        * score_scale
    )
    grad_key_part = (
        jnp.einsum(
            "hqk,qhd->khd", grad_scores, query_heads, preferred_element_type=high_type
        ).reshape(seq_rows, model_width)
        * score_scale
    )
    grad_value_part = jnp.einsum(
        "hqk,qhd->khd", probs_full.astype(low_type), grad_heads, preferred_element_type=high_type
    ).reshape(seq_rows, model_width)
    grad_key_sum, grad_value_sum = (
        lax.psum_scatter(
            grad_key_part.astype(jnp.bfloat16), "dp", scatter_dimension=0, tiled=True
        ).astype(jnp.float32),
        lax.psum_scatter(
            grad_value_part.astype(jnp.bfloat16), "dp", scatter_dimension=0, tiled=True
        ).astype(jnp.float32),
    )
    grad_value = grad_value_sum.astype(low_type)
    grad_key_raw, grad_key_gain = rms_back(
        rotate(grad_key_sum, cosine, -sine_table), key_normed, key_scale, gain_rows[2]
    )
    grad_query_raw, grad_query_gain = rms_back(
        rotate(grad_query, cosine, -sine_table), query_normed, query_scale, gain_rows[1]
    )
    grad_key_raw = grad_key_raw.astype(low_type)
    grad_query_raw = grad_query_raw.astype(low_type)
    grad_norm_in = jnp.dot(grad_query_raw, qkv_weights[0].T, preferred_element_type=high_type)
    grad_norm_in = grad_norm_in + jnp.dot(
        grad_key_raw, qkv_weights[1].T, preferred_element_type=high_type
    )
    grad_norm_in = grad_norm_in + jnp.dot(
        grad_value, qkv_weights[2].T, preferred_element_type=high_type
    )
    grad_qkv_local = jnp.stack(
        [
            jnp.dot(normed_in.T, grad_query_raw, preferred_element_type=high_type),
            jnp.dot(normed_in.T, grad_key_raw, preferred_element_type=high_type),
            jnp.dot(normed_in.T, grad_value, preferred_element_type=high_type),
        ]
    )
    grad_in_rows, grad_gain_in = rms_back(grad_norm_in, normed_in_f, scale_in, gain_rows[0])
    grad_input = grad_middle + grad_in_rows
    grad_gains_local = jnp.stack([grad_gain_in, grad_query_gain, grad_key_gain, grad_gain_mid])
    summed = (
        lax.psum_scatter(grad_qkv_local, ("expert", "dp"), scatter_dimension=1, tiled=True),
        lax.psum_scatter(grad_out_weight, ("expert", "dp"), scatter_dimension=0, tiled=True),
        lax.psum_scatter(grad_gains_local, ("expert", "dp"), scatter_dimension=1, tiled=True),
        lax.psum_scatter(grad_router, ("expert", "dp"), scatter_dimension=0, tiled=True),
    )
    return (
        output,
        grad_input,
        summed[0],
        summed[1],
        summed[2],
        summed[3],
        grad_expert_in,
        grad_expert_down,
    )


def solution(mesh):
    placed = (
        P(("expert", "dp"), None),
        P(("expert", "dp"), None),
        P("expert"),
        P(("expert", "dp"), None),
        P(None, ("expert", "dp"), None),
        P(("expert", "dp"), None),
        P(None, ("expert", "dp")),
        P(("expert", "dp"), None),
        P("dp", "expert", None, None),
        P("dp", "expert", None),
    )
    return jax.shard_map(
        shards,
        mesh=mesh,
        in_specs=placed,
        out_specs=(
            P(("expert", "dp"), None),
            P(("expert", "dp"), None),
            P(None, ("expert", "dp"), None),
            P(("expert", "dp"), None),
            P(None, ("expert", "dp")),
            P(("expert", "dp"), None),
            P("dp", "expert", None, None),
            P("dp", "expert", None),
        ),
        check_vma=False,
    )
```

profile of v0, /device:TPU:0, one launch (start us, length us, event | category | flops | bytes accessed | tf_op | source)
XLA Modules:
  0.0 2858.2 jit_solution(14464580669200395085)
XLA Ops:
  10.4 43.5 %all-gather = bf16[32,64,4]{1,2,0:T(4,128)(2,1)S(1)} all-gather(bf16[1,64,4]{1,2,0:T(4,128)(2,1)S(1)} %convert_bitcast_fusion.2), channel_id=1, replica_groups=mesh['expert'=4,'dp'=8] {'expert','dp'}, dimensions={0}, use_global_device_ids=true | all-gather | bytes 16896 | tf_op jit(solution)/shard_map/all_gather | solution.py:101
  56.1 113.0 %all-gather.9.cloned.1.call-done = bf16[3,2048,2048]{2,1,0:T(8,128)(2,1)} async-done(((bf16[3,64,2048]{2,1,0:T(8,128)(2,1)}), bf16[3,2048,2048]{2,1,0:T(8,128)(2,1)}) %all-gather.9.cloned.1.call-update) | async-done | bytes 25165840 | tf_op jit(solution)/shard_map/all_gather | solution.py:99
  169.0 5.0 multiply_reduce_fusion.10
  175.5 4.8 multiply_reduce_fusion.9
  185.3 5.5 fusion.64
  191.7 10.0 copy.212
  201.9 5.8 copy.213
  208.7 4.5 reduce-window.6
  214.1 17.3 all-gather.13.cloned.1.call-done
  240.7 38.2 %all-gather.11.cloned.1.call-done = bf16[1024,2048]{1,0:T(8,128)(2,1)} async-done(((bf16[128,2048]{1,0:T(8,128)(2,1)}), bf16[1024,2048]{1,0:T(8,128)(2,1)}) %all-gather.11.cloned.1.call-update) | async-done | bytes 4194320 | tf_op jit(solution)/shard_map/all_gather | solution.py:126
  278.9 7.7 fusion.69
  286.7 71.8 %all-gather.15.cloned.1.call-done = bf16[2048,2048]{1,0:T(8,128)(2,1)} async-done(((bf16[64,2048]{1,0:T(8,128)(2,1)}), bf16[2048,2048]{1,0:T(8,128)(2,1)}) %all-gather.15.cloned.1.call-update) | async-done | bytes 8388624 | tf_op jit(solution)/shard_map/all_gather | solution.py:100
  358.4 4.8 multiply_reduce_fusion.8
  364.4 25.4 scatter_custom_fusion
  389.8 5.6 all-to-all-start
  395.4 252.3 %all-gather.17.cloned.1.call-done = bf16[2048,4,2,1024]{3,0,2,1:T(8,128)(2,1)} async-done(((bf16[256,4,2,1024]{3,0,2,1:T(8,128)(2,1)}), bf16[2048,4,2,1024]{3,0,2,1:T(8,128)(2,1)}) %all-gather.17.cloned.1.call-update) | async-done | bytes 33554448 | tf_op jit(solution)/shard_map/all_gather | solution.py:165
  647.7 26.5 fusion.10
  674.2 9.1 multiply_convert_fusion.2
  683.3 115.2 %all-gather.19.cloned.1.call-done = bf16[2048,4,1024]{2,0,1:T(8,128)(2,1)} async-done(((bf16[256,4,1024]{2,0,1:T(8,128)(2,1)}), bf16[2048,4,1024]{2,0,1:T(8,128)(2,1)}) %all-gather.19.cloned.1.call-update) | async-done | bytes 16777232 | tf_op jit(solution)/shard_map/all_gather | solution.py:166
  798.5 15.8 convert_bitcast_fusion
  814.3 8.4 copy.124
  822.6 5.8 all-to-all-start.1
  828.5 40.6 %all-gather.1 = bf16[32,64,16]{1,2,0:T(8,128)(2,1)S(1)} all-gather(bf16[1,64,16]{1,2,0:T(8,128)(2,1)S(1)} %convert_bitcast_fusion.1), channel_id=1, replica_groups=mesh['expert'=4,'dp'=8] {'expert','dp'}, dimensions={0}, use_global_device_ids=true | all-gather | bytes 67584 | tf_op jit(solution)/shard_map/all_gather | solution.py:102
  870.5 51.7 %all-to-all-done.1 = bf16[4,512,2048]{2,1,0:T(8,128)(2,1)} async-done(((bf16[4,512,2048]{2,1,0:T(8,128)(2,1)}), bf16[4,512,2048]{2,1,0:T(8,128)(2,1)}, u32[]{:S(2)}, u32[]{:S(2)}) %all-to-all-start.1) | async-done | bytes 8388640 | tf_op jit(solution)/shard_map/all_to_all | solution.py:72
  922.2 13.3 gather_fusion
  935.5 4.9 fusion.44
  940.7 11.7 scatter_custom_fusion.1
  952.4 100.6 %all_to_all.20 = bf16[4,512,2048]{2,1,0:T(8,128)(2,1)} all-to-all(bf16[4,512,2048]{2,1,0:T(8,128)(2,1)} %bitcast.272), channel_id=1, replica_groups=mesh['expert'=4,'dp'=8] {'expert'}, dimensions={0} | all-to-all | bytes 16777216 | tf_op jit(solution)/shard_map/all_to_all | solution.py:68
  1052.9 22.5 fusion.54
  1075.5 25.1 fusion.3
  1100.6 8.3 copy.218
  1108.9 8.3 copy.127
  1117.2 5.8 all-to-all-start.3
  1123.7 7.5 multiply_reduce_fusion.1
  1131.1 82.8 %all-to-all-done.3 = bf16[4,512,2048]{2,1,0:T(8,128)(2,1)} async-done(((bf16[4,512,2048]{2,1,0:T(8,128)(2,1)}), bf16[4,512,2048]{2,1,0:T(8,128)(2,1)}, u32[]{:S(2)}, u32[]{:S(2)}) %all-to-all-start.3) | async-done | bytes 8388640 | tf_op jit(solution)/shard_map/all_to_all | solution.py:72
  1213.9 13.4 gather_fusion.1
  1227.3 5.1 convert_reduce_fusion
  1234.4 6.3 convolution_convert_fusion
  1241.0 8.0 multiply_reduce_fusion
  1248.9 5.1 multiply_convert_fusion.1
  1259.3 6.5 copy.167
  1265.9 7.9 fusion.58
  1273.8 6.5 copy.169
  1281.8 5.8 convolution_multiply_fusion.1
  1287.6 25.6 reduce-scatter.25.cloned.1.call-done
  1330.5 6.4 fusion.27
  1336.9 6.4 fusion.61
  1343.4 20.9 reduce-scatter.27.cloned.1.call-done
  1364.3 7.5 fusion.77
  1373.4 16.4 fusion.9
  1389.9 25.6 fusion
  1416.5 8.1 fusion.99
  1424.9 8.2 convolution_bitcast_fusion.1
  1433.1 8.2 convolution_bitcast_fusion.2
  1441.3 8.2 convolution_bitcast_fusion
  1449.5 35.7 %pad_maximum_fusion = f32[3,2048,2048]{2,1,0:T(8,128)} fusion(f32[1,2048,2048]{2,1,0:T(8,128)} %convolution_bitcast_fusion, f32[1,2048,2048]{2,1,0:T(8,128)} %convolution_bitcast_fusion.1, f32[1,2048,2048]{2,1,0:T(8,128)} %convolution_bitcast_fusion.2), kind=kLoop, calls=%fused_computation.6 | loop fusion | flops 25165824 | bytes 100663296 | tf_op jit(solution)/shard_map/stack | solution.py:291
  1485.2 14.4 reduce-scatter.31.cloned.1.call-done
  1502.3 131.5 %reduce-scatter.29.cloned.1.call-done = f32[64,4]{1,0:T(8,128)} async-done(((f32[2048,4]{1,0:T(8,128)}), f32[64,4]{1,0:T(8,128)}) %reduce-scatter.29.cloned.1.call-update) | async-done | bytes 1040
  1635.2 166.0 %reduce-scatter.23.cloned.1.call-done = bf16[256,4,1024]{0,2,1:T(8,128)(2,1)} async-done(((bf16[2048,4,1024]{0,2,1:T(8,128)(2,1)}), bf16[256,4,1024]{0,2,1:T(8,128)(2,1)}) %reduce-scatter.23.cloned.1.call-update) | async-done | bytes 2097168 | tf_op jit(solution)/shard_map/reduce_scatter | solution.py:226
  1801.2 4.8 copy.140
  1805.9 321.4 %reduce-scatter.21.cloned.1.call-done = bf16[256,4,2,1024]{0,3,2,1:T(8,128)(2,1)} async-done(((bf16[2048,4,2,1024]{0,3,2,1:T(8,128)(2,1)}), bf16[256,4,2,1024]{0,3,2,1:T(8,128)(2,1)}) %reduce-scatter.21.cloned.1.call-update) | async-done | bytes 4194320 | tf_op jit(solution)/shard_map/reduce_scatter | solution.py:217
  2127.3 11.7 copy.139
  2139.0 176.3 %reduce-scatter.19.cloned.1.call-done = f32[64,2048]{1,0:T(8,128)} async-done(((f32[2048,2048]{1,0:T(8,128)}), f32[64,2048]{1,0:T(8,128)}) %reduce-scatter.19.cloned.1.call-update) | async-done | bytes 524304 | tf_op jit(solution)/shard_map/reduce_scatter | solution.py:303
  2315.3 536.1 %reduce-scatter.17.cloned.1.call-done = f32[3,64,2048]{2,1,0:T(8,128)} async-done(((f32[3,2048,2048]{2,1,0:T(8,128)}), f32[3,64,2048]{2,1,0:T(8,128)}) %reduce-scatter.17.cloned.1.call-update) | async-done | bytes 1572880 | tf_op jit(solution)/shard_map/reduce_scatter | solution.py:302
  (209 shorter events, 59.9 us)
Async XLA Ops:
  7.2 161.9 %all-gather.9.cloned.1.call-start = ((), (), s32[]{:S(2)}) async-start(), calls=%async_computation.12 | async-start | bytes 25952256 | tf_op jit(solution)/shard_map/all_gather | solution.py:99
  9.6 221.7 %all-gather.13.cloned.1.call-start = ((), (), s32[]{:S(2)}) async-start(), calls=%async_computation.14 | async-start | bytes 4718592 | tf_op jit(solution)/shard_map/all_gather | solution.py:125
  55.2 130.1 %copy-start.39 = (f32[128]{0:T(128)}, f32[128]{0:T(128)S(1)}, u32[]{:S(2)}) copy-start(f32[128]{0:T(128)S(1)} %add_rsqrt_fusion.3) | copy-start | bytes 1540
  56.0 128.0 %copy-start.24 = (f32[128,64]{0,1:T(8,128)}, f32[128,64]{0,1:T(8,128)S(1)}, u32[]{:S(2)}) copy-start(f32[128,64]{0,1:T(8,128)S(1)} %get-tuple-element.72) | copy-start | bytes 98308
  56.0 119.5 %copy-start.26 = (f32[1,2048]{1,0:T(1,128)}, f32[1,2048]{1,0:T(1,128)S(1)}, u32[]{:S(2)}) copy-start(f32[1,2048]{1,0:T(1,128)S(1)} %get-tuple-element.68) | copy-start | bytes 24580
  56.1 124.3 %copy-start.28 = (f32[1,2048]{1,0:T(1,128)}, f32[1,2048]{1,0:T(1,128)S(1)}, u32[]{:S(2)}) copy-start(f32[1,2048]{1,0:T(1,128)S(1)} %get-tuple-element.67) | copy-start | bytes 24580
  56.1 129.2 %copy-start.22 = (f32[1,2048]{1,0:T(1,128)}, f32[1,2048]{1,0:T(1,128)S(1)}, u32[]{:S(2)}) copy-start(f32[1,2048]{1,0:T(1,128)S(1)} %get-tuple-element.69) | copy-start | bytes 24580
  56.1 307.2 %copy-start.30 = (f32[1,2048]{1,0:T(1,128)}, f32[1,2048]{1,0:T(1,128)S(1)}, u32[]{:S(2)}) copy-start(f32[1,2048]{1,0:T(1,128)S(1)} %get-tuple-element.66) | copy-start | bytes 24580
  169.0 6.5 copy-start.2
  174.0 1.0 copy-start.6
  174.1 6.2 copy-start.45
  180.3 1.0 copy-start.8
  180.3 3.7 copy-start.47
  184.3 6.5 copy-start.20
  185.2 93.7 %all-gather.11.cloned.1.call-start = ((), (), s32[]{:S(2)}) async-start(), calls=%async_computation.13 | async-start | bytes 4718592 | tf_op jit(solution)/shard_map/all_gather | solution.py:126
  190.8 167.7 %all-gather.15.cloned.1.call-start = ((), (), s32[]{:S(2)}) async-start(), calls=%async_computation.15 | async-start | bytes 8650752 | tf_op jit(solution)/shard_map/all_gather | solution.py:100
  191.6 456.1 %all-gather.17.cloned.1.call-start = ((), (), s32[]{:S(2)}) async-start(), calls=%async_computation.16 | async-start | bytes 37748736 | tf_op jit(solution)/shard_map/all_gather | solution.py:165
  201.7 6.1 copy-start.41
  201.7 596.8 %all-gather.19.cloned.1.call-start = ((), (), s32[]{:S(2)}) async-start(), calls=%async_computation.17 | async-start | bytes 18874368 | tf_op jit(solution)/shard_map/all_gather | solution.py:166
  213.8 65.1 %copy-start.37 = (pred[1024]{0:T(1024)(128)(4,1)}, pred[1024]{0:T(1024)(128)(4,1)S(1)}, u32[]{:S(2)}) copy-start(pred[1024]{0:T(1024)(128)(4,1)S(1)} %iota_compare_fusion.5) | copy-start | bytes 3076
  214.0 26.6 copy-start.9
  235.3 3.4 copy-start
  235.3 51.4 %copy-start.33 = (f32[16,128]{1,0:T(8,128)}, f32[16,128]{1,0:T(8,128)S(1)}, u32[]{:S(2)}) copy-start(f32[16,128]{1,0:T(8,128)S(1)} %get-tuple-element.77) | copy-start | bytes 24580
  240.7 45.9 %copy-start.35 = (f32[16,128]{1,0:T(8,128)}, f32[16,128]{1,0:T(8,128)S(1)}, u32[]{:S(2)}) copy-start(f32[16,128]{1,0:T(8,128)S(1)} %fusion.24) | copy-start | bytes 24580
  286.7 76.6 %copy-start.14 = (bf16[16,128,128]{2,1,0:T(8,128)(2,1)}, bf16[16,128,128]{2,1,0:T(8,128)(2,1)S(1)}, u32[]{:S(2)}) copy-start(bf16[16,128,128]{2,1,0:T(8,128)(2,1)S(1)} %fusion.69) | copy-start | bytes 1572868
  363.2 26.6 copy-start.43
  364.4 505.2 %copy-start.12 = (bf16[128,2048]{1,0:T(8,128)(2,1)}, bf16[128,2048]{1,0:T(8,128)(2,1)S(1)}, u32[]{:S(2)}) copy-start(bf16[128,2048]{1,0:T(8,128)(2,1)S(1)} %multiply_convert_fusion.4) | copy-start | bytes 1572868
  389.8 257.9 %all-to-all-start = ((bf16[4,512,2048]{2,1,0:T(8,128)(2,1)}), bf16[4,512,2048]{2,1,0:T(8,128)(2,1)}, u32[]{:S(2)}, u32[]{:S(2)}) async-start(bf16[4,512,2048]{2,1,0:T(8,128)(2,1)} %bitcast.271), calls=%async_computation | async-start | bytes 16777216 | tf_op jit(solution)/shard_map/all_to_all | solution.py:156
  822.6 5.8 copy-start.42
  822.6 46.6 %copy-start.11 = (bf16[128,2048]{1,0:T(8,128)(2,1)S(1)}, bf16[128,2048]{1,0:T(8,128)(2,1)}, u32[]{:S(2)}) copy-start(bf16[128,2048]{1,0:T(8,128)(2,1)} %param.11) | copy-start | bytes 1572868
  822.6 99.5 %all-to-all-start.1 = ((bf16[4,512,2048]{2,1,0:T(8,128)(2,1)}), bf16[4,512,2048]{2,1,0:T(8,128)(2,1)}, u32[]{:S(2)}, u32[]{:S(2)}) async-start(bf16[4,512,2048]{2,1,0:T(8,128)(2,1)} %bitcast.269), calls=%async_computation.1 | async-start | bytes 16777216 | tf_op jit(solution)/shard_map/all_to_all | solution.py:72
  1117.2 6.0 copy-start.34
  1117.2 6.0 copy-start.36
  1117.2 96.8 %all-to-all-start.3 = ((bf16[4,512,2048]{2,1,0:T(8,128)(2,1)}), bf16[4,512,2048]{2,1,0:T(8,128)(2,1)}, u32[]{:S(2)}, u32[]{:S(2)}) async-start(bf16[4,512,2048]{2,1,0:T(8,128)(2,1)} %bitcast.270), calls=%async_computation.3 | async-start | bytes 16777216 | tf_op jit(solution)/shard_map/all_to_all | solution.py:72
  1123.0 190.3 %reduce-scatter.25.cloned.1.call-start = ((), (), s32[]{:S(2)}) async-start(), calls=%async_computation.22 | async-start | bytes 4718592
  1213.9 18.5 copy-start.5
  1213.9 18.5 copy-start.31
  1213.9 18.5 copy-start.44
  1227.3 5.6 copy-start.16
  1232.9 8.0 copy-start.38
  1248.9 7.1 copy-start.10
  1254.1 2.0 copy-start.1
  1265.8 98.4 %reduce-scatter.27.cloned.1.call-start = ((), (), s32[]{:S(2)}) async-start(), calls=%async_computation.23 | async-start | bytes 4718592
  1273.8 6.6 copy-start.13
  1280.3 34.3 %copy-start.25 = (f32[128,64]{0,1:T(8,128)S(1)}, f32[128,64]{0,1:T(8,128)}, u32[]{:S(2)}) copy-start(f32[128,64]{0,1:T(8,128)} %copy-done.24) | copy-start | bytes 98308
  1280.3 34.3 %copy-start.32 = (f32[128,64]{0,1:T(8,128)S(1)}, f32[128,64]{0,1:T(8,128)}, u32[]{:S(2)}) copy-start(f32[128,64]{0,1:T(8,128)} %get-tuple-element.70) | copy-start | bytes 98308
  1280.3 219.2 %reduce-scatter.31.cloned.1.call-start = ((), (), s32[]{:S(2)}) async-start(), calls=%async_computation.25 | async-start | bytes 1081344
  1281.7 352.0 %reduce-scatter.29.cloned.1.call-start = ((), (), s32[]{:S(2)}) async-start(), calls=%async_computation.24 | async-start | bytes 1081344
  1287.6 32.8 %copy-start.29 = (f32[1,2048]{1,0:T(1,128)S(1)}, f32[1,2048]{1,0:T(1,128)}, u32[]{:S(2)}) copy-start(f32[1,2048]{1,0:T(1,128)} %copy-done.28) | copy-start | bytes 24580
  1287.6 32.8 %copy-start.48 = (f32[128]{0:T(128)S(1)}, f32[128]{0:T(128)}, u32[]{:S(2)}) copy-start(f32[128]{0:T(128)} %copy-done.47) | copy-start | bytes 1540
  1314.7 12.0 copy-start.7
  1314.7 11.9 copy-start.27
  1314.7 11.9 copy-start.46
  1336.9 27.3 copy-start.3
  1336.9 27.3 copy-start.23
  1336.9 27.3 copy-start.40
  1373.2 427.9 %reduce-scatter.23.cloned.1.call-start = ((), (), s32[]{:S(2)}) async-start(), calls=%async_computation.21 | async-start | bytes 18874368 | tf_op jit(solution)/shard_map/reduce_scatter | solution.py:226
  1389.8 737.5 %reduce-scatter.21.cloned.1.call-start = ((), (), s32[]{:S(2)}) async-start(), calls=%async_computation.20 | async-start | bytes 37748736 | tf_op jit(solution)/shard_map/reduce_scatter | solution.py:217
  1415.4 1.0 copy-start.15
  1415.5 899.8 %reduce-scatter.19.cloned.1.call-start = ((), (), s32[]{:S(2)}) async-start(), calls=%async_computation.19 | async-start | bytes 17301504 | tf_op jit(solution)/shard_map/reduce_scatter | solution.py:303
  1424.6 8.5 copy-start.18
  1424.6 1426.7 %reduce-scatter.17.cloned.1.call-start = ((), (), s32[]{:S(2)}) async-start(), calls=%async_computation.18 | async-start | bytes 51904512 | tf_op jit(solution)/shard_map/reduce_scatter | solution.py:302
  1433.1 8.2 copy-start.21
  1485.1 15.8 copy-start.19
  (2 other events, 1.8 us)
Sparse Core Ops, SparseCore 0:
  11.6 157.3 all-gather.8
  185.3 45.9 all-gather.12
  233.5 45.3 all-gather.10
  282.4 76.0 all-gather.14
  360.5 287.2 all-gather.16
  649.2 149.2 all-gather.18
  1265.9 47.2 reduce-scatter.24
  1316.1 48.1 reduce-scatter.26
  1366.5 132.9 reduce-scatter.30
  1502.3 131.4 reduce-scatter.28
  1636.2 164.9 reduce-scatter.22
  1803.4 323.8 reduce-scatter.20
  2130.3 184.9 reduce-scatter.18
  2318.1 533.2 reduce-scatter.16
where the time goes:
time: 2870 us; the launch traced here: 2860 us
  waiting for transfers between devices  2130 us (74%)
  matrix products  255 us (9%)
  blocking collectives  185 us (6%)
  local copies, waits for them, and re-layouts  146 us (5%)
  other arithmetic  103 us (4%)
    reduce_scatter x1, waiting for transfers between devices, shards(): lax.psum_scatter(grad_qkv_local, ('expert', 'dp'), scatter_dimension=1, t...  536 us
    reduce_scatter x1, waiting for transfers between devices, shards(): lax.psum_scatter(jnp.einsum('sxmd,sxmkf->dxkf', row_piece, grad_both, pre...  321 us
    all_gather x1, waiting for transfers between devices, shards(): lax.all_gather(expert_in.astype(low_type), 'dp', axis=0, tiled=True)  252 us
    unnamed x18, waiting for transfers between devices  193 us
    reduce_scatter x1, waiting for transfers between devices, shards(): lax.psum_scatter(grad_out_weight, ('expert', 'dp'), scatter_dimension=0,...  176 us
    reduce_scatter x1, waiting for transfers between devices, shards(): lax.psum_scatter(jnp.einsum('sxmd,sxmf->dxf', row_piece, hidden, preferre...  166 us
    all_to_all x2, waiting for transfers between devices, from_owners(): lax.all_to_all(buffer, 'expert', split_axis=0, concat_axis=0, tiled=True)  134 us
    all_gather x1, waiting for transfers between devices, shards(): lax.all_gather(expert_down.astype(low_type), 'dp', axis=0, tiled=True)  115 us
  transfers between devices with their start and end apart: 17, of which 16 were waited for; matrix products, arithmetic and copies ran while one was open for 11% of the time, Pallas kernels for 0%

commit v1 on v0

--- a/solution.py
+++ b/solution.py
@@ -1,15 +1,19 @@
 import jax
 import jax.numpy as jnp
+import numpy as np
 from jax import lax
+from jax.sharding import Mesh
 from jax.sharding import PartitionSpec as P
 
 HEADS = 16
 HD = 128
-
 
 epsilon = 1e-05
 rope_base = 10000.0
 masked_score = -1000000000.0
+
+low_type = jnp.bfloat16
+high_type = jnp.float32
 
 
 def rms_scale(values):
@@ -23,8 +27,8 @@
 
 
 def rotate(values, cosine, sine_table):
-    row_count = values.shape[0]
-    shaped = values.reshape(row_count, HEADS, 2, HD // 2)
+    row_count, width = values.shape
+    shaped = values.reshape(row_count, width // HD, 2, HD // 2)
     first_half = shaped[:, :, 0, :]
     second_half = shaped[:, :, 1, :]
     cos_rows = cosine[:, None, :]
@@ -36,7 +40,7 @@
         ],
         axis=2,
     )
-    return turned.reshape(row_count, HEADS * HD)
+    return turned.reshape(row_count, width)
 
 
 def rms_back(grad_rows, normed, scale, gain):
@@ -45,12 +49,434 @@
     return (scale * grad_normed - normed * scale * inner, jnp.sum(grad_rows * normed, axis=0))
 
 
+def dot(left, right):
+    return jnp.dot(left, right, preferred_element_type=high_type)
+
+
+def dot_t(left, right):
+    return lax.dot_general(left, right, (((1,), (1,)), ((), ())), preferred_element_type=high_type)
+
+
+def t_dot(left, right):
+    return lax.dot_general(left, right, (((0,), (0,)), ((), ())), preferred_element_type=high_type)
+
+
+GRID = ("ey", "ex", "dz", "dc")
+SEQ = ("dz", "dc")
+
+
+class Moves:
+    def __init__(self, depth):
+        self.depth = depth
+        self.count = 2 * 2 * depth * 2
+
+    def pairs(self, move):
+        result = []
+        for index in range(self.count):
+            c = index % 2
+            z = index // 2 % self.depth
+            x = index // (2 * self.depth) % 2
+            y = index // (4 * self.depth)
+            y, x, z, c = move(y, x, z, c)
+            result.append((index, ((y * 2 + x) * self.depth + z) * 2 + c))
+        return result
+
+    def send(self, values, move):
+        return lax.ppermute(values, GRID, self.pairs(move))
+
+    def core(self, values):
+        return self.send(values, lambda y, x, z, c: (y, x, z, 1 - c))
+
+    def from_z(self, values, step):
+        return self.send(values, lambda y, x, z, c: (y, x, (z - step) % self.depth, c))
+
+    def to_z(self, values, step):
+        return self.send(values, lambda y, x, z, c: (y, x, (z + step) % self.depth, c))
+
+    def near(self, values):
+        return self.send(
+            values, lambda y, x, z, c: (y, 1 - x, z, c) if c == 0 else (1 - y, x, z, c)
+        )
+
+    def far(self, values):
+        return self.send(
+            values, lambda y, x, z, c: (1 - y, x, z, c) if c == 0 else (y, 1 - x, z, c)
+        )
+
+    def sum_seq(self, values):
+        values = values + self.core(values)
+        total = values
+        for step in range(1, self.depth):
+            total = total + self.from_z(values, step)
+        return total
+
+    def spread(self, rows):
+        own = jnp.concatenate(
+            [rows] + [self.from_z(rows, step) for step in range(1, self.depth)], axis=0
+        )
+        near = self.near(own)
+        far = self.far(jnp.concatenate([own, near], axis=0))
+        return [jnp.concatenate([v, self.core(v)], axis=0) for v in (own, near, far)]
+
+    def collect(self, chunks, rows):
+        def both(chunk):
+            half = chunk.shape[0] // 2
+            arrived = self.core(chunk[half:])
+            return chunk[:half].astype(high_type) + arrived.astype(high_type)
+
+        far = self.far(both(chunks[2]).astype(low_type)).astype(high_type)
+        half = far.shape[0] // 2
+        near = self.near((both(chunks[1]) + far[half:]).astype(low_type))
+        own = (both(chunks[0]) + far[:half] + near.astype(high_type)).astype(low_type)
+        total = own[:rows].astype(high_type)
+        for step in range(1, self.depth):
+            total = total + self.to_z(own[step * rows : (step + 1) * rows], step).astype(high_type)
+        return total
+
+    def block_order(self):
+        y, x, z, c = (lax.axis_index(name) for name in GRID)
+
+        def at(y, x, step, c):
+            return ((y * 2 + x) * self.depth + (z + step) % self.depth) * 2 + c
+
+        order = []
+        for dy, dx in ((0, 0),):
+            for core in (c, 1 - c):
+                order += [at(y, x, k, core) for k in range(self.depth)]
+        for core in (c, 1 - c):
+            order += [at(y ^ core, x ^ (1 - core), k, core) for k in range(self.depth)]
+        for core in (c, 1 - c):
+            order += [at(y ^ (1 - core), x ^ core, k, core) for k in range(self.depth)]
+            order += [at(1 - y, 1 - x, k, core) for k in range(self.depth)]
+        return jnp.stack(order)
+
+
+def grid_shards(
+    residual_in,
+    cotangent,
+    lengths,
+    routes,
+    attn_qkv,
+    attn_out,
+    gains,
+    router,
+    expert_in,
+    expert_down,
+):
+    rows, width = residual_in.shape
+    depth = lax.axis_size("dz")
+    move = Moves(depth)
+    ranks = 2 * depth
+    columns = 4
+    seq_rows = rows * ranks
+    local_experts = expert_in.shape[1]
+    experts = local_experts * columns
+    hidden_width = expert_in.shape[3]
+    part = hidden_width // ranks
+    span = local_experts * part
+    chunk_rows = expert_in.shape[0]
+    weight_rows = attn_qkv.shape[1]
+    score_scale = HD ** (-0.5)
+    y, x, z, c = (lax.axis_index(name) for name in GRID)
+    column = y * 2 + x
+    own_heads = HEADS // ranks
+    own_width = own_heads * HD
+
+    def by_rank(values):
+        lead = values.shape[:-1]
+        shaped = values.reshape(lead + (2, own_heads, depth, HD))
+        n = len(lead)
+        return shaped.transpose((n + 2, n) + tuple(range(n)) + (n + 1, n + 3)).reshape(
+            (ranks,) + lead + (own_width,)
+        )
+
+    def by_head(values):
+        lead = values.shape[1:-1]
+        shaped = values.reshape((depth, 2) + lead + (own_heads, HD))
+        n = len(lead)
+        return shaped.transpose(tuple(range(2, n + 2)) + (1, n + 2, 0, n + 3)).reshape(
+            lead + (width,)
+        )
+
+    small = jnp.concatenate([gains.T, router], axis=1).astype(low_type)
+    small = lax.all_gather(small, GRID, axis=0, tiled=True)
+    gain_rows = small[:, :4].T.astype(high_type)
+    router_weight = small[:, 4:]
+    gain_own = [
+        lax.dynamic_index_in_dim(by_rank(gain_rows[i]), z * 2 + c, 0, keepdims=False)
+        for i in (1, 2)
+    ]
+
+    held = [residual_in] + [move.from_z(residual_in, k) for k in range(1, depth)]
+    crossed = [move.core(block) for block in held]
+    normed_in = jnp.zeros((depth, 2, rows, width), low_type)
+    for k in range(depth):
+        for block, core in ((held[k], c), (crossed[k], 1 - c)):
+            block = block.astype(high_type)
+            block = (block * rms_scale(block) * gain_rows[0]).astype(low_type)
+            normed_in = lax.dynamic_update_slice(
+                normed_in, block[None, None], ((z + k) % depth, core, 0, 0)
+            )
+    normed_in = normed_in.reshape(seq_rows, width)
+
+    packed = attn_qkv.astype(low_type).transpose(1, 0, 2)
+    packed = by_rank(packed).reshape(ranks, weight_rows, 3 * own_width)
+    packed = lax.all_to_all(packed, SEQ, 0, 0, tiled=True).reshape(-1, 3 * own_width)
+    near = move.near(packed)
+    far = move.far(jnp.stack([packed, near]))
+    in_x = jnp.where(c == 0, near, far[0])
+    in_y = jnp.where(c == 0, far[0], near)
+    in_row = [jnp.where(x == 0, packed, in_x), jnp.where(x == 0, in_x, packed)]
+    out_row = [jnp.where(x == 0, in_y, far[1]), jnp.where(x == 0, far[1], in_y)]
+    qkv_weight = jnp.concatenate(
+        [jnp.where(y == 0, a, b) for a, b in zip(in_row, out_row)]
+        + [jnp.where(y == 0, b, a) for a, b in zip(in_row, out_row)],
+        axis=0,
+    )
+    out_weight = lax.all_gather(attn_out.astype(low_type), GRID, axis=0, tiled=True)
+
+    sliced_in = expert_in.astype(low_type).reshape(chunk_rows, local_experts, 2, ranks, part)
+    sliced_in = sliced_in.transpose(3, 0, 2, 1, 4).reshape(ranks, chunk_rows, 2 * span)
+    weights_in = lax.all_to_all(sliced_in, SEQ, 0, 0, tiled=True).reshape(width, 2 * span)
+    sliced_down = expert_down.astype(low_type).reshape(chunk_rows, local_experts, ranks, part)
+    sliced_down = sliced_down.transpose(2, 0, 1, 3).reshape(ranks, chunk_rows, span)
+    weights_down = lax.all_to_all(sliced_down, SEQ, 0, 0, tiled=True).reshape(width, span)
+
+    raw = dot(normed_in, qkv_weight)
+    query_raw, key_raw = raw[:, :own_width], raw[:, own_width : 2 * own_width]
+    value_rows = raw[:, 2 * own_width :].astype(low_type)
+    squares = jnp.stack(
+        [jnp.sum(query_raw * query_raw, axis=1), jnp.sum(key_raw * key_raw, axis=1)]
+    )
+    scales = lax.rsqrt(move.sum_seq(squares) / width + epsilon)
+    query_scale, key_scale = scales[0][:, None], scales[1][:, None]
+    positions = jnp.arange(seq_rows, dtype=jnp.int32)
+    length_now = lengths[0]
+    key_live = positions < length_now
+    cosine, sine_table = angle_tables(positions)
+    query_normed = query_raw * query_scale
+    key_normed = key_raw * key_scale
+    query_rot = rotate(query_normed * gain_own[0], cosine, sine_table).astype(low_type)
+    key_rot = rotate(key_normed * gain_own[1], cosine, sine_table).astype(low_type)
+    query_heads = query_rot.reshape(seq_rows, own_heads, HD)
+    key_heads = key_rot.reshape(seq_rows, own_heads, HD)
+    value_heads = value_rows.reshape(seq_rows, own_heads, HD)
+
+    def per_head(spec, left, right):
+        return jnp.einsum(spec, left, right, preferred_element_type=high_type)
+
+    scores = per_head("qhd,khd->hqk", query_heads, key_heads) * score_scale
+    scores = jnp.where(key_live[None, None, :], scores, masked_score)
+    probs = jax.nn.softmax(scores, axis=-1)
+    probs_low = probs.astype(low_type)
+    attended = per_head("hqk,khd->qhd", probs_low, value_heads).astype(low_type)
+    attended = lax.all_to_all(attended.reshape(ranks, rows, own_width), SEQ, 0, 0, tiled=True)
+    attended = by_head(attended)
+
+    own_positions = (z * 2 + c) * rows + jnp.arange(rows, dtype=jnp.int32)
+    live_rows = (own_positions < length_now).astype(high_type)[:, None]
+    input_rows = residual_in.astype(high_type)
+    middle = input_rows + live_rows * dot(attended, out_weight)
+    scale_mid = rms_scale(middle)
+    normed_mid_f = middle * scale_mid
+    normed_mid = (normed_mid_f * gain_rows[3]).astype(low_type)
+
+    logits = dot(normed_mid, router_weight)
+    named = jnp.any(
+        routes[:, :, None] == jnp.arange(experts, dtype=jnp.int32)[None, None, :], axis=1
+    )
+    top = jnp.max(jnp.where(named, logits, -jnp.inf), axis=1, keepdims=True)
+    weight_of = jnp.where(named, jnp.exp(jnp.where(named, logits - top, 0.0)), 0.0)
+    gates = weight_of / jnp.sum(weight_of, axis=1, keepdims=True)
+
+    grad_rows = cotangent.astype(high_type)
+    grad_comb = live_rows * grad_rows
+    order = move.block_order()
+    gates_all = lax.all_gather(gates.T[None], GRID, axis=0, tiled=True)
+    gates_all = lax.dynamic_slice_in_dim(gates_all, column * local_experts, local_experts, 1)
+    chosen_block = (order[:, None] == jnp.arange(4 * ranks, dtype=jnp.int32)[None, :]).astype(
+        high_type
+    )
+
+    def permuted(spec, blocks):
+        return jnp.einsum(
+            spec,
+            chosen_block,
+            blocks,
+            precision=lax.Precision.HIGHEST,
+            preferred_element_type=high_type,
+        )
+
+    gates_all = permuted("ij,jer->ier", gates_all).transpose(0, 2, 1).reshape(-1, local_experts)
+    grad_chunks = move.spread(grad_comb.astype(low_type))
+    token_chunks = move.spread(normed_mid)
+    back_chunks, mixed_chunks, gate_sums = [], [], []
+    grad_in = jnp.zeros((width, 2 * span), high_type)
+    grad_down = jnp.zeros((width, span), high_type)
+    start = 0
+    for tokens, grads in zip(token_chunks, grad_chunks):
+        count = tokens.shape[0]
+        gate = gates_all[start : start + count]
+        start += count
+        wide = jnp.repeat(gate, part, axis=1)
+        both_parts = dot(tokens, weights_in)
+        gate_part, up_part = both_parts[:, :span], both_parts[:, span:]
+        down_grad = dot(grads, weights_down)
+        sigma = jax.nn.sigmoid(gate_part)
+        hidden = (gate_part * sigma * up_part).astype(low_type).astype(high_type)
+        gate_sums.append(
+            jnp.sum((hidden * down_grad).reshape(count, local_experts, part), axis=2)
+        )
+        weighted = (wide * hidden).astype(low_type)
+        grad_hidden = wide * down_grad
+        grad_gate = grad_hidden * up_part * sigma * (1.0 + gate_part * (1.0 - sigma))
+        grad_up = grad_hidden * gate_part * sigma
+        grad_both = jnp.concatenate([grad_gate, grad_up], axis=1).astype(low_type)
+        back_chunks.append(dot_t(grad_both, weights_in).astype(low_type))
+        mixed_chunks.append(dot_t(weighted, weights_down).astype(low_type))
+        grad_in = grad_in + t_dot(tokens, grad_both)
+        grad_down = grad_down + t_dot(grads, weighted)
+    grad_mid_norm = move.collect(back_chunks, rows)
+    combined = move.collect(mixed_chunks, rows)
+    output = middle + live_rows * combined
+
+    sliced = grad_in.astype(low_type).reshape(ranks, chunk_rows, 2 * span)
+    sliced = lax.all_to_all(sliced, SEQ, 0, 0, tiled=True)
+    sliced = sliced.reshape(ranks, chunk_rows, 2, local_experts, part).transpose(1, 3, 2, 0, 4)
+    grad_expert_in = sliced.reshape(expert_in.shape).astype(high_type)
+    sliced = grad_down.astype(low_type).reshape(ranks, chunk_rows, span)
+    sliced = lax.all_to_all(sliced, SEQ, 0, 0, tiled=True)
+    sliced = sliced.reshape(ranks, chunk_rows, local_experts, part).transpose(1, 2, 0, 3)
+    grad_expert_down = sliced.reshape(expert_down.shape).astype(high_type)
+
+    sums = jnp.concatenate(gate_sums, axis=0).reshape(-1, rows, local_experts).transpose(0, 2, 1)
+    placed = jnp.zeros((4 * ranks, columns, local_experts, rows), high_type)
+    sums = permuted("ij,ier->jer", sums)
+    placed = lax.dynamic_update_slice(placed, sums[:, None], (0, column, 0, 0))
+    grad_gates = lax.psum_scatter(
+        placed.reshape(4 * ranks, experts, rows), GRID, scatter_dimension=0, tiled=True
+    )[0].T
+    grad_chosen = gates * (grad_gates - jnp.sum(gates * grad_gates, axis=1, keepdims=True))
+    grad_logits = grad_chosen.astype(low_type)
+    grad_mid_norm = grad_mid_norm + dot_t(grad_logits, router_weight)
+    grad_router = t_dot(normed_mid, grad_logits)
+
+    grad_mid_rows, grad_gain_mid = rms_back(grad_mid_norm, normed_mid_f, scale_mid, gain_rows[3])
+    grad_middle = grad_rows + grad_mid_rows
+    grad_branch = (live_rows * grad_middle).astype(low_type)
+    grad_out = lax.psum_scatter(
+        t_dot(attended, grad_branch).astype(low_type), GRID, scatter_dimension=0, tiled=True
+    ).astype(high_type)
+
+    grad_attended = by_rank(dot_t(grad_branch, out_weight).astype(low_type))
+    grad_attended = lax.all_to_all(grad_attended, SEQ, 0, 0, tiled=True)
+    grad_heads = grad_attended.reshape(seq_rows, own_heads, HD)
+    grad_probs = per_head("qhd,khd->hqk", grad_heads, value_heads)
+    inner_rows = jnp.sum(probs * grad_probs, axis=-1, keepdims=True)
+    grad_scores = (probs * (grad_probs - inner_rows)).astype(low_type)
+    grad_query = per_head("hqk,khd->qhd", grad_scores, key_heads) * score_scale
+    grad_key = per_head("hqk,qhd->khd", grad_scores, query_heads) * score_scale
+    grad_value = per_head("hqk,qhd->khd", probs_low, grad_heads).astype(low_type)
+    grad_query = rotate(grad_query.reshape(seq_rows, own_width), cosine, -sine_table)
+    grad_key = rotate(grad_key.reshape(seq_rows, own_width), cosine, -sine_table)
+    query_inner = grad_query * gain_own[0]
+    key_inner = grad_key * gain_own[1]
+    inner = jnp.stack(
+        [
+            jnp.sum(query_inner * query_normed, axis=1),
+            jnp.sum(key_inner * key_normed, axis=1),
+        ]
+    )
+    inner = move.sum_seq(inner) / width
+    query_back = query_scale * (query_inner - query_normed * inner[0][:, None])
+    key_back = key_scale * (key_inner - key_normed * inner[1][:, None])
+    grad_raw = jnp.concatenate(
+        [
+            query_back.astype(low_type),
+            key_back.astype(low_type),
+            grad_value.reshape(seq_rows, own_width),
+        ],
+        axis=1,
+    )
+
+    by_core = grad_raw.reshape(depth, 2, rows, 3 * own_width)
+    other = lax.dynamic_index_in_dim(by_core, 1 - c, 1, keepdims=False)
+    mine = lax.dynamic_index_in_dim(by_core, c, 1, keepdims=False)
+    other = dot_t(other.reshape(depth * rows, -1), qkv_weight).astype(low_type)
+    mine = dot_t(mine.reshape(depth * rows, -1), qkv_weight)
+    share = (mine + move.core(other).astype(high_type)).astype(low_type)
+    share = share.reshape(depth, rows, width)
+    grad_norm_in = lax.dynamic_index_in_dim(share, z, 0, keepdims=False).astype(high_type)
+    for step in range(1, depth):
+        piece = lax.dynamic_index_in_dim(share, (z + step) % depth, 0, keepdims=False)
+        grad_norm_in = grad_norm_in + move.to_z(piece, step).astype(high_type)
+
+    grad_qkv = t_dot(normed_in, grad_raw).astype(low_type).reshape(columns, -1, 3 * own_width)
+
+    def for_column(index):
+        return lax.dynamic_index_in_dim(grad_qkv, index, 0, keepdims=False)
+
+    far_x, far_y = x ^ c, y ^ (1 - c)
+    near_x, near_y = x ^ (1 - c), y ^ c
+    arrived = move.far(
+        jnp.stack([for_column(far_y * 2 + far_x), for_column(3 - column)])
+    ).astype(high_type)
+    near = (for_column(near_y * 2 + near_x).astype(high_type) + arrived[1]).astype(low_type)
+    total = for_column(column).astype(high_type) + arrived[0] + move.near(near).astype(high_type)
+    total = total.astype(low_type).reshape(ranks, weight_rows, 3 * own_width)
+    total = lax.all_to_all(total, SEQ, 0, 0, tiled=True)
+    grad_qkv = by_head(total.reshape(ranks, weight_rows, 3, own_width))
+    grad_qkv = grad_qkv.transpose(1, 0, 2).astype(high_type)
+
+    scale_in = rms_scale(input_rows)
+    grad_in_rows, grad_gain_in = rms_back(
+        grad_norm_in, input_rows * scale_in, scale_in, gain_rows[0]
+    )
+    grad_input = grad_middle + grad_in_rows
+
+    def at_heads(values):
+        whole = jnp.zeros((2, own_heads, depth, HD), high_type)
+        values = values.reshape(1, own_heads, 1, HD)
+        return lax.dynamic_update_slice(whole, values, (c, 0, z, 0)).reshape(width)
+
+    grad_small = jnp.concatenate(
+        [
+            jnp.stack(
+                [
+                    grad_gain_in,
+                    at_heads(jnp.sum(grad_query * query_normed, axis=0)),
+                    at_heads(jnp.sum(grad_key * key_normed, axis=0)),
+                    grad_gain_mid,
+                ]
+            ).T,
+            grad_router,
+        ],
+        axis=1,
+    )
+    grad_small = lax.psum_scatter(grad_small, GRID, scatter_dimension=0, tiled=True)
+    return (
+        output,
+        grad_input,
+        grad_qkv,
+        grad_out,
+        grad_small[:, :4].T,
+        grad_small[:, 4:],
+        grad_expert_in,
+        grad_expert_down,
+    )
+
+
 def slot_index(route_rows, experts, capacity):
     flat_routes = route_rows.reshape(-1)
     onehot = (flat_routes[:, None] == jnp.arange(experts, dtype=jnp.int32)[None, :]).astype(
         jnp.int32
     )
-    rank_rows = jnp.sum((jnp.cumsum(onehot, axis=0) - onehot) * onehot, axis=1)
+    rows = jnp.arange(flat_routes.shape[0], dtype=jnp.int32)
+    earlier = (rows[None, :] < rows[:, None]).astype(jnp.bfloat16)
+    before = jnp.dot(
+        earlier, onehot.astype(jnp.bfloat16), preferred_element_type=jnp.float32
+    ).astype(jnp.int32)
+    rank_rows = jnp.sum(before * onehot, axis=1)
     return flat_routes * capacity + rank_rows
 
 
@@ -92,8 +518,6 @@
     capacity = tok_rows * top_count * 2 // experts
     local_slots = local_experts * capacity
     seq_rows = tok_rows * lax.axis_size("dp")
-    low_type = jnp.bfloat16
-    high_type = jnp.float32
     score_scale = HD ** (-0.5)
     qkv_weights, out_weight, gain_low, router_weight = (
         lax.all_gather(attn_qkv.astype(low_type), ("expert", "dp"), axis=1, tiled=True),
@@ -317,31 +741,31 @@
 
 
 def solution(mesh):
+    column_count, rank_count = mesh.shape["expert"], mesh.shape["dp"]
+    depth = rank_count // 2
+    tiled = column_count == 4 and rank_count % 2 == 0 and HEADS == column_count * depth
+    if tiled:
+        mesh = Mesh(mesh.devices.reshape(2, 2, depth, 2), GRID)
+        column, rank, body = ("ey", "ex"), SEQ, grid_shards
+    else:
+        column, rank, body = ("expert",), ("dp",), shards
+    device = column + rank
     placed = (
-        P(("expert", "dp"), None),
-        P(("expert", "dp"), None),
-        P("expert"),
-        P(("expert", "dp"), None),
-        P(None, ("expert", "dp"), None),
-        P(("expert", "dp"), None),
-        P(None, ("expert", "dp")),
-        P(("expert", "dp"), None),
-        P("dp", "expert", None, None),
-        P("dp", "expert", None),
+        P(device, None),
+        P(device, None),
+        P(column),
+        P(device, None),
+        P(None, device, None),
+        P(device, None),
+        P(None, device),
+        P(device, None),
+        P(rank, column, None, None),
+        P(rank, column, None),
     )
     return jax.shard_map(
-        shards,
+        body,
         mesh=mesh,
         in_specs=placed,
-        out_specs=(
-            P(("expert", "dp"), None),
-            P(("expert", "dp"), None),
-            P(None, ("expert", "dp"), None),
-            P(("expert", "dp"), None),
-            P(None, ("expert", "dp")),
-            P(("expert", "dp"), None),
-            P("dp", "expert", None, None),
-            P("dp", "expert", None),
-        ),
+        out_specs=placed[:1] * 2 + placed[4:],
         check_vma=False,
     )

time: 2870 us -> 1390 us (0.48)
  waiting for transfers between devices: 2130 us -> 597 us
  starting transfers between devices: 18.5 us -> 116 us
  matrix products: 255 us -> 195 us
  local copies, waits for them, and re-layouts: 146 us -> 197 us
    reduce_scatter x4 -> x2, waiting for transfers between devices: 1200 us -> 120 us  [the longest x1 71.6 us: grid_shards(): lax.psum_scatter(placed.reshape(4 * ranks, experts, rows), GRID, scatter_...]
    all_gather x6 -> x1, waiting for transfers between devices: 608 us -> 0.02 us  [grid_shards(): lax.all_gather(attn_out.astype(low_type), GRID, axis=0, tiled=True)]
    ppermute x0 -> x55, waiting for transfers between devices: none -> 379 us  [send(): return lax.ppermute(values, GRID, self.pairs(move))]
    unnamed x18 -> x5, waiting for transfers between devices: 193 us -> 0.07 us
    all_to_all x1, blocking collectives: 101 us -> 27.2 us  [grid_shards(): grad_attended = lax.all_to_all(grad_attended, SEQ, 0, 0, tiled=True)]
    dot_general x29 -> x35, matrix products: 254 us -> 188 us  [the longest x9 66.4 us: t_dot(): lax.dot_general(left, right, (((0,), (0,)), ((), ())), preferred_element_...]
    all_gather x2, blocking collectives: 84 us -> 143 us  [the longest x1 106 us: grid_shards(): small = lax.all_gather(small, GRID, axis=0, tiled=True)]
    ppermute x0 -> x55, starting transfers between devices: none -> 55.5 us  [send(): return lax.ppermute(values, GRID, self.pairs(move))]
  transfers between devices with their start and end apart: 17 -> 66, of which waited for: 16 -> 25; matrix products, arithmetic and copies ran while one was open for 11% -> 30% of each run, Pallas kernels for 0% -> 0%
where the time goes in v1:
time: 1390 us
  waiting for transfers between devices  597 us (43%)
  local copies, waits for them, and re-layouts  197 us (14%)
  matrix products  195 us (14%)
  blocking collectives  170 us (12%)
  starting transfers between devices  116 us (8%)
  other arithmetic  95.4 us (7%)
  between operations  16.8 us (1%)
    ppermute x55, waiting for transfers between devices, send(): return lax.ppermute(values, GRID, self.pairs(move))  379 us
    all_gather x1, blocking collectives, grid_shards(): small = lax.all_gather(small, GRID, axis=0, tiled=True)  106 us
    all_to_all x2, waiting for transfers between devices, grid_shards(): sliced = lax.all_to_all(sliced, SEQ, 0, 0, tiled=True)  92.6 us
    unnamed x280, local copies, waits for them, and re-layouts  79.3 us
    reduce_scatter x1, waiting for transfers between devices, grid_shards(): lax.psum_scatter(placed.reshape(4 * ranks, experts, rows), GRID, scatter_...  71.6 us
    dot_general x9, matrix products, t_dot(): lax.dot_general(left, right, (((0,), (0,)), ((), ())), preferred_element_...  66.4 us
    dot_general x9, matrix products, dot(): return jnp.dot(left, right, preferred_element_type=high_type)  59.7 us
    ppermute x55, starting transfers between devices, send(): return lax.ppermute(values, GRID, self.pairs(move))  55.5 us
  transfers between devices with their start and end apart: 66, of which 25 were waited for; matrix products, arithmetic and copies ran while one was open for 30% of the time, Pallas kernels for 0%

profile of v1, /device:TPU:0, one launch (start us, length us, event | category | flops | bytes accessed | tf_op | source)
XLA Modules:
  0.0 1386.7 jit_solution(3121493171369986028)
XLA Ops:
  23.3 105.5 %all-gather.1 = bf16[32,64,20]{1,2,0:T(8,128)(2,1)S(1)} all-gather(bf16[1,64,20]{1,2,0:T(8,128)(2,1)S(1)} %maximum_bitcast_fusion.2), channel_id=1, replica_groups=mesh['ey'=2,'ex'=2,'dz'=4,'dc'=2] {'ey','ex','dz','dc'}, dimensions={0}, use_global_device_ids=true | all-gather | bytes 84480 | tf_op jit(solution)/shard_map/all_gather | solution.py:202
  145.1 10.8 collective-permute-done.7
  159.1 17.4 %collective-permute-done.8 = bf16[2,512,768]{2,1,0:T(8,128)(2,1)S(1)} collective-permute-done((bf16[2,512,768]{2,1,0:T(8,128)(2,1)S(1)}, bf16[2,512,768]{2,1,0:T(8,128)(2,1)S(1)}, u32[]{:S(2)}, u32[]{:S(2)}) %collective-permute-start.8) | collective-permute-done | bytes 1572896 | tf_op jit(solution)/shard_map/ppermute | solution.py:85
  185.7 9.9 collective-permute-start.12
  202.2 6.5 fusion.135
  228.3 4.9 all-to-all-done.1
  234.0 24.6 %all-to-all-start.3 = ((bf16[8,256,512]{1,2,0:T(8,128)(2,1)}), bf16[8,256,512]{1,2,0:T(8,128)(2,1)S(1)}, u32[]{:S(2)}, u32[]{:S(2)}) async-start(bf16[8,256,512]{1,2,0:T(8,128)(2,1)} %bitcast.419), calls=%async_computation.3 | async-start | bytes 4194304 | tf_op jit(solution)/shard_map/all_to_all | solution.py:243
  258.6 42.1 %collective-permute-done.30 = bf16[128,2048]{1,0:T(8,128)(2,1)} collective-permute-done((bf16[128,2048]{1,0:T(8,128)(2,1)}, bf16[128,2048]{1,0:T(8,128)(2,1)}, u32[]{:S(2)}, u32[]{:S(2)}) %collective-permute-start.30) | collective-permute-done | bytes 524320 | tf_op jit(solution)/shard_map/ppermute | solution.py:85
  304.0 4.9 multiply_reduce_fusion.5
  316.6 15.5 %collective-permute-done.13 = bf16[128,2048]{1,0:T(8,128)(2,1)S(1)} collective-permute-done((bf16[128,2048]{1,0:T(8,128)(2,1)S(1)}, bf16[128,2048]{1,0:T(8,128)(2,1)S(1)}, u32[]{:S(2)}, u32[]{:S(2)}) %collective-permute-start.13) | collective-permute-done | bytes 524320 | tf_op jit(solution)/shard_map/ppermute | solution.py:85
  332.1 35.5 %collective-permute-done.14 = bf16[128,2048]{1,0:T(8,128)(2,1)S(1)} collective-permute-done((bf16[128,2048]{1,0:T(8,128)(2,1)S(1)}, bf16[128,2048]{1,0:T(8,128)(2,1)S(1)}, u32[]{:S(2)}, u32[]{:S(2)}) %collective-permute-start.14) | collective-permute-done | bytes 524320 | tf_op jit(solution)/shard_map/ppermute | solution.py:85
  371.9 4.8 copy.218
  381.5 11.8 copy.132
  407.3 5.0 copy.217
  416.9 23.1 %collective-permute-done.35 = bf16[1024,2048]{1,0:T(8,128)(2,1)} collective-permute-done((bf16[1024,2048]{1,0:T(8,128)(2,1)}, bf16[1024,2048]{1,0:T(8,128)(2,1)}, u32[]{:S(2)}, u32[]{:S(2)}) %collective-permute-start.35) | collective-permute-done | bytes 4194336 | tf_op jit(solution)/shard_map/ppermute | solution.py:85
  441.9 43.0 %collective-permute-done.19 = bf16[1024,2048]{1,0:T(8,128)(2,1)} collective-permute-done((bf16[1024,2048]{1,0:T(8,128)(2,1)S(1)}, bf16[1024,2048]{1,0:T(8,128)(2,1)}, u32[]{:S(2)}, u32[]{:S(2)}) %collective-permute-start.19) | collective-permute-done | bytes 4194336 | tf_op jit(solution)/shard_map/ppermute | solution.py:85
  495.3 4.8 constant_dynamic-update-slice_fusion.25
  500.1 6.4 copy.134
  506.5 4.8 constant_dynamic-update-slice_fusion.24
  511.6 37.4 %all-gather = f32[512,128]{1,0:T(8,128)S(1)} all-gather(f32[16,128]{1,0:T(8,128)S(1)} %fusion.110), channel_id=2, replica_groups=mesh['ey'=2,'ex'=2,'dz'=4,'dc'=2] {'ey','ex','dz','dc'}, dimensions={0}, use_global_device_ids=true | all-gather | bytes 270336 | tf_op jit(solution)/shard_map/all_gather | solution.py:295
  558.2 12.3 fusion.137
  570.5 12.3 bitcast_reduce_fusion
  582.8 6.8 multiply_convert_fusion.2
  589.6 11.0 convolution_convert_fusion
  604.3 4.9 convolution_convert_fusion.1
  615.0 6.2 fusion.136
  624.4 8.6 fusion.138
  637.8 7.2 bitcast_reduce_fusion.1
  647.5 6.6 add_convert_fusion.2
  655.2 6.7 convolution_convert_fusion.5
  678.0 6.4 convolution_convert_fusion.6
  688.6 5.7 fusion.3
  702.6 51.0 %collective-permute-done.22 = bf16[1024,2048]{1,0:T(8,128)(2,1)} collective-permute-done((bf16[1024,2048]{1,0:T(8,128)(2,1)}, bf16[1024,2048]{1,0:T(8,128)(2,1)}, u32[]{:S(2)}, u32[]{:S(2)}) %collective-permute-start.22) | collective-permute-done | bytes 4194336 | tf_op jit(solution)/shard_map/ppermute | solution.py:85
  757.0 5.8 fusion.6
  762.8 71.6 %reduce-scatter.6.cloned.1.call-done = f32[1,16,128]{2,1,0:T(8,128)} async-done(((f32[32,16,128]{2,1,0:T(8,128)}), f32[1,16,128]{2,1,0:T(8,128)}) %reduce-scatter.6.cloned.1.call-update) | async-done | bytes 8208 | tf_op jit(solution)/shard_map/reduce_scatter | solution.py:356
  836.3 5.7 fusion.5
  853.4 6.7 collective-permute-done.42
  860.3 32.4 %collective-permute-done.43 = bf16[128,2048]{1,0:T(8,128)(2,1)S(1)} collective-permute-done((bf16[128,2048]{1,0:T(8,128)(2,1)}, bf16[128,2048]{1,0:T(8,128)(2,1)S(1)}, u32[]{:S(2)}, u32[]{:S(2)}) %collective-permute-start.43) | collective-permute-done | bytes 524320 | tf_op jit(solution)/shard_map/ppermute | solution.py:85
  893.7 27.5 %collective-permute-done.27 = bf16[128,2048]{1,0:T(8,128)(2,1)S(1)} collective-permute-done((bf16[128,2048]{1,0:T(8,128)(2,1)S(1)}, bf16[128,2048]{1,0:T(8,128)(2,1)S(1)}, u32[]{:S(2)}, u32[]{:S(2)}) %collective-permute-start.27) | collective-permute-done | bytes 524320 | tf_op jit(solution)/shard_map/ppermute | solution.py:85
  927.8 27.2 %all_to_all.40 = bf16[8,128,256]{1,2,0:T(8,128)(2,1)S(1)} all-to-all(bf16[8,128,256]{1,2,0:T(8,128)(2,1)S(1)} %bitcast.454), channel_id=1, replica_groups=mesh['ey'=2,'ex'=2,'dz'=4,'dc'=2] {'dz','dc'}, dimensions={0} | all-to-all | bytes 1048576 | tf_op jit(solution)/shard_map/all_to_all | solution.py:372
  955.5 4.9 multiply_reduce_fusion
  990.3 5.4 convolution_convert_fusion.8
  1000.0 5.5 add_convert_fusion.4
  1014.1 10.9 collective-permute-done.50
  1025.0 21.7 %collective-permute-done.51 = bf16[128,2048]{1,0:T(8,128)(2,1)} collective-permute-done((bf16[128,2048]{1,0:T(8,128)(2,1)}, bf16[128,2048]{1,0:T(8,128)(2,1)}, u32[]{:S(2)}, u32[]{:S(2)}) %collective-permute-start.51) | collective-permute-done | bytes 524320 | tf_op jit(solution)/shard_map/ppermute | solution.py:85
  1050.4 5.8 convolution_convert_fusion.2
  1056.2 5.0 fusion.139
  1065.8 8.2 add_convert_fusion.3
  1074.0 14.7 %all-to-all-start.7 = ((bf16[8,256,512]{2,1,0:T(8,128)(2,1)}), bf16[8,256,512]{2,1,0:T(8,128)(2,1)}, u32[]{:S(2)}, u32[]{:S(2)}) async-start(bf16[8,256,512]{2,1,0:T(8,128)(2,1)} %bitcast.451), calls=%async_computation.9 | async-start | bytes 4194304 | tf_op jit(solution)/shard_map/all_to_all | solution.py:348
  1088.7 10.9 fusion.33
  1099.6 8.0 fusion.32
  1107.7 17.7 %add_convert_fusion = bf16[2048,1024]{1,0:T(8,128)(2,1)} fusion(f32[2048,1024]{1,0:T(8,128)} %fusion.33, f32[2048,1024]{1,0:T(8,128)} %fusion.32, bf16[2048,2048]{1,0:T(8,128)(2,1)} %copy-done.46, bf16[2048,512]{0,1:T(8,128)(2,1)} %get-tuple-element.36, bf16[2048,512]{0,1:T(8,128)(2,1)S(1)} %copy-done.40), kind=kOutput, calls=%fused_computation.2 | convolution fusion | flops 8604614656 | bytes 33554432 | tf_op jit(solution)/shard_map/dot_general | solution.py:61
  1125.4 16.6 %all-to-all-done.7 = bf16[8,256,512]{2,1,0:T(8,128)(2,1)} async-done(((bf16[8,256,512]{2,1,0:T(8,128)(2,1)}), bf16[8,256,512]{2,1,0:T(8,128)(2,1)}, u32[]{:S(2)}, u32[]{:S(2)}) %all-to-all-start.7) | async-done | bytes 2097184 | tf_op jit(solution)/shard_map/all_to_all | solution.py:348
  1146.8 6.0 convolution_convert_fusion.7
  1157.7 19.6 %collective-permute-done.53 = bf16[2,512,768]{2,1,0:T(8,128)(2,1)} collective-permute-done((bf16[2,512,768]{2,1,0:T(8,128)(2,1)}, bf16[2,512,768]{2,1,0:T(8,128)(2,1)}, u32[]{:S(2)}, u32[]{:S(2)}) %collective-permute-start.53) | collective-permute-done | bytes 1572896 | tf_op jit(solution)/shard_map/ppermute | solution.py:85
  1181.1 10.5 collective-permute-done.54
  1192.7 76.0 %all-to-all-done.6 = bf16[8,256,1024]{2,1,0:T(8,128)(2,1)} async-done(((bf16[8,256,1024]{2,1,0:T(8,128)(2,1)}), bf16[8,256,1024]{2,1,0:T(8,128)(2,1)}, u32[]{:S(2)}, u32[]{:S(2)}) %all-to-all-start.6) | async-done | bytes 4194336 | tf_op jit(solution)/shard_map/all_to_all | solution.py:344
  1273.2 4.7 reshape.405
  1277.9 6.7 copy.190
  1284.5 5.2 reshape.402
  1289.8 8.8 reshape.404
  1298.6 11.6 copy.189
  1310.2 10.8 reshape.401
  1330.0 48.2 %reduce-scatter.8.cloned.1.call-done = bf16[64,2048]{1,0:T(8,128)(2,1)} async-done(((bf16[2048,2048]{1,0:T(8,128)(2,1)}), bf16[64,2048]{1,0:T(8,128)(2,1)}) %reduce-scatter.8.cloned.1.call-update) | async-done | bytes 262160 | tf_op jit(solution)/shard_map/reduce_scatter | solution.py:367
  (549 shorter events, 284.8 us)
Async XLA Ops:
  7.2 296.8 %all-gather.4.cloned.1.call-start = ((), (), s32[]{:S(2)}) async-start(), calls=%async_computation.11 | async-start | bytes 8650752 | tf_op jit(solution)/shard_map/all_gather | solution.py:236
  9.0 128.0 %collective-permute-start = (bf16[128,2048]{1,0:T(8,128)(2,1)}, bf16[128,2048]{1,0:T(8,128)(2,1)}, u32[]{:S(2)}, u32[]{:S(2)}) collective-permute-start(bf16[128,2048]{1,0:T(8,128)(2,1)} %param.10), channel_id=1, source_target_pairs={{0,1},{1,0},{2,3},{3,2},{4,5},{5,4},{6,7},{7,6},{8,9},{9,8},{10,11... | collective-permute-start | bytes 1572872 | tf_op jit(solution)/shard_map/ppermute | solution.py:85
  9.6 125.1 %collective-permute-start.1 = (bf16[128,2048]{1,0:T(8,128)(2,1)}, bf16[128,2048]{1,0:T(8,128)(2,1)}, u32[]{:S(2)}, u32[]{:S(2)}) collective-permute-start(bf16[128,2048]{1,0:T(8,128)(2,1)} %param.10), channel_id=1, source_target_pairs={{0,6},{1,7},{2,0},{3,1},{4,2},{5,3},{6,4},{7,5},{8,14},{9,15},{10,... | collective-permute-start | bytes 1572872 | tf_op jit(solution)/shard_map/ppermute | solution.py:85
  14.2 120.8 %collective-permute-start.3 = (bf16[128,2048]{1,0:T(8,128)(2,1)}, bf16[128,2048]{1,0:T(8,128)(2,1)S(1)}, u32[]{:S(2)}, u32[]{:S(2)}) collective-permute-start(bf16[128,2048]{1,0:T(8,128)(2,1)} %param.10), channel_id=1, source_target_pairs={{0,4},{1,5},{2,6},{3,7},{4,0},{5,1},{6,2},{7,3},{8,12},{9,13},{10,... | collective-permute-start | bytes 1572872 | tf_op jit(solution)/shard_map/ppermute | solution.py:85
  14.2 121.0 %collective-permute-start.5 = (bf16[128,2048]{1,0:T(8,128)(2,1)}, bf16[128,2048]{1,0:T(8,128)(2,1)S(1)}, u32[]{:S(2)}, u32[]{:S(2)}) collective-permute-start(bf16[128,2048]{1,0:T(8,128)(2,1)} %param.10), channel_id=1, source_target_pairs={{0,2},{1,3},{2,4},{3,5},{4,6},{5,7},{6,0},{7,1},{8,10},{9,11},{10,... | collective-permute-start | bytes 1572872 | tf_op jit(solution)/shard_map/ppermute | solution.py:85
  19.2 124.7 %all-to-all-start = ((bf16[8,64,768]{2,1,0:T(8,128)(2,1)}), bf16[8,64,768]{2,1,0:T(8,128)(2,1)S(1)}, u32[]{:S(2)}, u32[]{:S(2)}) async-start(bf16[8,64,768]{2,1,0:T(8,128)(2,1)} %reshape_reshape.10), calls=%async_computation | async-start | bytes 1572864 | tf_op jit(solution)/shard_map/all_to_all | solution.py:224
  134.7 7.8 collective-permute-start.2
  135.1 7.7 collective-permute-start.4
  135.2 8.7 collective-permute-start.6
  143.9 12.0 collective-permute-start.7
  156.0 20.5 %collective-permute-start.8 = (bf16[2,512,768]{2,1,0:T(8,128)(2,1)S(1)}, bf16[2,512,768]{2,1,0:T(8,128)(2,1)S(1)}, u32[]{:S(2)}, u32[]{:S(2)}) collective-permute-start(bf16[2,512,768]{2,1,0:T(8,128)(2,1)S(1)} %pad_maximum_fusion.8), channel_id=1, source_target_pairs={{0,16},{1,9},{2,18},{3,11},{4,20},{5,13},{6,22},{7,15},{8,24},{9,1... | collective-permute-start | bytes 4718600 | tf_op jit(solution)/shard_map/ppermute | solution.py:85
  182.2 14.3 %collective-permute-start.10 = (f32[2,1024]{1,0:T(2,128)S(1)}, f32[2,1024]{1,0:T(2,128)S(1)}, u32[]{:S(2)}, u32[]{:S(2)}) collective-permute-start(f32[2,1024]{1,0:T(2,128)S(1)} %fusion.125), channel_id=1, source_target_pairs={{0,6},{1,7},{2,0},{3,1},{4,2},{5,3},{6,4},{7,5},{8,14},{9,15},{10,... | collective-permute-start | bytes 24584 | tf_op jit(solution)/shard_map/ppermute | solution.py:85
  182.5 14.0 %collective-permute-start.11 = (f32[2,1024]{1,0:T(2,128)S(1)}, f32[2,1024]{1,0:T(2,128)S(1)}, u32[]{:S(2)}, u32[]{:S(2)}) collective-permute-start(f32[2,1024]{1,0:T(2,128)S(1)} %fusion.125), channel_id=1, source_target_pairs={{0,4},{1,5},{2,6},{3,7},{4,0},{5,1},{6,2},{7,3},{8,12},{9,13},{10,... | collective-permute-start | bytes 24584 | tf_op jit(solution)/shard_map/ppermute | solution.py:85
  185.7 15.4 %collective-permute-start.12 = (f32[2,1024]{1,0:T(2,128)S(1)}, f32[2,1024]{1,0:T(2,128)S(1)}, u32[]{:S(2)}, u32[]{:S(2)}) collective-permute-start(f32[2,1024]{1,0:T(2,128)S(1)} %fusion.125), channel_id=1, source_target_pairs={{0,2},{1,3},{2,4},{3,5},{4,6},{5,7},{6,0},{7,1},{8,10},{9,11},{10,... | collective-permute-start | bytes 24584 | tf_op jit(solution)/shard_map/ppermute | solution.py:85
  214.0 19.3 %all-to-all-start.1 = ((bf16[8,128,256]{1,2,0:T(8,128)(2,1)}), bf16[8,128,256]{1,2,0:T(8,128)(2,1)S(1)}, u32[]{:S(2)}, u32[]{:S(2)}) async-start(bf16[8,128,256]{1,2,0:T(8,128)(2,1)} %copy.128), calls=%async_computation.1 | async-start | bytes 1048576 | tf_op jit(solution)/shard_map/all_to_all | solution.py:273
  218.6 40.0 %collective-permute-start.29 = (bf16[128,2048]{1,0:T(8,128)(2,1)}, bf16[128,2048]{1,0:T(8,128)(2,1)}, u32[]{:S(2)}, u32[]{:S(2)}) collective-permute-start(bf16[128,2048]{1,0:T(8,128)(2,1)} %get-tuple-element.29), channel_id=1, source_target_pairs={{0,6},{1,7},{2,0},{3,1},{4,2},{5,3},{6,4},{7,5},{8,14},{9,15},{10,... | collective-permute-start | bytes 1572872 | tf_op jit(solution)/shard_map/ppermute | solution.py:85
  222.3 78.4 %collective-permute-start.30 = (bf16[128,2048]{1,0:T(8,128)(2,1)}, bf16[128,2048]{1,0:T(8,128)(2,1)}, u32[]{:S(2)}, u32[]{:S(2)}) collective-permute-start(bf16[128,2048]{1,0:T(8,128)(2,1)} %get-tuple-element.29), channel_id=1, source_target_pairs={{0,4},{1,5},{2,6},{3,7},{4,0},{5,1},{6,2},{7,3},{8,12},{9,13},{10,... | collective-permute-start | bytes 1572872 | tf_op jit(solution)/shard_map/ppermute | solution.py:85
  222.4 78.4 %collective-permute-start.31 = (bf16[128,2048]{1,0:T(8,128)(2,1)}, bf16[128,2048]{1,0:T(8,128)(2,1)}, u32[]{:S(2)}, u32[]{:S(2)}) collective-permute-start(bf16[128,2048]{1,0:T(8,128)(2,1)} %get-tuple-element.29), channel_id=1, source_target_pairs={{0,2},{1,3},{2,4},{3,5},{4,6},{5,7},{6,0},{7,1},{8,10},{9,11},{10,... | collective-permute-start | bytes 1572872 | tf_op jit(solution)/shard_map/ppermute | solution.py:85
  234.0 164.0 %all-to-all-start.3 = ((bf16[8,256,512]{1,2,0:T(8,128)(2,1)}), bf16[8,256,512]{1,2,0:T(8,128)(2,1)S(1)}, u32[]{:S(2)}, u32[]{:S(2)}) async-start(bf16[8,256,512]{1,2,0:T(8,128)(2,1)} %bitcast.419), calls=%async_computation.3 | async-start | bytes 4194304 | tf_op jit(solution)/shard_map/all_to_all | solution.py:243
  303.8 72.8 %collective-permute-start.34 = (bf16[512,2048]{1,0:T(8,128)(2,1)}, bf16[512,2048]{1,0:T(8,128)(2,1)}, u32[]{:S(2)}, u32[]{:S(2)}) collective-permute-start(bf16[512,2048]{1,0:T(8,128)(2,1)} %pad_maximum_fusion.5), channel_id=1, source_target_pairs={{0,8},{1,17},{2,10},{3,19},{4,12},{5,21},{6,14},{7,23},{8,0},{9,25... | collective-permute-start | bytes 6291464 | tf_op jit(solution)/shard_map/ppermute | solution.py:85
  310.8 21.3 %collective-permute-start.13 = (bf16[128,2048]{1,0:T(8,128)(2,1)S(1)}, bf16[128,2048]{1,0:T(8,128)(2,1)S(1)}, u32[]{:S(2)}, u32[]{:S(2)}) collective-permute-start(bf16[128,2048]{1,0:T(8,128)(2,1)S(1)} %get-tuple-element.31), channel_id=1, source_target_pairs={{0,6},{1,7},{2,0},{3,1},{4,2},{5,3},{6,4},{7,5},{8,14},{9,15},{10,... | collective-permute-start | bytes 1572872 | tf_op jit(solution)/shard_map/ppermute | solution.py:85
  310.8 56.8 %collective-permute-start.14 = (bf16[128,2048]{1,0:T(8,128)(2,1)S(1)}, bf16[128,2048]{1,0:T(8,128)(2,1)S(1)}, u32[]{:S(2)}, u32[]{:S(2)}) collective-permute-start(bf16[128,2048]{1,0:T(8,128)(2,1)S(1)} %get-tuple-element.31), channel_id=1, source_target_pairs={{0,4},{1,5},{2,6},{3,7},{4,0},{5,1},{6,2},{7,3},{8,12},{9,13},{10,... | collective-permute-start | bytes 1572872 | tf_op jit(solution)/shard_map/ppermute | solution.py:85
  310.8 56.8 %collective-permute-start.15 = (bf16[128,2048]{1,0:T(8,128)(2,1)S(1)}, bf16[128,2048]{1,0:T(8,128)(2,1)S(1)}, u32[]{:S(2)}, u32[]{:S(2)}) collective-permute-start(bf16[128,2048]{1,0:T(8,128)(2,1)S(1)} %get-tuple-element.31), channel_id=1, source_target_pairs={{0,2},{1,3},{2,4},{3,5},{4,6},{5,7},{6,0},{7,1},{8,10},{9,11},{10,... | collective-permute-start | bytes 1572872 | tf_op jit(solution)/shard_map/ppermute | solution.py:85
  370.0 42.3 %collective-permute-start.18 = (bf16[512,2048]{1,0:T(8,128)(2,1)}, bf16[512,2048]{1,0:T(8,128)(2,1)}, u32[]{:S(2)}, u32[]{:S(2)}) collective-permute-start(bf16[512,2048]{1,0:T(8,128)(2,1)} %pad_maximum_fusion.4), channel_id=1, source_target_pairs={{0,8},{1,17},{2,10},{3,19},{4,12},{5,21},{6,14},{7,23},{8,0},{9,25... | collective-permute-start | bytes 6291464 | tf_op jit(solution)/shard_map/ppermute | solution.py:85
  380.8 59.2 %collective-permute-start.35 = (bf16[1024,2048]{1,0:T(8,128)(2,1)}, bf16[1024,2048]{1,0:T(8,128)(2,1)}, u32[]{:S(2)}, u32[]{:S(2)}) collective-permute-start(bf16[1024,2048]{1,0:T(8,128)(2,1)} %get-tuple-element.62), channel_id=1, source_target_pairs={{0,16},{1,9},{2,18},{3,11},{4,20},{5,13},{6,22},{7,15},{8,24},{9,1... | collective-permute-start | bytes 12582920 | tf_op jit(solution)/shard_map/ppermute | solution.py:85
  398.0 102.1 %all-to-all-start.2 = ((bf16[8,256,1024]{1,2,0:T(8,128)(2,1)}), bf16[8,256,1024]{1,2,0:T(8,128)(2,1)}, u32[]{:S(2)}, u32[]{:S(2)}) async-start(bf16[8,256,1024]{1,2,0:T(8,128)(2,1)} %bitcast.409), calls=%async_computation.2 | async-start | bytes 8388608 | tf_op jit(solution)/shard_map/all_to_all | solution.py:240
  402.6 431.9 %reduce-scatter.6.cloned.1.call-start = ((), (), s32[]{:S(2)}) async-start(), calls=%async_computation.12 | async-start | bytes 270336 | tf_op jit(solution)/shard_map/reduce_scatter | solution.py:356
  415.5 69.4 %collective-permute-start.19 = (bf16[1024,2048]{1,0:T(8,128)(2,1)S(1)}, bf16[1024,2048]{1,0:T(8,128)(2,1)}, u32[]{:S(2)}, u32[]{:S(2)}) collective-permute-start(bf16[1024,2048]{1,0:T(8,128)(2,1)S(1)} %get-tuple-element.60), channel_id=1, source_target_pairs={{0,16},{1,9},{2,18},{3,11},{4,20},{5,13},{6,22},{7,15},{8,24},{9,1... | collective-permute-start | bytes 12582920 | tf_op jit(solution)/shard_map/ppermute | solution.py:85
  440.0 66.5 %collective-permute-start.36 = (bf16[1024,2048]{1,0:T(8,128)(2,1)}, bf16[1024,2048]{1,0:T(8,128)(2,1)}, u32[]{:S(2)}, u32[]{:S(2)}) collective-permute-start(bf16[1024,2048]{1,0:T(8,128)(2,1)} %collective-permute-done.35), channel_id=1, source_target_pairs={{0,1},{1,0},{2,3},{3,2},{4,5},{5,4},{6,7},{7,6},{8,9},{9,8},{10,11... | collective-permute-start | bytes 12582920 | tf_op jit(solution)/shard_map/ppermute | solution.py:85
  441.4 45.1 %collective-permute-start.32 = (bf16[512,2048]{1,0:T(8,128)(2,1)}, bf16[512,2048]{1,0:T(8,128)(2,1)}, u32[]{:S(2)}, u32[]{:S(2)}) collective-permute-start(bf16[512,2048]{1,0:T(8,128)(2,1)} %pad_maximum_fusion.5), channel_id=1, source_target_pairs={{0,1},{1,0},{2,3},{3,2},{4,5},{5,4},{6,7},{7,6},{8,9},{9,8},{10,11... | collective-permute-start | bytes 6291464 | tf_op jit(solution)/shard_map/ppermute | solution.py:85
  441.4 50.7 %collective-permute-start.39 = (bf16[512,2048]{1,0:T(8,128)(2,1)}, bf16[512,2048]{1,0:T(8,128)(2,1)}, u32[]{:S(2)}, u32[]{:S(2)}) collective-permute-start(bf16[512,2048]{1,0:T(8,128)(2,1)} %collective-permute-done.34), channel_id=1, source_target_pairs={{0,1},{1,0},{2,3},{3,2},{4,5},{5,4},{6,7},{7,6},{8,9},{9,8},{10,11... | collective-permute-start | bytes 6291464 | tf_op jit(solution)/shard_map/ppermute | solution.py:85
  484.9 67.3 %collective-permute-start.20 = (bf16[1024,2048]{1,0:T(8,128)(2,1)}, bf16[1024,2048]{1,0:T(8,128)(2,1)}, u32[]{:S(2)}, u32[]{:S(2)}) collective-permute-start(bf16[1024,2048]{1,0:T(8,128)(2,1)} %collective-permute-done.19), channel_id=1, source_target_pairs={{0,1},{1,0},{2,3},{3,2},{4,5},{5,4},{6,7},{7,6},{8,9},{9,8},{10,11... | collective-permute-start | bytes 12582920 | tf_op jit(solution)/shard_map/ppermute | solution.py:85
  549.3 62.5 %collective-permute-start.16 = (bf16[512,2048]{1,0:T(8,128)(2,1)}, bf16[512,2048]{1,0:T(8,128)(2,1)}, u32[]{:S(2)}, u32[]{:S(2)}) collective-permute-start(bf16[512,2048]{1,0:T(8,128)(2,1)} %pad_maximum_fusion.4), channel_id=1, source_target_pairs={{0,1},{1,0},{2,3},{3,2},{4,5},{5,4},{6,7},{7,6},{8,9},{9,8},{10,11... | collective-permute-start | bytes 6291464 | tf_op jit(solution)/shard_map/ppermute | solution.py:85
  603.0 29.9 %collective-permute-start.37 = (bf16[1024,2048]{1,0:T(8,128)(2,1)}, bf16[1024,2048]{1,0:T(8,128)(2,1)}, u32[]{:S(2)}, u32[]{:S(2)}) collective-permute-start(bf16[1024,2048]{1,0:T(8,128)(2,1)} %slice.305), channel_id=1, source_target_pairs={{0,1},{1,0},{2,3},{3,2},{4,5},{5,4},{6,7},{7,6},{8,9},{9,8},{10,11... | collective-permute-start | bytes 12582920 | tf_op jit(solution)/shard_map/ppermute | solution.py:85
  603.2 18.0 %collective-permute-start.23 = (bf16[512,2048]{1,0:T(8,128)(2,1)}, bf16[512,2048]{1,0:T(8,128)(2,1)}, u32[]{:S(2)}, u32[]{:S(2)}) collective-permute-start(bf16[512,2048]{1,0:T(8,128)(2,1)} %collective-permute-done.18), channel_id=1, source_target_pairs={{0,1},{1,0},{2,3},{3,2},{4,5},{5,4},{6,7},{7,6},{8,9},{9,8},{10,11... | collective-permute-start | bytes 6291464 | tf_op jit(solution)/shard_map/ppermute | solution.py:85
  611.6 35.9 %collective-permute-start.21 = (bf16[1024,2048]{1,0:T(8,128)(2,1)}, bf16[1024,2048]{1,0:T(8,128)(2,1)}, u32[]{:S(2)}, u32[]{:S(2)}) collective-permute-start(bf16[1024,2048]{1,0:T(8,128)(2,1)} %slice.290), channel_id=1, source_target_pairs={{0,1},{1,0},{2,3},{3,2},{4,5},{5,4},{6,7},{7,6},{8,9},{9,8},{10,11... | collective-permute-start | bytes 12582920 | tf_op jit(solution)/shard_map/ppermute | solution.py:85
  637.1 50.5 %collective-permute-start.38 = (bf16[1024,2048]{1,0:T(8,128)(2,1)S(1)}, bf16[1024,2048]{1,0:T(8,128)(2,1)S(1)}, u32[]{:S(2)}, u32[]{:S(2)}) collective-permute-start(bf16[1024,2048]{1,0:T(8,128)(2,1)S(1)} %add_convert_fusion.1), channel_id=1, source_target_pairs={{0,16},{1,9},{2,18},{3,11},{4,20},{5,13},{6,22},{7,15},{8,24},{9,1... | collective-permute-start | bytes 12582920 | tf_op jit(solution)/shard_map/ppermute | solution.py:85
  654.1 99.5 %collective-permute-start.22 = (bf16[1024,2048]{1,0:T(8,128)(2,1)}, bf16[1024,2048]{1,0:T(8,128)(2,1)}, u32[]{:S(2)}, u32[]{:S(2)}) collective-permute-start(bf16[1024,2048]{1,0:T(8,128)(2,1)} %add_convert_fusion.2), channel_id=1, source_target_pairs={{0,16},{1,9},{2,18},{3,11},{4,20},{5,13},{6,22},{7,15},{8,24},{9,1... | collective-permute-start | bytes 12582920 | tf_op jit(solution)/shard_map/ppermute | solution.py:85
  663.4 25.3 %collective-permute-start.40 = (bf16[512,2048]{1,0:T(8,128)(2,1)}, bf16[512,2048]{1,0:T(8,128)(2,1)}, u32[]{:S(2)}, u32[]{:S(2)}) collective-permute-start(bf16[512,2048]{1,0:T(8,128)(2,1)} %slice.308), channel_id=1, source_target_pairs={{0,1},{1,0},{2,3},{3,2},{4,5},{5,4},{6,7},{7,6},{8,9},{9,8},{10,11... | collective-permute-start | bytes 6291464 | tf_op jit(solution)/shard_map/ppermute | solution.py:85
  675.0 82.0 %collective-permute-start.24 = (bf16[512,2048]{1,0:T(8,128)(2,1)}, bf16[512,2048]{1,0:T(8,128)(2,1)}, u32[]{:S(2)}, u32[]{:S(2)}) collective-permute-start(bf16[512,2048]{1,0:T(8,128)(2,1)} %slice.296), channel_id=1, source_target_pairs={{0,1},{1,0},{2,3},{3,2},{4,5},{5,4},{6,7},{7,6},{8,9},{9,8},{10,11... | collective-permute-start | bytes 6291464 | tf_op jit(solution)/shard_map/ppermute | solution.py:85
  687.6 148.7 %collective-permute-start.33 = (bf16[512,2048]{1,0:T(8,128)(2,1)}, bf16[512,2048]{1,0:T(8,128)(2,1)}, u32[]{:S(2)}, u32[]{:S(2)}) collective-permute-start(bf16[512,2048]{1,0:T(8,128)(2,1)} %slice.303), channel_id=1, source_target_pairs={{0,1},{1,0},{2,3},{3,2},{4,5},{5,4},{6,7},{7,6},{8,9},{9,8},{10,11... | collective-permute-start | bytes 6291464 | tf_op jit(solution)/shard_map/ppermute | solution.py:85
  694.4 141.9 %collective-permute-start.41 = (bf16[512,2048]{1,0:T(8,128)(2,1)}, bf16[512,2048]{1,0:T(8,128)(2,1)}, u32[]{:S(2)}, u32[]{:S(2)}) collective-permute-start(bf16[512,2048]{1,0:T(8,128)(2,1)} %fusion.3), channel_id=1, source_target_pairs={{0,8},{1,17},{2,10},{3,19},{4,12},{5,21},{6,14},{7,23},{8,0},{9,25... | collective-permute-start | bytes 6291464 | tf_op jit(solution)/shard_map/ppermute | solution.py:85
  700.3 146.7 %collective-permute-start.17 = (bf16[512,2048]{1,0:T(8,128)(2,1)}, bf16[512,2048]{1,0:T(8,128)(2,1)}, u32[]{:S(2)}, u32[]{:S(2)}) collective-permute-start(bf16[512,2048]{1,0:T(8,128)(2,1)} %slice.285), channel_id=1, source_target_pairs={{0,1},{1,0},{2,3},{3,2},{4,5},{5,4},{6,7},{7,6},{8,9},{9,8},{10,11... | collective-permute-start | bytes 6291464 | tf_op jit(solution)/shard_map/ppermute | solution.py:85
  702.6 619.7 %reduce-scatter.10.cloned.1.call-start = ((), (), s32[]{:S(2)}) async-start(), calls=%async_computation.14 | async-start | bytes 1081344
  762.8 84.2 %collective-permute-start.25 = (bf16[512,2048]{1,0:T(8,128)(2,1)}, bf16[512,2048]{1,0:T(8,128)(2,1)}, u32[]{:S(2)}, u32[]{:S(2)}) collective-permute-start(bf16[512,2048]{1,0:T(8,128)(2,1)} %fusion.6), channel_id=1, source_target_pairs={{0,8},{1,17},{2,10},{3,19},{4,12},{5,21},{6,14},{7,23},{8,0},{9,25... | collective-permute-start | bytes 6291464 | tf_op jit(solution)/shard_map/ppermute | solution.py:85
  843.2 16.9 %collective-permute-start.42 = (bf16[128,2048]{1,0:T(8,128)(2,1)}, bf16[128,2048]{1,0:T(8,128)(2,1)S(1)}, u32[]{:S(2)}, u32[]{:S(2)}) collective-permute-start(bf16[128,2048]{1,0:T(8,128)(2,1)} %get-tuple-element.53), channel_id=1, source_target_pairs={{0,2},{1,3},{2,4},{3,5},{4,6},{5,7},{6,0},{7,1},{8,10},{9,11},{10,... | collective-permute-start | bytes 1572872 | tf_op jit(solution)/shard_map/ppermute | solution.py:85
  843.2 49.5 %collective-permute-start.43 = (bf16[128,2048]{1,0:T(8,128)(2,1)}, bf16[128,2048]{1,0:T(8,128)(2,1)S(1)}, u32[]{:S(2)}, u32[]{:S(2)}) collective-permute-start(bf16[128,2048]{1,0:T(8,128)(2,1)} %get-tuple-element.55), channel_id=1, source_target_pairs={{0,4},{1,5},{2,6},{3,7},{4,0},{5,1},{6,2},{7,3},{8,12},{9,13},{10,... | collective-permute-start | bytes 1572872 | tf_op jit(solution)/shard_map/ppermute | solution.py:85
  843.2 49.5 %collective-permute-start.44 = (bf16[128,2048]{1,0:T(8,128)(2,1)}, bf16[128,2048]{1,0:T(8,128)(2,1)S(1)}, u32[]{:S(2)}, u32[]{:S(2)}) collective-permute-start(bf16[128,2048]{1,0:T(8,128)(2,1)} %get-tuple-element.54), channel_id=1, source_target_pairs={{0,6},{1,7},{2,0},{3,1},{4,2},{5,3},{6,4},{7,5},{8,14},{9,15},{10,... | collective-permute-start | bytes 1572872 | tf_op jit(solution)/shard_map/ppermute | solution.py:85
  851.3 42.5 %collective-permute-start.26 = (bf16[128,2048]{1,0:T(8,128)(2,1)S(1)}, bf16[128,2048]{1,0:T(8,128)(2,1)S(1)}, u32[]{:S(2)}, u32[]{:S(2)}) collective-permute-start(bf16[128,2048]{1,0:T(8,128)(2,1)S(1)} %get-tuple-element.56), channel_id=1, source_target_pairs={{0,2},{1,3},{2,4},{3,5},{4,6},{5,7},{6,0},{7,1},{8,10},{9,11},{10,... | collective-permute-start | bytes 1572872 | tf_op jit(solution)/shard_map/ppermute | solution.py:85
  851.8 69.4 %collective-permute-start.27 = (bf16[128,2048]{1,0:T(8,128)(2,1)S(1)}, bf16[128,2048]{1,0:T(8,128)(2,1)S(1)}, u32[]{:S(2)}, u32[]{:S(2)}) collective-permute-start(bf16[128,2048]{1,0:T(8,128)(2,1)S(1)} %get-tuple-element.58), channel_id=1, source_target_pairs={{0,4},{1,5},{2,6},{3,7},{4,0},{5,1},{6,2},{7,3},{8,12},{9,13},{10,... | collective-permute-start | bytes 1572872 | tf_op jit(solution)/shard_map/ppermute | solution.py:85
  860.1 61.2 %collective-permute-start.28 = (bf16[128,2048]{1,0:T(8,128)(2,1)S(1)}, bf16[128,2048]{1,0:T(8,128)(2,1)S(1)}, u32[]{:S(2)}, u32[]{:S(2)}) collective-permute-start(bf16[128,2048]{1,0:T(8,128)(2,1)S(1)} %get-tuple-element.57), channel_id=1, source_target_pairs={{0,6},{1,7},{2,0},{3,1},{4,2},{5,3},{6,4},{7,5},{8,14},{9,15},{10,... | collective-permute-start | bytes 1572872 | tf_op jit(solution)/shard_map/ppermute | solution.py:85
  972.6 9.0 collective-permute-start.46
  974.0 7.7 collective-permute-start.47
  974.0 7.7 collective-permute-start.48
  995.7 4.2 collective-permute-start.49
  1008.0 17.0 %collective-permute-start.50 = (bf16[128,2048]{1,0:T(8,128)(2,1)}, bf16[128,2048]{1,0:T(8,128)(2,1)}, u32[]{:S(2)}, u32[]{:S(2)}) collective-permute-start(bf16[128,2048]{1,0:T(8,128)(2,1)} %get-tuple-element.50), channel_id=1, source_target_pairs={{0,2},{1,3},{2,4},{3,5},{4,6},{5,7},{6,0},{7,1},{8,10},{9,11},{10,... | collective-permute-start | bytes 1572872 | tf_op jit(solution)/shard_map/ppermute | solution.py:85
  1010.7 36.0 %collective-permute-start.51 = (bf16[128,2048]{1,0:T(8,128)(2,1)}, bf16[128,2048]{1,0:T(8,128)(2,1)}, u32[]{:S(2)}, u32[]{:S(2)}) collective-permute-start(bf16[128,2048]{1,0:T(8,128)(2,1)} %get-tuple-element.52), channel_id=1, source_target_pairs={{0,4},{1,5},{2,6},{3,7},{4,0},{5,1},{6,2},{7,3},{8,12},{9,13},{10,... | collective-permute-start | bytes 1572872 | tf_op jit(solution)/shard_map/ppermute | solution.py:85
  1011.6 35.1 %collective-permute-start.52 = (bf16[128,2048]{1,0:T(8,128)(2,1)S(1)}, bf16[128,2048]{1,0:T(8,128)(2,1)}, u32[]{:S(2)}, u32[]{:S(2)}) collective-permute-start(bf16[128,2048]{1,0:T(8,128)(2,1)S(1)} %get-tuple-element.51), channel_id=1, source_target_pairs={{0,6},{1,7},{2,0},{3,1},{4,2},{5,3},{6,4},{7,5},{8,14},{9,15},{10,... | collective-permute-start | bytes 1572872 | tf_op jit(solution)/shard_map/ppermute | solution.py:85
  1050.2 328.0 %reduce-scatter.8.cloned.1.call-start = ((), (), s32[]{:S(2)}) async-start(), calls=%async_computation.13 | async-start | bytes 8650752 | tf_op jit(solution)/shard_map/reduce_scatter | solution.py:367
  1074.0 68.1 %all-to-all-start.7 = ((bf16[8,256,512]{2,1,0:T(8,128)(2,1)}), bf16[8,256,512]{2,1,0:T(8,128)(2,1)}, u32[]{:S(2)}, u32[]{:S(2)}) async-start(bf16[8,256,512]{2,1,0:T(8,128)(2,1)} %bitcast.451), calls=%async_computation.9 | async-start | bytes 4194304 | tf_op jit(solution)/shard_map/all_to_all | solution.py:348
  1142.0 126.7 %all-to-all-start.6 = ((bf16[8,256,1024]{2,1,0:T(8,128)(2,1)}), bf16[8,256,1024]{2,1,0:T(8,128)(2,1)}, u32[]{:S(2)}, u32[]{:S(2)}) async-start(bf16[8,256,1024]{2,1,0:T(8,128)(2,1)} %bitcast.429), calls=%async_computation.8 | async-start | bytes 8388608 | tf_op jit(solution)/shard_map/all_to_all | solution.py:344
  1155.9 21.5 %collective-permute-start.53 = (bf16[2,512,768]{2,1,0:T(8,128)(2,1)}, bf16[2,512,768]{2,1,0:T(8,128)(2,1)}, u32[]{:S(2)}, u32[]{:S(2)}) collective-permute-start(bf16[2,512,768]{2,1,0:T(8,128)(2,1)} %pad_maximum_fusion.10), channel_id=1, source_target_pairs={{0,16},{1,9},{2,18},{3,11},{4,20},{5,13},{6,22},{7,15},{8,24},{9,1... | collective-permute-start | bytes 4718600 | tf_op jit(solution)/shard_map/ppermute | solution.py:85
  1179.2 12.4 collective-permute-start.54
  1268.8 56.4 %all-to-all-start.5 = ((bf16[8,64,768]{2,1,0:T(8,128)(2,1)}), bf16[8,64,768]{2,1,0:T(8,128)(2,1)}, u32[]{:S(2)}, u32[]{:S(2)}) async-start(bf16[8,64,768]{2,1,0:T(8,128)(2,1)} %bitcast.437), calls=%async_computation.6 | async-start | bytes 1572864 | tf_op jit(solution)/shard_map/all_to_all | solution.py:427
  (129 other events, 3367.6 us)
Sparse Core Ops, SparseCore 0:
  11.6 110.9 all-gather.3
  702.7 131.7 reduce-scatter.5
  1050.3 152.4 reduce-scatter.9
  1204.9 173.2 reduce-scatter.7

commit v2 on v1

--- a/solution.py
+++ b/solution.py
@@ -1,7 +1,10 @@
+import functools
+
 import jax
 import jax.numpy as jnp
-import numpy as np
 from jax import lax
+from jax.experimental import pallas as pl
+from jax.experimental.pallas import tpu as pltpu
 from jax.sharding import Mesh
 from jax.sharding import PartitionSpec as P
 
@@ -65,90 +68,625 @@
 SEQ = ("dz", "dc")
 
 
-class Moves:
+MESH_ID = pl.DeviceIdType.MESH
+
+
+class Place:
     def __init__(self, depth):
         self.depth = depth
-        self.count = 2 * 2 * depth * 2
-
-    def pairs(self, move):
-        result = []
-        for index in range(self.count):
-            c = index % 2
-            z = index // 2 % self.depth
-            x = index // (2 * self.depth) % 2
-            y = index // (4 * self.depth)
-            y, x, z, c = move(y, x, z, c)
-            result.append((index, ((y * 2 + x) * self.depth + z) * 2 + c))
-        return result
-
-    def send(self, values, move):
-        return lax.ppermute(values, GRID, self.pairs(move))
-
-    def core(self, values):
-        return self.send(values, lambda y, x, z, c: (y, x, z, 1 - c))
-
-    def from_z(self, values, step):
-        return self.send(values, lambda y, x, z, c: (y, x, (z - step) % self.depth, c))
-
-    def to_z(self, values, step):
-        return self.send(values, lambda y, x, z, c: (y, x, (z + step) % self.depth, c))
-
-    def near(self, values):
-        return self.send(
-            values, lambda y, x, z, c: (y, 1 - x, z, c) if c == 0 else (1 - y, x, z, c)
+        self.y, self.x, self.z, self.c = (lax.axis_index(name) for name in GRID)
+
+    def near_of(self, core):
+        return self.y + core * (1 - 2 * self.y), self.x + (1 - core) * (1 - 2 * self.x)
+
+    def far_of(self, core):
+        return self.near_of(1 - core)
+
+    def along(self, step):
+        return lax.rem(self.z + step, self.depth)
+
+    def block(self, column, z, core):
+        return ((column[0] * 2 + column[1]) * self.depth + z) * 2 + core
+
+    @property
+    def own_column(self):
+        return self.y, self.x
+
+    @property
+    def other_column(self):
+        return 1 - self.y, 1 - self.x
+
+    def core(self):
+        return self.y, self.x, self.z, 1 - self.c
+
+    def chip(self, step, core=None):
+        return self.y, self.x, self.along(step), self.c if core is None else core
+
+    def near(self):
+        return (*self.near_of(self.c), self.z, self.c)
+
+    def far(self):
+        return (*self.far_of(self.c), self.z, self.c)
+
+
+def meet(partners):
+    barrier = pltpu.get_barrier_semaphore()
+    for partner in partners:
+        pl.semaphore_signal(barrier, inc=1, device_id=partner, device_id_type=MESH_ID)
+    pl.semaphore_wait(barrier, len(partners))
+
+
+def remote(source, target, sems, slot, partner):
+    return pltpu.make_async_remote_copy(
+        src_ref=source,
+        dst_ref=target,
+        send_sem=sems[0].at[slot],
+        recv_sem=sems[1].at[slot],
+        device_id=partner,
+        device_id_type=MESH_ID,
+    )
+
+
+def pair(count):
+    return [pltpu.SemaphoreType.DMA((count,)), pltpu.SemaphoreType.DMA((count,))]
+
+
+def in_hbm(count):
+    return [pl.BlockSpec(memory_space=pl.ANY)] * count
+
+
+def spread_kernel(depth, count, extra, *refs):
+    whole = count + extra
+    sources, targets, sems = refs[:count], refs[whole : whole + count], refs[2 * whole :]
+    extra_sources, extra_targets = refs[count:whole], refs[whole + count : 2 * whole]
+    extra_sems = sems[9 * count :]
+    at = Place(depth)
+    others = range(1, depth)
+    ranks = [(k, core) for k in range(depth) for core in range(2) if k or core]
+    peers = [at.chip(k, lax.rem(at.c + core, 2)) for k, core in ranks]
+    meet([at.near(), at.far()] + peers)
+    started, local = [], []
+
+    def push(n, source, index, kind, slot, partner):
+        copy = remote(source, targets[n].at[index], sems[9 * n + 2 * kind :], slot, partner)
+        copy.start()
+        started.append(copy)
+
+    def arrive(n, index, kind, slot):
+        target = targets[n].at[index]
+        remote(target, target, sems[9 * n + 2 * kind :], slot, at.core()).wait_recv()
+
+    z_kind, near_kind, far_kind, core_kind = range(4)
+    own = at.block(at.own_column, at.z, at.c)
+    for n in range(count):
+        for k in others:
+            push(n, sources[n], own, z_kind, k - 1, at.chip(k))
+        push(n, sources[n], own, near_kind, 0, at.near())
+        push(n, sources[n], own, far_kind, 0, at.far())
+        push(n, sources[n], own, core_kind, 0, at.core())
+        copy = pltpu.make_async_copy(sources[n], targets[n].at[own], sems[9 * n + 8])
+        copy.start()
+        local.append(copy)
+    own_rank = at.z * 2 + at.c
+    for n in range(extra):
+        for slot, there in enumerate(peers):
+            copy = remote(
+                extra_sources[n].at[there[2] * 2 + there[3]],
+                extra_targets[n].at[own_rank],
+                extra_sems[3 * n :],
+                slot,
+                there,
+            )
+            copy.start()
+            started.append(copy)
+        copy = pltpu.make_async_copy(
+            extra_sources[n].at[own_rank], extra_targets[n].at[own_rank], extra_sems[3 * n + 2]
         )
-
-    def far(self, values):
-        return self.send(
-            values, lambda y, x, z, c: (1 - y, x, z, c) if c == 0 else (y, 1 - x, z, c)
+        copy.start()
+        local.append(copy)
+    for k in others:
+        index = at.block(at.own_column, at.along(depth - k), at.c)
+        for n in range(count):
+            arrive(n, index, z_kind, k - 1)
+            push(n, targets[n].at[index], index, near_kind, k, at.near())
+            push(n, targets[n].at[index], index, far_kind, k, at.far())
+            push(n, targets[n].at[index], index, core_kind, k, at.core())
+    for k in range(depth):
+        index = at.block(at.near_of(at.c), at.along(depth - k), at.c)
+        for n in range(count):
+            arrive(n, index, near_kind, k)
+            push(n, targets[n].at[index], index, far_kind, depth + k, at.far())
+            push(n, targets[n].at[index], index, core_kind, depth + k, at.core())
+    for j in range(2 * depth):
+        column = at.far_of(at.c) if j < depth else at.other_column
+        index = at.block(column, at.along(depth - j % depth), at.c)
+        for n in range(count):
+            arrive(n, index, far_kind, j)
+            push(n, targets[n].at[index], index, core_kind, 2 * depth + j, at.core())
+    core = 1 - at.c
+    columns = [at.own_column, at.near_of(core), at.far_of(core), at.other_column]
+    for j in range(4 * depth):
+        index = at.block(columns[j // depth], at.along(depth - j % depth), core)
+        for n in range(count):
+            arrive(n, index, core_kind, j)
+    for n in range(extra):
+        for slot, (k, core) in enumerate(ranks):
+            target = extra_targets[n].at[at.along(depth - k) * 2 + lax.rem(at.c + core, 2)]
+            remote(target, target, extra_sems[3 * n :], slot, at.core()).wait_recv()
+    for copy in started:
+        copy.wait_send()
+    for copy in local:
+        copy.wait()
+
+
+def spread(depth, ident, arrays, extras=()):
+    sems = []
+    for _ in arrays:
+        sems += pair(depth - 1) + pair(depth) + pair(2 * depth) + pair(4 * depth)
+        sems.append(pltpu.SemaphoreType.DMA)
+    for _ in extras:
+        sems += pair(2 * depth - 1) + [pltpu.SemaphoreType.DMA]
+    count = len(arrays) + len(extras)
+    shapes = [((8 * depth,) + a.shape, a.dtype) for a in arrays]
+    shapes += [(a.shape, a.dtype) for a in extras]
+    return pl.pallas_call(
+        functools.partial(spread_kernel, depth, len(arrays), len(extras)),
+        out_shape=[jax.ShapeDtypeStruct(*shape) for shape in shapes],
+        in_specs=in_hbm(count),
+        out_specs=in_hbm(count),
+        scratch_shapes=sems,
+        compiler_params=pltpu.CompilerParams(
+            collective_id=ident, has_side_effects=True, vmem_limit_bytes=16 << 20
+        ),
+        cost_estimate=pl.CostEstimate(
+            flops=0,
+            bytes_accessed=sum(64 * depth * a.size * a.dtype.itemsize for a in arrays),
+            transcendentals=0,
+        ),
+    )(*arrays, *extras)
+
+
+def sum_rows(target, lead, terms):
+    rows = target.shape[-2]
+    tile = min(rows, 16)
+
+    def body(i, carry):
+        at = pl.ds(pl.multiple_of(i * tile, tile), tile)
+        total = terms[0][0][(*terms[0][1], at, slice(None))].astype(high_type)
+        for ref, where in terms[1:]:
+            total = total + ref[(*where, at, slice(None))].astype(high_type)
+        target[(*lead, at, slice(None))] = total.astype(target.dtype)
+        return carry
+
+    lax.fori_loop(0, rows // tile, body, 0)
+
+
+def collect_kernel(depth, count, shared, *refs):
+    whole = count + shared
+    parts, totals = refs[:count], refs[whole : whole + count]
+    scratch, sems = refs[2 * whole : 2 * whole + 5 * count], refs[2 * whole + 5 * count :]
+    at = Place(depth)
+    ranks = [(k, core) for k in range(depth) for core in range(2) if k or core]
+    peers = [at.chip(k, lax.rem(at.c + core, 2)) for k, core in ranks]
+    meet([at.near(), at.far()] + peers)
+    started = []
+    groups = (3, 2, 1, 0)
+    per = 9
+
+    def block(slot, core):
+        column = (at.own_column, at.near_of(core), at.far_of(core), at.other_column)[
+            groups[slot // depth]
+        ]
+        return at.block(column, at.along(1 + slot % depth), core)
+
+    def push(copy):
+        copy.start()
+        started.append(copy)
+
+    def arrive(buffer, pair_of, slot):
+        remote(buffer.at[slot], buffer.at[slot], pair_of, slot, at.core()).wait_recv()
+
+    def load(n, slot):
+        return pltpu.make_async_copy(
+            parts[n].at[block(slot, at.c)], scratch[5 * n].at[slot], sems[per * n + 8].at[slot]
         )
 
-    def sum_seq(self, values):
-        values = values + self.core(values)
-        total = values
-        for step in range(1, self.depth):
-            total = total + self.from_z(values, step)
-        return total
-
-    def spread(self, rows):
-        own = jnp.concatenate(
-            [rows] + [self.from_z(rows, step) for step in range(1, self.depth)], axis=0
+    def number(column):
+        return column[0] * 2 + column[1]
+
+    if shared:
+        part, arrived = refs[count], refs[whole + count]
+        mine, far_in, near_in, local = refs[-10:-6]
+        far_sems, near_sems, out_sems = refs[-6:-4], refs[-4:-2], refs[-2:]
+        columns = [at.other_column, at.far_of(at.c), at.near_of(at.c), at.own_column]
+        for i in range(2):
+            push(remote(part.at[number(columns[i])], far_in.at[i], far_sems, i, at.far()))
+            pltpu.make_async_copy(
+                part.at[number(columns[2 + i])], mine.at[i], local.at[i]
+            ).start()
+    for slot in range(4 * depth):
+        for n in range(count):
+            push(
+                remote(
+                    parts[n].at[block(slot, 1 - at.c)],
+                    scratch[5 * n + 1].at[slot],
+                    sems[per * n :],
+                    slot,
+                    at.core(),
+                )
+            )
+            load(n, slot).start()
+
+    def add(n, slot, more):
+        mine, crossed = scratch[5 * n : 5 * n + 2]
+        load(n, slot).wait()
+        arrive(crossed, sems[per * n :], slot)
+        terms = [(mine, (slot,)), (crossed, (slot,))] + more
+        if slot < 4 * depth - 1:
+            sum_rows(mine, (slot,), terms)
+        else:
+            sum_rows(totals[n], (), terms)
+        return mine.at[slot]
+
+    for n in range(count):
+        for slot in range(2 * depth):
+            total = add(n, slot, [])
+            far_in = scratch[5 * n + 2]
+            push(remote(total, far_in.at[slot], sems[per * n + 2 :], slot, at.far()))
+    if shared:
+        mine, far_in, near_in, local = refs[-10:-6]
+        pltpu.make_async_copy(part.at[number(columns[2])], mine.at[0], local.at[0]).wait()
+        arrive(far_in, far_sems, 0)
+        sum_rows(mine, (0,), [(mine, (0,)), (far_in, (0,))])
+        push(remote(mine.at[0], near_in.at[0], near_sems, 0, at.near()))
+    for n in range(count):
+        far_in, near_in = scratch[5 * n + 2 : 5 * n + 4]
+        for k in range(depth):
+            arrive(far_in, sems[per * n + 2 :], k)
+            total = add(n, 2 * depth + k, [(far_in, (k,))])
+            push(remote(total, near_in.at[k], sems[per * n + 4 :], k, at.near()))
+    if shared:
+        mine, far_in, near_in, local = refs[-10:-6]
+        pltpu.make_async_copy(part.at[number(columns[3])], mine.at[1], local.at[1]).wait()
+        arrive(far_in, far_sems, 1)
+        arrive(near_in, near_sems, 0)
+        sum_rows(mine, (1,), [(mine, (1,)), (far_in, (1,)), (near_in, (0,))])
+        rows = arrived.shape[0] // (2 * depth)
+
+        def piece(ref, rank):
+            return ref.at[pl.ds(pl.multiple_of(rank * rows, rows), rows)]
+
+        own_rank = at.z * 2 + at.c
+        for slot, there in enumerate(peers):
+            source = piece(mine.at[1], there[2] * 2 + there[3])
+            push(remote(source, piece(arrived, own_rank), out_sems, slot, there))
+        kept = pltpu.make_async_copy(
+            piece(mine.at[1], own_rank), piece(arrived, own_rank), local.at[2]
         )
-        near = self.near(own)
-        far = self.far(jnp.concatenate([own, near], axis=0))
-        return [jnp.concatenate([v, self.core(v)], axis=0) for v in (own, near, far)]
-
-    def collect(self, chunks, rows):
-        def both(chunk):
-            half = chunk.shape[0] // 2
-            arrived = self.core(chunk[half:])
-            return chunk[:half].astype(high_type) + arrived.astype(high_type)
-
-        far = self.far(both(chunks[2]).astype(low_type)).astype(high_type)
-        half = far.shape[0] // 2
-        near = self.near((both(chunks[1]) + far[half:]).astype(low_type))
-        own = (both(chunks[0]) + far[:half] + near.astype(high_type)).astype(low_type)
-        total = own[:rows].astype(high_type)
-        for step in range(1, self.depth):
-            total = total + self.to_z(own[step * rows : (step + 1) * rows], step).astype(high_type)
-        return total
-
-    def block_order(self):
-        y, x, z, c = (lax.axis_index(name) for name in GRID)
-
-        def at(y, x, step, c):
-            return ((y * 2 + x) * self.depth + (z + step) % self.depth) * 2 + c
-
-        order = []
-        for dy, dx in ((0, 0),):
-            for core in (c, 1 - c):
-                order += [at(y, x, k, core) for k in range(self.depth)]
-        for core in (c, 1 - c):
-            order += [at(y ^ core, x ^ (1 - core), k, core) for k in range(self.depth)]
-        for core in (c, 1 - c):
-            order += [at(y ^ (1 - core), x ^ core, k, core) for k in range(self.depth)]
-            order += [at(1 - y, 1 - x, k, core) for k in range(self.depth)]
-        return jnp.stack(order)
+        kept.start()
+    for n in range(count):
+        far_in, near_in, z_in = scratch[5 * n + 2 : 5 * n + 5]
+        for k in range(depth):
+            arrive(far_in, sems[per * n + 2 :], depth + k)
+            arrive(near_in, sems[per * n + 4 :], k)
+            total = add(n, 3 * depth + k, [(far_in, (depth + k,)), (near_in, (k,))])
+            if k < depth - 1:
+                push(remote(total, z_in.at[k], sems[per * n + 6 :], k, at.chip(1 + k)))
+    for n in range(count):
+        z_in = scratch[5 * n + 4]
+        for k in range(depth - 1):
+            arrive(z_in, sems[per * n + 6 :], k)
+        sum_rows(totals[n], (), [(totals[n], ())] + [(z_in, (k,)) for k in range(depth - 1)])
+    if shared:
+        for slot, (k, core) in enumerate(ranks):
+            target = piece(arrived, at.along(depth - k) * 2 + lax.rem(at.c + core, 2))
+            remote(target, target, out_sems, slot, at.core()).wait_recv()
+        kept.wait()
+    for copy in started:
+        copy.wait_send()
+
+
+def collect(depth, ident, *arrays, shared=None):
+    count = len(arrays)
+    buffers, sems, shapes = [], [], []
+    for a in arrays:
+        for slots in (4 * depth, 4 * depth, 2 * depth, depth, depth - 1):
+            buffers.append(pltpu.VMEM((slots,) + a.shape[1:], a.dtype))
+        sems += pair(4 * depth) + pair(2 * depth) + pair(depth) + pair(depth - 1)
+        sems.append(pltpu.SemaphoreType.DMA((4 * depth,)))
+        shapes.append(jax.ShapeDtypeStruct(a.shape[1:], high_type))
+    specs = [pl.BlockSpec(memory_space=pltpu.VMEM)] * count
+    if shared is not None:
+        block = shared.shape[1:]
+        arrays += (shared,)
+        specs += in_hbm(1)
+        shapes.append(jax.ShapeDtypeStruct(block, shared.dtype))
+        sems += [pltpu.VMEM((slots,) + block, shared.dtype) for slots in (2, 2, 1)]
+        sems.append(pltpu.SemaphoreType.DMA((3,)))
+        sems += pair(2) + pair(1) + pair(2 * depth - 1)
+    return pl.pallas_call(
+        functools.partial(collect_kernel, depth, count, shared is not None),
+        out_shape=shapes,
+        in_specs=in_hbm(len(arrays)),
+        out_specs=specs,
+        scratch_shapes=buffers + sems,
+        compiler_params=pltpu.CompilerParams(
+            collective_id=ident, has_side_effects=True, vmem_limit_bytes=56 << 20
+        ),
+        cost_estimate=pl.CostEstimate(
+            flops=0,
+            bytes_accessed=sum(16 * a.size * a.dtype.itemsize for a in arrays),
+            transcendentals=0,
+        ),
+    )(*arrays)
+
+
+def gather_kernel(depth, x_ref, w_ref, s_ref, x_out, w_out, s_out, *sems):
+    at = Place(depth)
+    ranks = [(k, core) for k in range(depth) for core in range(2) if k or core]
+
+    def peer(k, core):
+        return at.chip(k, lax.rem(at.c + core, 2))
+
+    meet([peer(k, core) for k, core in ranks] + [at.near(), at.far()])
+    started, local = [], []
+
+    def push(copy):
+        copy.start()
+        started.append(copy)
+
+    def rank(z, c):
+        return z * 2 + c
+
+    own, column = rank(at.z, at.c), at.y * 2 + at.x
+    x_z, x_core, w_sems, s_sems, w_side, s_side = (sems[2 * i : 2 * i + 2] for i in range(6))
+    for slot, (k, core) in enumerate(ranks):
+        there = peer(k, core)
+        push(remote(s_ref, s_out.at[column, own], s_sems, slot, there))
+        push(
+            remote(
+                w_ref.at[rank(there[2], there[3])], w_out.at[column, own], w_sems, slot, there
+            )
+        )
+    for k in range(1, depth):
+        push(remote(x_ref, x_out.at[own], x_z, k - 1, at.chip(k)))
+    push(remote(x_ref, x_out.at[own], x_core, 0, at.core()))
+    for i, (source, target) in enumerate(
+        ((x_ref, x_out.at[own]), (w_ref.at[own], w_out.at[column, own]), (s_ref, s_out.at[column, own]))
+    ):
+        copy = pltpu.make_async_copy(source, target, sems[12].at[i])
+        copy.start()
+        local.append(copy)
+
+    def arrive(target, pair_of, slot):
+        remote(target, target, pair_of, slot, at.core()).wait_recv()
+
+    for slot, (k, core) in enumerate(ranks):
+        source = rank(at.along(depth - k), lax.rem(at.c + core, 2))
+        arrive(s_out.at[column, source], s_sems, slot)
+        arrive(w_out.at[column, source], w_sems, slot)
+    for copy in local:
+        copy.wait()
+    near_y, near_x = at.near_of(at.c)
+    far_y, far_x = at.far_of(at.c)
+    beside, across = near_y * 2 + near_x, far_y * 2 + far_x
+    for target, pair_of in ((s_out, s_side), (w_out, w_side)):
+        push(remote(target.at[column], target.at[column], pair_of, 0, at.near()))
+        push(remote(target.at[column], target.at[column], pair_of, 1, at.far()))
+    for k in range(1, depth):
+        source = rank(at.along(depth - k), at.c)
+        arrive(x_out.at[source], x_z, k - 1)
+        push(remote(x_out.at[source], x_out.at[source], x_core, k, at.core()))
+    for target, pair_of in ((s_out, s_side), (w_out, w_side)):
+        arrive(target.at[beside], pair_of, 0)
+        push(remote(target.at[beside], target.at[beside], pair_of, 2, at.far()))
+    for k in range(depth):
+        arrive(x_out.at[rank(at.along(depth - k), 1 - at.c)], x_core, k)
+    for target, pair_of in ((s_out, s_side), (w_out, w_side)):
+        arrive(target.at[across], pair_of, 1)
+        arrive(target.at[3 - column], pair_of, 2)
+    for copy in started:
+        copy.wait_send()
+
+
+def gather(depth, ident, x, w, s):
+    ranks = 2 * depth
+    sems = pair(depth - 1) + pair(depth) + pair(ranks - 1) * 2 + pair(3) * 2
+    sems.append(pltpu.SemaphoreType.DMA((3,)))
+    return pl.pallas_call(
+        functools.partial(gather_kernel, depth),
+        out_shape=[
+            jax.ShapeDtypeStruct((ranks,) + x.shape, x.dtype),
+            jax.ShapeDtypeStruct((4,) + w.shape, w.dtype),
+            jax.ShapeDtypeStruct((4, ranks) + s.shape, s.dtype),
+        ],
+        in_specs=in_hbm(3),
+        out_specs=in_hbm(3),
+        scratch_shapes=sems,
+        compiler_params=pltpu.CompilerParams(
+            collective_id=ident, has_side_effects=True, vmem_limit_bytes=16 << 20
+        ),
+        cost_estimate=pl.CostEstimate(
+            flops=0, bytes_accessed=64 * depth * x.size, transcendentals=0
+        ),
+    )(x, w, s)
+
+
+def exchange_kernel(depth, same, x_ref, out_ref, send_sems, recv_sems, local_sem):
+    at = Place(depth)
+    ranks = [(k, core) for k in range(depth) for core in range(2) if k or core]
+    peers = [at.chip(k, lax.rem(at.c + core, 2)) for k, core in ranks]
+    meet(peers)
+    own = at.z * 2 + at.c
+    copies = []
+    for slot, there in enumerate(peers):
+        source = x_ref if same else x_ref.at[there[2] * 2 + there[3]]
+        copy = remote(source, out_ref.at[own], (send_sems, recv_sems), slot, there)
+        copy.start()
+        copies.append(copy)
+    local = pltpu.make_async_copy(x_ref if same else x_ref.at[own], out_ref.at[own], local_sem)
+    local.start()
+    for slot, (k, core) in enumerate(ranks):
+        target = out_ref.at[at.along(depth - k) * 2 + lax.rem(at.c + core, 2)]
+        remote(target, target, (send_sems, recv_sems), slot, at.core()).wait_recv()
+    for copy in copies:
+        copy.wait_send()
+    local.wait()
+
+
+def exchange(depth, ident, x, same=False):
+    ranks = 2 * depth
+    return pl.pallas_call(
+        functools.partial(exchange_kernel, depth, same),
+        out_shape=jax.ShapeDtypeStruct((ranks,) + x.shape if same else x.shape, x.dtype),
+        in_specs=in_hbm(1),
+        out_specs=in_hbm(1)[0],
+        scratch_shapes=pair(ranks - 1) + [pltpu.SemaphoreType.DMA],
+        compiler_params=pltpu.CompilerParams(
+            collective_id=ident, has_side_effects=True, vmem_limit_bytes=16 << 20
+        ),
+        cost_estimate=pl.CostEstimate(
+            flops=0, bytes_accessed=16 * x.size * x.dtype.itemsize, transcendentals=0
+        ),
+    )(x)
+
+
+def column_kernel(depth, part, total, mine, crossed, z_in, z_out, *sems):
+    at = Place(depth)
+    meet([at.core()] + [at.chip(k) for k in range(1, depth)])
+    started = []
+
+    def push(copy):
+        copy.start()
+        started.append(copy)
+
+    def local(k):
+        return pltpu.make_async_copy(
+            part.at[at.along(1 + k) * 2 + at.c], mine.at[k], sems[4].at[k]
+        )
+
+    def arrive(buffer, pair_of, slot):
+        remote(buffer.at[slot], buffer.at[slot], pair_of, slot, at.core()).wait_recv()
+
+    for k in range(depth):
+        push(
+            remote(
+                part.at[at.along(1 + k) * 2 + 1 - at.c], crossed.at[k], sems[0:2], k, at.core()
+            )
+        )
+        local(k).start()
+    for k in range(depth):
+        local(k).wait()
+        arrive(crossed, sems[0:2], k)
+        terms = [(mine, (k,)), (crossed, (k,))]
+        if k < depth - 1:
+            sum_rows(z_out, (k,), terms)
+            push(remote(z_out.at[k], z_in.at[k], sems[2:4], k, at.chip(1 + k)))
+        else:
+            sum_rows(total, (), terms)
+    for k in range(depth - 1):
+        arrive(z_in, sems[2:4], k)
+    sum_rows(total, (), [(total, ())] + [(z_in, (k,)) for k in range(depth - 1)])
+    for copy in started:
+        copy.wait_send()
+
+
+def collect_column(depth, ident, part):
+    block = part.shape[1:]
+    return pl.pallas_call(
+        functools.partial(column_kernel, depth),
+        out_shape=jax.ShapeDtypeStruct(block, high_type),
+        in_specs=in_hbm(1),
+        out_specs=pl.BlockSpec(memory_space=pltpu.VMEM),
+        scratch_shapes=[pltpu.VMEM((depth,) + block, part.dtype)] * 2
+        + [pltpu.VMEM((depth - 1,) + block, part.dtype)] * 2
+        + pair(depth)
+        + pair(depth - 1)
+        + [pltpu.SemaphoreType.DMA((depth,))],
+        compiler_params=pltpu.CompilerParams(
+            collective_id=ident, has_side_effects=True, vmem_limit_bytes=32 << 20
+        ),
+        cost_estimate=pl.CostEstimate(
+            flops=0, bytes_accessed=16 * part.size * part.dtype.itemsize, transcendentals=0
+        ),
+    )(part)
+
+
+def lines_in(values):
+    rows, local, two, hidden = values.shape
+    values = values.reshape(rows, local, two, hidden // 128, 128)
+    return values.transpose(0, 1, 3, 2, 4).reshape(-1, 128)
+
+
+def lines_down(values):
+    rows, local, hidden = values.shape
+    return values.reshape(rows, local, hidden // 128, 128).transpose(0, 2, 1, 3).reshape(-1, 128)
+
+
+def places(ranks, local):
+    for rank in range(ranks):
+        for x in range(local):
+            for k in range(2):
+                yield rank, (k * local + x) * 128, (x * ranks + rank) * 2 + k, None
+            yield rank, x * 128, None, rank * local + x
+
+
+def pack_kernel(ranks, local, step, in_ref, down_ref, in_out, down_out):
+    for rank, column, of_in, of_down in places(ranks, local):
+        if of_down is None:
+            value = in_ref[pl.ds(of_in, step, stride=2 * local * ranks), :]
+            in_out[rank, :, column : column + 128] = value.astype(low_type)
+        else:
+            value = down_ref[pl.ds(of_down, step, stride=local * ranks), :]
+            down_out[rank, :, column : column + 128] = value.astype(low_type)
+
+
+def pack(ranks, expert_in, expert_down):
+    rows, local = expert_in.shape[:2]
+    step = 32
+    lines = step * local * ranks
+    span = local * 128
+    return pl.pallas_call(
+        functools.partial(pack_kernel, ranks, local, step),
+        grid=(rows // step,),
+        in_specs=[
+            pl.BlockSpec((2 * lines, 128), lambda i: (i, 0)),
+            pl.BlockSpec((lines, 128), lambda i: (i, 0)),
+        ],
+        out_specs=[
+            pl.BlockSpec((ranks, step, 2 * span), lambda i: (0, i, 0)),
+            pl.BlockSpec((ranks, step, span), lambda i: (0, i, 0)),
+        ],
+        out_shape=[
+            jax.ShapeDtypeStruct((ranks, rows, 2 * span), low_type),
+            jax.ShapeDtypeStruct((ranks, rows, span), low_type),
+        ],
+        compiler_params=pltpu.CompilerParams(vmem_limit_bytes=32 << 20),
+    )(lines_in(expert_in), lines_down(expert_down))
+
+
+def unpack_kernel(ranks, local, step, in_ref, out_ref):
+    for rank, column, of_in, of_down in places(ranks, local):
+        down = in_ref.shape[2] == local * 128
+        if down == (of_in is None):
+            first = of_down if down else of_in
+            stride = (1 if down else 2) * local * ranks
+            value = in_ref[rank, :, column : column + 128].astype(high_type)
+            out_ref[pl.ds(first, step, stride=stride), :] = value
+
+
+def unpack(local, sliced):
+    ranks, rows, span = sliced.shape
+    step = 32
+    lines = step * ranks * span // 128
+    return pl.pallas_call(
+        functools.partial(unpack_kernel, ranks, local, step),
+        grid=(rows // step,),
+        in_specs=[pl.BlockSpec((ranks, step, span), lambda i: (0, i, 0))],
+        out_specs=pl.BlockSpec((lines, 128), lambda i: (i, 0)),
+        out_shape=jax.ShapeDtypeStruct((rows * ranks * span // 128, 128), high_type),
+        compiler_params=pltpu.CompilerParams(vmem_limit_bytes=32 << 20),
+    )(sliced)
 
 
 def grid_shards(
@@ -165,7 +703,6 @@
 ):
     rows, width = residual_in.shape
     depth = lax.axis_size("dz")
-    move = Moves(depth)
     ranks = 2 * depth
     columns = 4
     seq_rows = rows * ranks
@@ -182,6 +719,10 @@
     own_heads = HEADS // ranks
     own_width = own_heads * HD
 
+    def sum_column(ident, pairs):
+        flat = exchange(depth, ident, pairs.reshape(-1, 128), same=True)
+        return jnp.sum(flat, axis=0).reshape(pairs.shape)
+
     def by_rank(values):
         lead = values.shape[:-1]
         shaped = values.reshape(lead + (2, own_heads, depth, HD))
@@ -199,48 +740,23 @@
         )
 
     small = jnp.concatenate([gains.T, router], axis=1).astype(low_type)
-    small = lax.all_gather(small, GRID, axis=0, tiled=True)
+    small = jnp.pad(small, ((0, 0), (0, 128 - small.shape[1])))
+    packed = attn_qkv.astype(low_type).transpose(1, 0, 2)
+    packed = by_rank(packed).reshape(ranks, weight_rows, 3 * own_width)
+    seq_input, qkv_weight, small = gather(depth, 0, residual_in, packed, small)
+    qkv_weight = qkv_weight.reshape(width, 3 * own_width)
+    small = small.reshape(width, 128)
     gain_rows = small[:, :4].T.astype(high_type)
-    router_weight = small[:, 4:]
+    router_weight = small[:, 4 : 4 + experts]
     gain_own = [
         lax.dynamic_index_in_dim(by_rank(gain_rows[i]), z * 2 + c, 0, keepdims=False)
         for i in (1, 2)
     ]
-
-    held = [residual_in] + [move.from_z(residual_in, k) for k in range(1, depth)]
-    crossed = [move.core(block) for block in held]
-    normed_in = jnp.zeros((depth, 2, rows, width), low_type)
-    for k in range(depth):
-        for block, core in ((held[k], c), (crossed[k], 1 - c)):
-            block = block.astype(high_type)
-            block = (block * rms_scale(block) * gain_rows[0]).astype(low_type)
-            normed_in = lax.dynamic_update_slice(
-                normed_in, block[None, None], ((z + k) % depth, core, 0, 0)
-            )
-    normed_in = normed_in.reshape(seq_rows, width)
-
-    packed = attn_qkv.astype(low_type).transpose(1, 0, 2)
-    packed = by_rank(packed).reshape(ranks, weight_rows, 3 * own_width)
-    packed = lax.all_to_all(packed, SEQ, 0, 0, tiled=True).reshape(-1, 3 * own_width)
-    near = move.near(packed)
-    far = move.far(jnp.stack([packed, near]))
-    in_x = jnp.where(c == 0, near, far[0])
-    in_y = jnp.where(c == 0, far[0], near)
-    in_row = [jnp.where(x == 0, packed, in_x), jnp.where(x == 0, in_x, packed)]
-    out_row = [jnp.where(x == 0, in_y, far[1]), jnp.where(x == 0, far[1], in_y)]
-    qkv_weight = jnp.concatenate(
-        [jnp.where(y == 0, a, b) for a, b in zip(in_row, out_row)]
-        + [jnp.where(y == 0, b, a) for a, b in zip(in_row, out_row)],
-        axis=0,
-    )
+    normed_in = seq_input.reshape(seq_rows, width).astype(high_type)
+    normed_in = (normed_in * rms_scale(normed_in) * gain_rows[0]).astype(low_type)
     out_weight = lax.all_gather(attn_out.astype(low_type), GRID, axis=0, tiled=True)
 
-    sliced_in = expert_in.astype(low_type).reshape(chunk_rows, local_experts, 2, ranks, part)
-    sliced_in = sliced_in.transpose(3, 0, 2, 1, 4).reshape(ranks, chunk_rows, 2 * span)
-    weights_in = lax.all_to_all(sliced_in, SEQ, 0, 0, tiled=True).reshape(width, 2 * span)
-    sliced_down = expert_down.astype(low_type).reshape(chunk_rows, local_experts, ranks, part)
-    sliced_down = sliced_down.transpose(2, 0, 1, 3).reshape(ranks, chunk_rows, span)
-    weights_down = lax.all_to_all(sliced_down, SEQ, 0, 0, tiled=True).reshape(width, span)
+    sliced_in, sliced_down = pack(ranks, expert_in, expert_down)
 
     raw = dot(normed_in, qkv_weight)
     query_raw, key_raw = raw[:, :own_width], raw[:, own_width : 2 * own_width]
@@ -248,7 +764,7 @@
     squares = jnp.stack(
         [jnp.sum(query_raw * query_raw, axis=1), jnp.sum(key_raw * key_raw, axis=1)]
     )
-    scales = lax.rsqrt(move.sum_seq(squares) / width + epsilon)
+    scales = lax.rsqrt(sum_column(1, squares) / width + epsilon)
     query_scale, key_scale = scales[0][:, None], scales[1][:, None]
     positions = jnp.arange(seq_rows, dtype=jnp.int32)
     length_now = lengths[0]
@@ -270,7 +786,7 @@
     probs = jax.nn.softmax(scores, axis=-1)
     probs_low = probs.astype(low_type)
     attended = per_head("hqk,khd->qhd", probs_low, value_heads).astype(low_type)
-    attended = lax.all_to_all(attended.reshape(ranks, rows, own_width), SEQ, 0, 0, tiled=True)
+    attended = exchange(depth, 2, attended.reshape(ranks, rows, own_width))
     attended = by_head(attended)
 
     own_positions = (z * 2 + c) * rows + jnp.arange(rows, dtype=jnp.int32)
@@ -291,71 +807,44 @@
 
     grad_rows = cotangent.astype(high_type)
     grad_comb = live_rows * grad_rows
-    order = move.block_order()
-    gates_all = lax.all_gather(gates.T[None], GRID, axis=0, tiled=True)
+    own_grads, normed_mid = lax.optimization_barrier((grad_comb.astype(low_type), normed_mid))
+    grads = lax.all_gather(own_grads, GRID, axis=0, tiled=True)
+    tokens, gates_all, weights_in, weights_down = spread(
+        depth, 3, (normed_mid, gates.T), (sliced_in, sliced_down)
+    )
+    weights_in, weights_down = weights_in.reshape(width, -1), weights_down.reshape(width, -1)
+    tokens = tokens.reshape(-1, width)
     gates_all = lax.dynamic_slice_in_dim(gates_all, column * local_experts, local_experts, 1)
-    chosen_block = (order[:, None] == jnp.arange(4 * ranks, dtype=jnp.int32)[None, :]).astype(
-        high_type
-    )
-
-    def permuted(spec, blocks):
-        return jnp.einsum(
-            spec,
-            chosen_block,
-            blocks,
-            precision=lax.Precision.HIGHEST,
-            preferred_element_type=high_type,
-        )
-
-    gates_all = permuted("ij,jer->ier", gates_all).transpose(0, 2, 1).reshape(-1, local_experts)
-    grad_chunks = move.spread(grad_comb.astype(low_type))
-    token_chunks = move.spread(normed_mid)
-    back_chunks, mixed_chunks, gate_sums = [], [], []
-    grad_in = jnp.zeros((width, 2 * span), high_type)
-    grad_down = jnp.zeros((width, span), high_type)
-    start = 0
-    for tokens, grads in zip(token_chunks, grad_chunks):
-        count = tokens.shape[0]
-        gate = gates_all[start : start + count]
-        start += count
-        wide = jnp.repeat(gate, part, axis=1)
-        both_parts = dot(tokens, weights_in)
-        gate_part, up_part = both_parts[:, :span], both_parts[:, span:]
-        down_grad = dot(grads, weights_down)
-        sigma = jax.nn.sigmoid(gate_part)
-        hidden = (gate_part * sigma * up_part).astype(low_type).astype(high_type)
-        gate_sums.append(
-            jnp.sum((hidden * down_grad).reshape(count, local_experts, part), axis=2)
-        )
-        weighted = (wide * hidden).astype(low_type)
-        grad_hidden = wide * down_grad
-        grad_gate = grad_hidden * up_part * sigma * (1.0 + gate_part * (1.0 - sigma))
-        grad_up = grad_hidden * gate_part * sigma
-        grad_both = jnp.concatenate([grad_gate, grad_up], axis=1).astype(low_type)
-        back_chunks.append(dot_t(grad_both, weights_in).astype(low_type))
-        mixed_chunks.append(dot_t(weighted, weights_down).astype(low_type))
-        grad_in = grad_in + t_dot(tokens, grad_both)
-        grad_down = grad_down + t_dot(grads, weighted)
-    grad_mid_norm = move.collect(back_chunks, rows)
-    combined = move.collect(mixed_chunks, rows)
-    output = middle + live_rows * combined
-
-    sliced = grad_in.astype(low_type).reshape(ranks, chunk_rows, 2 * span)
-    sliced = lax.all_to_all(sliced, SEQ, 0, 0, tiled=True)
-    sliced = sliced.reshape(ranks, chunk_rows, 2, local_experts, part).transpose(1, 3, 2, 0, 4)
-    grad_expert_in = sliced.reshape(expert_in.shape).astype(high_type)
-    sliced = grad_down.astype(low_type).reshape(ranks, chunk_rows, span)
-    sliced = lax.all_to_all(sliced, SEQ, 0, 0, tiled=True)
-    sliced = sliced.reshape(ranks, chunk_rows, local_experts, part).transpose(1, 2, 0, 3)
-    grad_expert_down = sliced.reshape(expert_down.shape).astype(high_type)
-
-    sums = jnp.concatenate(gate_sums, axis=0).reshape(-1, rows, local_experts).transpose(0, 2, 1)
-    placed = jnp.zeros((4 * ranks, columns, local_experts, rows), high_type)
-    sums = permuted("ij,ier->jer", sums)
-    placed = lax.dynamic_update_slice(placed, sums[:, None], (0, column, 0, 0))
-    grad_gates = lax.psum_scatter(
-        placed.reshape(4 * ranks, experts, rows), GRID, scatter_dimension=0, tiled=True
-    )[0].T
+    gates_all = gates_all.transpose(0, 2, 1).reshape(-1, local_experts)
+    wide = jnp.repeat(gates_all, part, axis=1)
+    both_parts = dot(tokens, weights_in)
+    gate_part, up_part = both_parts[:, :span], both_parts[:, span:]
+    down_grad = dot(grads, weights_down)
+    sigma = jax.nn.sigmoid(gate_part)
+    hidden = (gate_part * sigma * up_part).astype(low_type).astype(high_type)
+    gate_sums = jnp.sum((hidden * down_grad).reshape(-1, rows, local_experts, part), axis=3)
+    weighted = (wide * hidden).astype(low_type)
+    grad_hidden = wide * down_grad
+    grad_gate = grad_hidden * up_part * sigma * (1.0 + gate_part * (1.0 - sigma))
+    grad_up = grad_hidden * gate_part * sigma
+    grad_both = jnp.concatenate([grad_gate, grad_up], axis=1).astype(low_type)
+    grad_in = t_dot(tokens, grad_both).astype(low_type)
+    grad_both, grad_in = lax.optimization_barrier((grad_both, grad_in))
+    back = dot_t(grad_both, weights_in).astype(low_type)
+    placed = jnp.zeros((4 * ranks, experts, rows), high_type)
+    placed = lax.dynamic_update_slice(
+        placed, gate_sums.transpose(0, 2, 1), (0, column * local_experts, 0)
+    )
+    mixed = dot_t(weighted, weights_down).astype(low_type)
+    back, mixed = lax.optimization_barrier((back, mixed))
+    grad_mid_norm, grad_gates = collect(depth, 4, back.reshape(-1, rows, width), placed)
+    sliced = lax.all_to_all(grad_in.reshape(ranks, chunk_rows, 2 * span), SEQ, 0, 0, tiled=True)
+    grad_expert_in = unpack(local_experts, sliced).reshape(
+        chunk_rows, local_experts, ranks, 2, part
+    )
+    grad_expert_in = grad_expert_in.transpose(0, 1, 3, 2, 4).reshape(expert_in.shape)
+
+    grad_gates = grad_gates.T
     grad_chosen = gates * (grad_gates - jnp.sum(gates * grad_gates, axis=1, keepdims=True))
     grad_logits = grad_chosen.astype(low_type)
     grad_mid_norm = grad_mid_norm + dot_t(grad_logits, router_weight)
@@ -364,12 +853,9 @@
     grad_mid_rows, grad_gain_mid = rms_back(grad_mid_norm, normed_mid_f, scale_mid, gain_rows[3])
     grad_middle = grad_rows + grad_mid_rows
     grad_branch = (live_rows * grad_middle).astype(low_type)
-    grad_out = lax.psum_scatter(
-        t_dot(attended, grad_branch).astype(low_type), GRID, scatter_dimension=0, tiled=True
-    ).astype(high_type)
 
     grad_attended = by_rank(dot_t(grad_branch, out_weight).astype(low_type))
-    grad_attended = lax.all_to_all(grad_attended, SEQ, 0, 0, tiled=True)
+    grad_attended = exchange(depth, 6, grad_attended)
     grad_heads = grad_attended.reshape(seq_rows, own_heads, HD)
     grad_probs = per_head("qhd,khd->hqk", grad_heads, value_heads)
     inner_rows = jnp.sum(probs * grad_probs, axis=-1, keepdims=True)
@@ -387,7 +873,7 @@
             jnp.sum(key_inner * key_normed, axis=1),
         ]
     )
-    inner = move.sum_seq(inner) / width
+    inner = sum_column(7, inner) / width
     query_back = query_scale * (query_inner - query_normed * inner[0][:, None])
     key_back = key_scale * (key_inner - key_normed * inner[1][:, None])
     grad_raw = jnp.concatenate(
@@ -399,35 +885,15 @@
         axis=1,
     )
 
-    by_core = grad_raw.reshape(depth, 2, rows, 3 * own_width)
-    other = lax.dynamic_index_in_dim(by_core, 1 - c, 1, keepdims=False)
-    mine = lax.dynamic_index_in_dim(by_core, c, 1, keepdims=False)
-    other = dot_t(other.reshape(depth * rows, -1), qkv_weight).astype(low_type)
-    mine = dot_t(mine.reshape(depth * rows, -1), qkv_weight)
-    share = (mine + move.core(other).astype(high_type)).astype(low_type)
-    share = share.reshape(depth, rows, width)
-    grad_norm_in = lax.dynamic_index_in_dim(share, z, 0, keepdims=False).astype(high_type)
-    for step in range(1, depth):
-        piece = lax.dynamic_index_in_dim(share, (z + step) % depth, 0, keepdims=False)
-        grad_norm_in = grad_norm_in + move.to_z(piece, step).astype(high_type)
-
-    grad_qkv = t_dot(normed_in, grad_raw).astype(low_type).reshape(columns, -1, 3 * own_width)
-
-    def for_column(index):
-        return lax.dynamic_index_in_dim(grad_qkv, index, 0, keepdims=False)
-
-    far_x, far_y = x ^ c, y ^ (1 - c)
-    near_x, near_y = x ^ (1 - c), y ^ c
-    arrived = move.far(
-        jnp.stack([for_column(far_y * 2 + far_x), for_column(3 - column)])
-    ).astype(high_type)
-    near = (for_column(near_y * 2 + near_x).astype(high_type) + arrived[1]).astype(low_type)
-    total = for_column(column).astype(high_type) + arrived[0] + move.near(near).astype(high_type)
-    total = total.astype(low_type).reshape(ranks, weight_rows, 3 * own_width)
-    total = lax.all_to_all(total, SEQ, 0, 0, tiled=True)
-    grad_qkv = by_head(total.reshape(ranks, weight_rows, 3, own_width))
-    grad_qkv = grad_qkv.transpose(1, 0, 2).astype(high_type)
-
+    share = dot_t(grad_raw, qkv_weight).astype(low_type).reshape(ranks, rows, width)
+    grad_norm_in = collect_column(depth, 8, share)
+    grad_norm_in, grads, attended = lax.optimization_barrier((grad_norm_in, grads, attended))
+    grad_down = t_dot(grads, weighted).astype(low_type)
+    sliced = lax.all_to_all(grad_down.reshape(ranks, chunk_rows, span), SEQ, 0, 0, tiled=True)
+    grad_expert_down = unpack(local_experts, sliced).reshape(
+        chunk_rows, ranks, local_experts, part
+    )
+    grad_expert_down = grad_expert_down.transpose(0, 2, 1, 3).reshape(expert_down.shape)
     scale_in = rms_scale(input_rows)
     grad_in_rows, grad_gain_in = rms_back(
         grad_norm_in, input_rows * scale_in, scale_in, gain_rows[0]
@@ -453,14 +919,27 @@
         ],
         axis=1,
     )
-    grad_small = lax.psum_scatter(grad_small, GRID, scatter_dimension=0, tiled=True)
+    grad_small = jnp.pad(grad_small, ((0, 0), (0, 128 - grad_small.shape[1])))
+    grad_out = t_dot(attended, grad_branch).astype(low_type)
+    grad_qkv = t_dot(normed_in, grad_raw).astype(low_type)
+    combined, grad_out, grad_small, grad_qkv = collect(
+        depth,
+        5,
+        mixed.reshape(-1, rows, width),
+        grad_out.reshape(-1, weight_rows, width),
+        grad_small.reshape(-1, weight_rows, 128),
+        shared=grad_qkv.reshape(columns, -1, 3 * own_width),
+    )
+    output = middle + live_rows * combined
+    grad_qkv = by_head(grad_qkv.reshape(ranks, weight_rows, 3, own_width))
+    grad_qkv = grad_qkv.transpose(1, 0, 2).astype(high_type)
     return (
         output,
         grad_input,
         grad_qkv,
         grad_out,
         grad_small[:, :4].T,
-        grad_small[:, 4:],
+        grad_small[:, 4 : 4 + experts],
         grad_expert_in,
         grad_expert_down,
     )

time: 1390 us -> 1220 us (0.88)
  Pallas kernels: 0 us -> 824 us
  waiting for transfers between devices: 597 us -> 0.04 us
  local copies, waits for them, and re-layouts: 197 us -> 63.8 us
  starting transfers between devices: 116 us -> 4.94 us
  blocking collectives: 170 us -> 64 us
  matrix products: 195 us -> 166 us
  other arithmetic: 95.4 us -> 69.2 us
    pallas_call x0 -> x12, Pallas kernels: none -> 824 us  [the longest x2 362 us: collect(): pl.pallas_call(functools.partial(collect_kernel, depth, count, shared is...]
    ppermute x55 -> x0, waiting for transfers between devices: 379 us -> none  [send(): return lax.ppermute(values, GRID, self.pairs(move))]
    all_gather x2 -> x0, blocking collectives: 143 us -> none  [the longest x1 106 us: grid_shards(): small = lax.all_gather(small, GRID, axis=0, tiled=True)]
    reduce_scatter x2 -> x0, waiting for transfers between devices: 120 us -> none  [the longest x1 71.6 us: grid_shards(): lax.psum_scatter(placed.reshape(4 * ranks, experts, rows), GRID, scatter_...]
    all_to_all x7 -> x1, waiting for transfers between devices: 97.6 us -> 0.01 us  [grid_shards(): lax.all_to_all(grad_in.reshape(ranks, chunk_rows, 2 * span), SEQ, 0, 0, t...]
    all_to_all x7 -> x1, starting transfers between devices: 60.5 us -> 4.86 us  [grid_shards(): lax.all_to_all(grad_in.reshape(ranks, chunk_rows, 2 * span), SEQ, 0, 0, t...]
    ppermute x55 -> x0, starting transfers between devices: 55.5 us -> none  [send(): return lax.ppermute(values, GRID, self.pairs(move))]
    convert_element_type x6 -> x0, local copies, waits for them, and re-layouts: 47.8 us -> none  [the longest x3 31.2 us: grid_shards(): grad_expert_in = sliced.reshape(expert_in.shape).astype(high_type)]
  transfers between devices with their start and end apart: 66 -> 3, of which waited for: 25 -> 0; matrix products, arithmetic and copies ran while one was open for 30% -> 8% of each run, Pallas kernels for 0% -> 51%
where the time goes in v2:
time: 1220 us; the launch traced here: 1210 us
  Pallas kernels  824 us (68%)
  matrix products  166 us (14%)
  other arithmetic  69.2 us (6%)
  blocking collectives  64 us (5%)
  local copies, waits for them, and re-layouts  63.8 us (5%)
  between operations  16.3 us (1%)
    pallas_call x2, Pallas kernels, collect(): pl.pallas_call(functools.partial(collect_kernel, depth, count, shared is...  362 us
    pallas_call x1, Pallas kernels, spread(): pl.pallas_call(functools.partial(spread_kernel, depth, len(arrays), len(e...  245 us
    pallas_call x1, Pallas kernels, gather(): pl.pallas_call(functools.partial(gather_kernel, depth), out_shape=[jax.Sh...  94.9 us
    all_to_all x1, blocking collectives, grid_shards(): lax.all_to_all(grad_down.reshape(ranks, chunk_rows, span), SEQ, 0, 0, til...  64 us
    pallas_call x4, Pallas kernels, exchange(): pl.pallas_call(functools.partial(exchange_kernel, depth, same), out_shape...  56.2 us
    dot_general x5, matrix products, dot_t(): lax.dot_general(left, right, (((1,), (1,)), ((), ())), preferred_element_...  51.7 us
    dot_general x5, matrix products, t_dot(): lax.dot_general(left, right, (((0,), (0,)), ((), ())), preferred_element_...  47.7 us
    unnamed x173, local copies, waits for them, and re-layouts  47.5 us
  transfers between devices with their start and end apart: 3, of which 0 were waited for; matrix products, arithmetic and copies ran while one was open for 8% of the time, Pallas kernels for 51%

profile of v2, /device:TPU:0, one launch (start us, length us, event | category | flops | bytes accessed | tf_op | source)
XLA Modules:
  0.0 1208.1 jit_solution(10298360059715866056)
XLA Ops:
  7.2 1.8 convert_element_type.195
  9.1 1.5 convert_bitcast_fusion
  13.7 94.9 %shard_map.161 = (bf16[8,128,2048]{2,1,0:T(8,128)(2,1)S(1)}, bf16[4,8,64,768]{3,2,1,0:T(8,128)(2,1)S(1)}, bf16[4,8,64,128]{3,2,1,0:T(8,128)(2,1)S(1)}) custom-call(bf16[128,2048]{1,0:T(8,128)(2,1)S(1)} %copy-done.1, bf16[8,64,768]{2,1,0:T(8,128)(2,1)S(1)} %reshape_reshape.10.w_ref, bf16[64,128]{1,0:T(8,128)(2,1)S(1)} %pad.8.s_ref), custom_call_target="tpu_custom_call" | custom-call | bytes 67108864 | tf_op jit(solution)/shard_map/pallas_call | solution.py:496
  108.6 2.0 copy-done
  110.6 1.6 copy-done.14
  112.8 3.2 multiply_reduce_fusion.1
  116.6 3.2 multiply_convert_fusion.4
  119.8 3.6 fusion.56
  125.2 23.3 %shard_map.162 = f32[8,16,128]{2,1,0:T(8,128)S(1)} custom-call(f32[16,128]{1,0:T(8,128)S(1)} %reshape.334.x_ref), custom_call_target="tpu_custom_call" | custom-call | bytes 131072 | tf_op jit(solution)/shard_map/pallas_call | solution.py:539
  149.3 2.2 fusion.39
  151.5 1.9 fusion.35
  153.9 6.5 fusion.55
  160.5 4.2 fusion.17
  165.2 13.2 %shard_map.163 = bf16[8,128,256]{2,1,0:T(8,128)(2,1)S(1)} custom-call(bf16[8,128,256]{2,1,0:T(8,128)(2,1)S(1)} %copy.130.x_ref), custom_call_target="tpu_custom_call" | custom-call | bytes 8388608 | tf_op jit(solution)/shard_map/pallas_call | solution.py:539
  180.0 4.8 multiply_reduce_fusion.6
  186.0 3.5 copy-done.4
  189.5 2.2 copy-done.9
  191.7 7.8 shard_map.164
  199.5 2.0 copy-done.10
  202.7 2.2 copy-done.11
  204.9 245.2 %shard_map.165 = (bf16[32,128,2048]{2,1,0:T(8,128)(2,1)S(1)}, f32[32,16,128]{2,1,0:T(8,128)S(1)}, bf16[8,256,1024]{2,1,0:T(8,128)(2,1)S(1)}, bf16[8,256,512]{2,1,0:T(8,128)(2,1)S(1)}) custom-call(bf16[128,2048]{1,0:T(8,128)(2,1)S(1)} %multiply_convert_fusion.8.refs_0_, f32[16,128]{1,0:T(8,128)S(1)} %fusion.46.refs_1_, bf16[8,256,1024]{2,1,0:T(8,128)(2,1)S(1)} %copy-done.11, ...), custom_call_target="tpu_custom_call" | custom-call | bytes 136314880 | tf_op jit(solution)/shard_map/pallas_call | solution.py:232
  450.2 5.7 copy-done.12
  457.3 2.0 copy-done.13
  459.3 23.1 %fusion.58 = f32[4096,1024]{0,1:T(8,128)} fusion(bf16[4096,2048]{1,0:T(8,128)(2,1)} %bitcast.226, bf16[2048,1024]{1,0:T(8,128)(2,1)S(1)} %bitcast.228), kind=kOutput, calls=%fused_computation.157 | convolution fusion | flops 17179869184 | bytes 37748736 | tf_op jit(solution)/shard_map/dot_general | solution.py:56
  482.4 14.5 %fusion.57 = f32[4096,512]{0,1:T(8,128)} fusion(bf16[4096,2048]{1,0:T(8,128)(2,1)} %all-gather.5.cloned.1.call-done, bf16[2048,512]{1,0:T(8,128)(2,1)S(1)} %bitcast.232), kind=kOutput, calls=%fused_computation.156 | convolution fusion | flops 8589934592 | bytes 27262976 | tf_op jit(solution)/shard_map/dot_general | solution.py:56
  496.9 14.6 %fusion.1 = (f32[64,8,32,128]{3,1,2,0:T(8,128)}, bf16[4096,512]{0,1:T(8,128)(2,1)}, bf16[4096,512]{0,1:T(8,128)(2,1)S(1)}, bf16[4096,512]{0,1:T(8,128)(2,1)}) fusion(f32[4096,512]{0,1:T(8,128)} %fusion.57, f32[4096,1024]{0,1:T(8,128)} %fusion.58, f32[4096,4]{0,1:T(4,128)S(1)} %dynamic-slice_bitcast_fusion), kind=kLoop, calls=%fused_computation.6 | loop fusion | flops 39845888 | bytes 46202880
  511.5 2.1 copy-done.26
  513.6 23.2 %convolution_convert_fusion.3 = bf16[2048,1024]{1,0:T(8,128)(2,1)} fusion(bf16[4096,2048]{1,0:T(8,128)(2,1)} %bitcast.227, bf16[4096,512]{0,1:T(8,128)(2,1)S(1)} %get-tuple-element.104, bf16[4096,512]{0,1:T(8,128)(2,1)} %get-tuple-element.105), kind=kOutput, calls=%fused_computation.28 | convolution fusion | flops 17198743552 | bytes 29360128 | tf_op jit(solution)/shard_map/dot_general | solution.py:64
  536.8 7.9 pad_maximum_fusion
  544.7 3.3 fusion.2
  548.0 2.0 copy-done.32
  550.0 12.5 %convolution_convert_fusion = bf16[4096,2048]{1,0:T(8,128)(2,1)} fusion(bf16[4096,512]{0,1:T(8,128)(2,1)S(1)} %fusion.2, bf16[2048,512]{1,0:T(8,128)(2,1)S(1)} %bitcast.233), kind=kOutput, calls=%fused_computation.1 | convolution fusion | flops 8598323200 | bytes 23068672 | tf_op jit(solution)/shard_map/dot_general | solution.py:60
  562.4 25.9 %convolution_convert_fusion.1 = bf16[4096,2048]{1,0:T(8,128)(2,1)} fusion(bf16[4096,1024]{0,1:T(8,128)(2,1)} %pad_maximum_fusion, bf16[2048,1024]{1,0:T(8,128)(2,1)} %bitcast.229), kind=kOutput, calls=%fused_computation.2 | convolution fusion | flops 17188257792 | bytes 29360128 | tf_op jit(solution)/shard_map/dot_general | solution.py:60
  588.3 8.5 copy.136
  596.8 4.0 reduce_sum.187
  601.7 135.7 %shard_map.166 = (f32[128,2048]{1,0:T(8,128)}, f32[16,128]{1,0:T(8,128)}) custom-call(bf16[32,128,2048]{2,1,0:T(8,128)(2,1)} %bitcast.237, f32[32,16,128]{2,1,0:T(8,128)} %copy-done.41), custom_call_target="tpu_custom_call" | custom-call | bytes 272629760 | tf_op jit(solution)/shard_map/pallas_call | solution.py:407
  739.0 1.8 multiply_reduce_fusion.2
  742.2 6.4 convolution_convert_fusion.7
  749.7 12.1 %shard_map.167 = bf16[8,128,256]{2,1,0:T(8,128)(2,1)S(1)} custom-call(bf16[8,128,256]{2,1,0:T(8,128)(2,1)S(1)} %reshape.355.x_ref), custom_call_target="tpu_custom_call" | custom-call | bytes 8388608 | tf_op jit(solution)/shard_map/pallas_call | solution.py:539
  762.4 4.8 multiply_reduce_fusion
  767.3 5.2 multiply_convert_fusion
  772.5 1.5 convolution_multiply_fusion.1
  774.8 2.3 fusion.20
  777.8 1.7 copy-done.23
  780.5 7.6 shard_map.168
  788.1 2.6 multiply_convert_fusion.6
  790.8 5.2 convolution_convert_fusion.4
  796.0 41.0 %shard_map.169 = f32[128,2048]{1,0:T(8,128)S(1)} custom-call(bf16[8,128,2048]{2,1,0:T(8,128)(2,1)S(1)} %bitcast.225), custom_call_target="tpu_custom_call" | custom-call | bytes 67108864 | tf_op jit(solution)/shard_map/pallas_call | solution.py:596
  836.9 12.6 %convolution_convert_fusion.6 = bf16[2048,512]{1,0:T(8,128)(2,1)S(1)} fusion(bf16[4096,2048]{1,0:T(8,128)(2,1)} %all-gather.5.cloned.1.call-done, bf16[4096,512]{0,1:T(8,128)(2,1)S(1)} %copy-done.33), kind=kOutput, calls=%fused_computation.31 | convolution fusion | flops 8590983168 | bytes 23068672 | tf_op jit(solution)/shard_map/dot_general | solution.py:64
  849.6 64.0 %all_to_all.10.in_ref = bf16[8,256,512]{2,1,0:T(8,128)(2,1)} all-to-all(bf16[8,256,512]{2,1,0:T(8,128)(2,1)S(1)} %bitcast.256), channel_id=1, replica_groups=mesh['ey'=2,'ex'=2,'dz'=4,'dc'=2] {'dz','dc'}, dimensions={0} | all-to-all | bytes 4194304 | tf_op jit(solution)/shard_map/all_to_all | solution.py:892
  913.6 4.9 all-to-all-start
  918.7 5.3 fusion.4
  926.0 2.4 pad.9.clone
  928.5 6.8 convolution_convert_fusion.2
  935.3 4.9 convolution_convert_fusion.5
  940.2 225.9 %shard_map.170 = (f32[128,2048]{1,0:T(8,128)}, f32[64,2048]{1,0:T(8,128)}, f32[64,128]{1,0:T(8,128)}, bf16[512,768]{1,0:T(8,128)(2,1)}) custom-call(bf16[32,128,2048]{2,1,0:T(8,128)(2,1)} %bitcast.236, bf16[32,64,2048]{2,1,0:T(8,128)(2,1)} %bitcast.234, f32[32,64,128]{2,1,0:T(8,128)} %bitcast.247, bf16[4,512,768]{2,1,0:T(8,128)(2,1)} %bitcast.254), custom_call_target="tpu_custom_call" | custom-call | bytes 469762048 | tf_op jit(solution)/shard_map/pallas_call | solution.py:407
  1166.2 2.9 reshape.375
  1169.1 3.6 copy.118
  1172.6 2.8 reshape.374
  1176.8 2.4 multiply_add_fusion
  1179.2 2.5 fusion.27
  1181.7 1.6 copy-done.3
  1183.3 5.7 shard_map.172
  1189.0 11.3 shard_map.171
  (241 shorter events, 24.3 us)
Async XLA Ops:
  7.2 6.6 copy-start.1
  7.2 172.8 %all-gather.3.cloned.1.call-start = ((), (), s32[]{:S(2)}) async-start(), calls=%async_computation.2 | async-start | bytes 8650752 | tf_op jit(solution)/shard_map/all_gather | solution.py:757
  9.1 473.3 %all-gather.5.cloned.1.call-start = ((), (), s32[]{:S(2)}) async-start(), calls=%async_computation.3 | async-start | bytes 17301504 | tf_op jit(solution)/shard_map/all_gather | solution.py:811
  112.2 89.3 %copy-start.7 = (bf16[4,8,64,128]{3,2,1,0:T(8,128)(2,1)}, bf16[4,8,64,128]{3,2,1,0:T(8,128)(2,1)S(1)}, u32[]{:S(2)}) copy-start(bf16[4,8,64,128]{3,2,1,0:T(8,128)(2,1)S(1)} %get-tuple-element.33) | copy-start | bytes 1572868
  112.6 7.2 copy-start.15
  112.7 7.1 copy-start.50
  112.7 72.1 %copy-start.54 = (f32[1,2048]{1,0:T(1,128)}, f32[1,2048]{1,0:T(1,128)S(1)}, u32[]{:S(2)}) copy-start(f32[1,2048]{1,0:T(1,128)S(1)} %get-tuple-element.122) | copy-start | bytes 24580
  123.5 37.0 %copy-start.47 = (bf16[1024,256]{0,1:T(8,128)(2,1)}, bf16[1024,256]{0,1:T(8,128)(2,1)S(1)}, u32[]{:S(2)}) copy-start(bf16[1024,256]{0,1:T(8,128)(2,1)S(1)} %slice.182) | copy-start | bytes 1572868
  149.2 11.3 copy-start.64
  149.2 11.3 copy-start.66
  149.2 11.2 copy-start.59
  149.3 11.2 copy-start.61
  151.5 2.3 copy-start.35
  153.8 10.9 copy-start.30
  153.9 10.8 copy-start.39
  160.5 4.2 copy-start.72
  160.5 18.5 %copy-start.37 = (bf16[128,2048]{1,0:T(8,128)(2,1)S(1)}, bf16[128,2048]{1,0:T(8,128)(2,1)}, u32[]{:S(2)}) copy-start(bf16[128,2048]{1,0:T(8,128)(2,1)} %param.11) | copy-start | bytes 1572868
  179.0 5.8 copy-start.27
  179.0 5.7 copy-start.70
  184.8 16.7 %copy-start.78 = (s32[128,8]{0,1:T(8,128)S(1)}, s32[128,8]{0,1:T(8,128)}, u32[]{:S(2)}) copy-start(s32[128,8]{0,1:T(8,128)} %param.13) | copy-start | bytes 12292
  185.9 264.3 %copy-start.5 = (bf16[128,2048]{1,0:T(8,128)(2,1)}, bf16[128,2048]{1,0:T(8,128)(2,1)S(1)}, u32[]{:S(2)}) copy-start(bf16[128,2048]{1,0:T(8,128)(2,1)S(1)} %multiply_convert_fusion.8.refs_0_) | copy-start | bytes 1572868
  186.0 3.5 copy-start.4
  450.2 5.7 copy-start.12
  459.3 23.2 %copy-start.18 = (bf16[8,256,512]{2,1,0:T(8,128)(2,1)S(1)}, bf16[8,256,512]{2,1,0:T(8,128)(2,1)}, u32[]{:S(2)}) copy-start(bf16[8,256,512]{2,1,0:T(8,128)(2,1)} %copy-done.17) | copy-start | bytes 6291460
  601.6 135.8 %copy-start.53 = (f32[128,16]{0,1:T(8,128)S(1)}, f32[128,16]{0,1:T(8,128)}, u32[]{:S(2)}) copy-start(f32[128,16]{0,1:T(8,128)} %copy-done.52) | copy-start | bytes 24580
  601.6 135.8 %copy-start.58 = (pred[128,16]{0,1:T(8,128)(4,1)S(1)}, pred[128,16]{0,1:T(8,128)(4,1)}, u32[]{:S(2)}) copy-start(pred[128,16]{0,1:T(8,128)(4,1)} %copy-done.57) | copy-start | bytes 6148
  601.6 135.8 %copy-start.69 = (f32[128]{0:T(128)S(1)}, f32[128]{0:T(128)}, u32[]{:S(2)}) copy-start(f32[128]{0:T(128)} %copy-done.68) | copy-start | bytes 1540
  601.6 135.8 %copy-start.75 = (f32[128]{0:T(128)S(1)}, f32[128]{0:T(128)}, u32[]{:S(2)}) copy-start(f32[128]{0:T(128)} %copy-done.74) | copy-start | bytes 1540
  601.6 137.3 %copy-start.8 = (bf16[4,8,64,128]{3,2,1,0:T(8,128)(2,1)S(1)}, bf16[4,8,64,128]{3,2,1,0:T(8,128)(2,1)}, u32[]{:S(2)}) copy-start(bf16[4,8,64,128]{3,2,1,0:T(8,128)(2,1)} %copy-done.7) | copy-start | bytes 1572868
  601.6 137.3 %copy-start.20 = (f32[128,2048]{1,0:T(8,128)S(1)}, f32[128,2048]{1,0:T(8,128)}, u32[]{:S(2)}) copy-start(f32[128,2048]{1,0:T(8,128)} %copy-done.19) | copy-start | bytes 3145732
  601.7 137.3 %copy-start.55 = (f32[1,2048]{1,0:T(1,128)S(1)}, f32[1,2048]{1,0:T(1,128)}, u32[]{:S(2)}) copy-start(f32[1,2048]{1,0:T(1,128)} %copy-done.54) | copy-start | bytes 24580
  601.7 137.3 %copy-start.77 = (f32[128]{0:T(128)S(1)}, f32[128]{0:T(128)}, u32[]{:S(2)}) copy-start(f32[128]{0:T(128)} %copy-done.76) | copy-start | bytes 1540
  601.7 139.1 %copy-start.38 = (bf16[128,2048]{1,0:T(8,128)(2,1)S(1)}, bf16[128,2048]{1,0:T(8,128)(2,1)}, u32[]{:S(2)}) copy-start(bf16[128,2048]{1,0:T(8,128)(2,1)} %param.11) | copy-start | bytes 1572868
  601.7 140.5 %copy-start.71 = (f32[128]{0:T(128)S(1)}, f32[128]{0:T(128)}, u32[]{:S(2)}) copy-start(f32[128]{0:T(128)} %copy-done.70) | copy-start | bytes 1540
  742.2 20.2 %copy-start.48 = (bf16[1024,256]{0,1:T(8,128)(2,1)S(1)}, bf16[1024,256]{0,1:T(8,128)(2,1)}, u32[]{:S(2)}) copy-start(bf16[1024,256]{0,1:T(8,128)(2,1)} %copy-done.47) | copy-start | bytes 1572868
  742.2 20.2 %copy-start.73 = (f32[2,1024]{1,0:T(2,128)S(1)}, f32[2,1024]{1,0:T(2,128)}, u32[]{:S(2)}) copy-start(f32[2,1024]{1,0:T(2,128)} %copy-done.72) | copy-start | bytes 24580
  762.4 12.4 %slice-start = ((s8[8388608]{0:T(1024)(128)(4,1)}), s8[4194304]{0:T(1024)(128)(4,1)S(1)}, s32[]{:S(2)}) async-start(s8[8388608]{0:T(1024)(128)(4,1)} %bitcast.242), calls=%async_computation.4 | async-start | bytes 8388608
  767.3 5.2 copy-start.40
  767.3 6.8 copy-start.31
  767.3 7.5 slice-start.1
  774.8 2.4 copy-start.36
  774.8 2.4 copy-start.42
  777.2 2.3 copy-start.23
  777.2 2.3 copy-start.60
  777.2 2.3 copy-start.62
  777.2 2.3 copy-start.65
  777.2 13.5 %copy-start.16 = (bf16[4,8,64,768]{3,2,1,0:T(8,128)(2,1)S(1)}, bf16[4,8,64,768]{3,2,1,0:T(8,128)(2,1)}, u32[]{:S(2)}) copy-start(bf16[4,8,64,768]{3,2,1,0:T(8,128)(2,1)} %copy-done.14) | copy-start | bytes 9437188
  777.6 2.5 copy-start.28
  790.7 5.2 copy-start.43
  790.7 5.2 copy-start.45
  790.7 46.2 %copy-start.33 = (bf16[4096,512]{0,1:T(8,128)(2,1)S(1)}, bf16[4096,512]{0,1:T(8,128)(2,1)}, u32[]{:S(2)}) copy-start(bf16[4096,512]{0,1:T(8,128)(2,1)} %copy-done.32) | copy-start | bytes 12582916
  849.5 68.9 %copy-start.2 = (bf16[128,2048]{1,0:T(8,128)(2,1)S(1)}, bf16[128,2048]{1,0:T(8,128)(2,1)}, u32[]{:S(2)}) copy-start(bf16[128,2048]{1,0:T(8,128)(2,1)} %x_ref.1) | copy-start | bytes 1572868
  849.5 69.1 %copy-start.51 = (f32[1,2048]{1,0:T(1,128)S(1)}, f32[1,2048]{1,0:T(1,128)}, u32[]{:S(2)}) copy-start(f32[1,2048]{1,0:T(1,128)} %copy-done.50) | copy-start | bytes 24580
  849.6 69.1 %copy-start.63 = (f32[1024]{0:T(1024)S(1)}, f32[1024]{0:T(1024)}, u32[]{:S(2)}) copy-start(f32[1024]{0:T(1024)} %get-tuple-element.133) | copy-start | bytes 12292
  913.6 10.9 copy-start.6
  913.6 275.4 %all-to-all-start = ((bf16[8,256,1024]{2,1,0:T(8,128)(2,1)}), bf16[8,256,1024]{2,1,0:T(8,128)(2,1)}, u32[]{:S(2)}, u32[]{:S(2)}) async-start(bf16[8,256,1024]{2,1,0:T(8,128)(2,1)} %bitcast.249), calls=%async_computation | async-start | bytes 8388608 | tf_op jit(solution)/shard_map/all_to_all | solution.py:841
  918.4 10.0 copy-start.25
  926.0 9.3 copy-start.34
  926.0 9.3 copy-start.44
  926.0 9.3 copy-start.46
  926.0 9.3 copy-start.79
  1166.1 9.3 copy-start.56
  1166.1 10.7 copy-start.21
  1183.3 17.0 %copy-start.49 = (f32[64,2048]{1,0:T(8,128)S(1)}, f32[64,2048]{1,0:T(8,128)}, u32[]{:S(2)}) copy-start(f32[64,2048]{1,0:T(8,128)} %get-tuple-element.157) | copy-start | bytes 1572868
  (21 other events, 30.2 us)
Sparse Core Ops, SparseCore 0:
  11.6 118.8 all-gather.2
  186.1 235.3 all-gather.4

commit v3 on v2

--- a/solution.py
+++ b/solution.py
@@ -85,6 +85,11 @@
     def along(self, step):
         return lax.rem(self.z + step, self.depth)
 
+    def next_z(self, k):
+        first = self.z - 1 + 2 * lax.div(4 - self.z, 4)
+        last = 3 * lax.div(3 - self.z, 2)
+        return (self.z, first, 6 - self.z - first - last, last)[k]
+
     def block(self, column, z, core):
         return ((column[0] * 2 + column[1]) * self.depth + z) * 2 + core
 
@@ -159,14 +164,47 @@
     z_kind, near_kind, far_kind, core_kind = range(4)
     own = at.block(at.own_column, at.z, at.c)
     for n in range(count):
-        for k in others:
-            push(n, sources[n], own, z_kind, k - 1, at.chip(k))
+        push(n, sources[n], own, z_kind, at.z, (at.y, at.x, at.next_z(1), at.c))
         push(n, sources[n], own, near_kind, 0, at.near())
         push(n, sources[n], own, far_kind, 0, at.far())
         push(n, sources[n], own, core_kind, 0, at.core())
         copy = pltpu.make_async_copy(sources[n], targets[n].at[own], sems[9 * n + 8])
         copy.start()
         local.append(copy)
+
+    inner = lax.rem(at.z, depth - 1) != 0
+    onward = (at.z + 1, at.z + 1, at.z - 1, 3 * at.z - 3)
+
+    def forward(n, source, k):
+        z = at.next_z(k)
+        return pltpu.make_async_remote_copy(
+            src_ref=source,
+            dst_ref=targets[n].at[at.block(at.own_column, z, at.c)],
+            send_sem=sems[9 * n].at[z if k else depth],
+            recv_sem=sems[9 * n + 1].at[z],
+            device_id=(at.y, at.x, onward[k], at.c),
+            device_id_type=MESH_ID,
+        )
+
+    @pl.when(inner)
+    def _():
+        for n in range(count):
+            forward(n, sources[n], 0).start()
+
+    for k in others:
+        index = at.block(at.own_column, at.next_z(k), at.c)
+        for n in range(count):
+            arrive(n, index, z_kind, at.next_z(k))
+
+        @pl.when(inner)
+        def _(index=index, k=k):
+            for n in range(count):
+                forward(n, targets[n].at[index], k).start()
+
+        for n in range(count):
+            push(n, targets[n].at[index], index, near_kind, k, at.near())
+            push(n, targets[n].at[index], index, far_kind, k, at.far())
+            push(n, targets[n].at[index], index, core_kind, k, at.core())
     own_rank = at.z * 2 + at.c
     for n in range(extra):
         for slot, there in enumerate(peers):
@@ -184,35 +222,37 @@
         )
         copy.start()
         local.append(copy)
-    for k in others:
-        index = at.block(at.own_column, at.along(depth - k), at.c)
-        for n in range(count):
-            arrive(n, index, z_kind, k - 1)
-            push(n, targets[n].at[index], index, near_kind, k, at.near())
-            push(n, targets[n].at[index], index, far_kind, k, at.far())
-            push(n, targets[n].at[index], index, core_kind, k, at.core())
     for k in range(depth):
-        index = at.block(at.near_of(at.c), at.along(depth - k), at.c)
+        index = at.block(at.near_of(at.c), at.next_z(k), at.c)
         for n in range(count):
             arrive(n, index, near_kind, k)
             push(n, targets[n].at[index], index, far_kind, depth + k, at.far())
             push(n, targets[n].at[index], index, core_kind, depth + k, at.core())
     for j in range(2 * depth):
         column = at.far_of(at.c) if j < depth else at.other_column
-        index = at.block(column, at.along(depth - j % depth), at.c)
+        index = at.block(column, at.next_z(j % depth), at.c)
         for n in range(count):
             arrive(n, index, far_kind, j)
             push(n, targets[n].at[index], index, core_kind, 2 * depth + j, at.core())
     core = 1 - at.c
     columns = [at.own_column, at.near_of(core), at.far_of(core), at.other_column]
     for j in range(4 * depth):
-        index = at.block(columns[j // depth], at.along(depth - j % depth), core)
+        index = at.block(columns[j // depth], at.next_z(j % depth), core)
         for n in range(count):
             arrive(n, index, core_kind, j)
     for n in range(extra):
         for slot, (k, core) in enumerate(ranks):
             target = extra_targets[n].at[at.along(depth - k) * 2 + lax.rem(at.c + core, 2)]
             remote(target, target, extra_sems[3 * n :], slot, at.core()).wait_recv()
+
+    @pl.when(inner)
+    def _():
+        for n in range(count):
+            forward(n, sources[n], 0).wait_send()
+            for k in others:
+                index = at.block(at.own_column, at.next_z(k), at.c)
+                forward(n, targets[n].at[index], k).wait_send()
+
     for copy in started:
         copy.wait_send()
     for copy in local:
@@ -222,7 +262,7 @@
 def spread(depth, ident, arrays, extras=()):
     sems = []
     for _ in arrays:
-        sems += pair(depth - 1) + pair(depth) + pair(2 * depth) + pair(4 * depth)
+        sems += pair(depth + 1) + pair(depth) + pair(2 * depth) + pair(4 * depth)
         sems.append(pltpu.SemaphoreType.DMA)
     for _ in extras:
         sems += pair(2 * depth - 1) + [pltpu.SemaphoreType.DMA]
@@ -261,23 +301,34 @@
     lax.fori_loop(0, rows // tile, body, 0)
 
 
-def collect_kernel(depth, count, shared, *refs):
-    whole = count + shared
-    parts, totals = refs[:count], refs[whole : whole + count]
-    scratch, sems = refs[2 * whole : 2 * whole + 5 * count], refs[2 * whole + 5 * count :]
+def collect_kernel(depth, counts, *refs):
+    rest = iter(refs)
+
+    def take(count):
+        return [next(rest) for _ in range(count)]
+
+    mains, smalls, shareds, extras = (take(count) for count in counts)
+    main_totals, small_totals, shared_totals, extra_outs = (take(count) for count in counts)
+    main_buffers = [take(5) for _ in mains]
+    small_buffers = [take(5) for _ in smalls]
+    shared_buffers = [take(3) for _ in shareds]
+    shared_outs = [take(1)[0] for _ in shareds]
+    main_sems = [take(9) for _ in mains]
+    small_sems = [take(9) for _ in smalls]
+    shared_sems = [take(7) for _ in shareds]
+    extra_sems = [take(3) for _ in extras]
     at = Place(depth)
     ranks = [(k, core) for k in range(depth) for core in range(2) if k or core]
     peers = [at.chip(k, lax.rem(at.c + core, 2)) for k, core in ranks]
     meet([at.near(), at.far()] + peers)
     started = []
-    groups = (3, 2, 1, 0)
-    per = 9
-
-    def block(slot, core):
-        column = (at.own_column, at.near_of(core), at.far_of(core), at.other_column)[
-            groups[slot // depth]
-        ]
-        return at.block(column, at.along(1 + slot % depth), core)
+    own_rank = at.z * 2 + at.c
+
+    def columns(core):
+        return at.other_column, at.far_of(core), at.near_of(core), at.own_column
+
+    def number(column):
+        return column[0] * 2 + column[1]
 
     def push(copy):
         copy.start()
@@ -286,129 +337,241 @@
     def arrive(buffer, pair_of, slot):
         remote(buffer.at[slot], buffer.at[slot], pair_of, slot, at.core()).wait_recv()
 
-    def load(n, slot):
+    def piece(ref, rank):
+        rows = ref.shape[0] // (2 * depth)
+        return ref.at[pl.ds(pl.multiple_of(rank * rows, rows), rows)]
+
+    def block(group, k, core):
+        return at.block(columns(core)[group], at.along(1 + k), core)
+
+    def main_load(n, group, k):
+        slot = group * depth + k
         return pltpu.make_async_copy(
-            parts[n].at[block(slot, at.c)], scratch[5 * n].at[slot], sems[per * n + 8].at[slot]
+            mains[n].at[block(group, k, at.c)], main_buffers[n][0].at[slot], main_sems[n][8].at[slot]
         )
 
-    def number(column):
-        return column[0] * 2 + column[1]
-
-    if shared:
-        part, arrived = refs[count], refs[whole + count]
-        mine, far_in, near_in, local = refs[-10:-6]
-        far_sems, near_sems, out_sems = refs[-6:-4], refs[-4:-2], refs[-2:]
-        columns = [at.other_column, at.far_of(at.c), at.near_of(at.c), at.own_column]
-        for i in range(2):
-            push(remote(part.at[number(columns[i])], far_in.at[i], far_sems, i, at.far()))
-            pltpu.make_async_copy(
-                part.at[number(columns[2 + i])], mine.at[i], local.at[i]
-            ).start()
-    for slot in range(4 * depth):
-        for n in range(count):
-            push(
-                remote(
-                    parts[n].at[block(slot, 1 - at.c)],
-                    scratch[5 * n + 1].at[slot],
-                    sems[per * n :],
-                    slot,
-                    at.core(),
-                )
-            )
-            load(n, slot).start()
-
-    def add(n, slot, more):
-        mine, crossed = scratch[5 * n : 5 * n + 2]
-        load(n, slot).wait()
-        arrive(crossed, sems[per * n :], slot)
+    def main_cross(group, k):
+        slot = group * depth + k
+        for n, (part, buffers, sems) in enumerate(zip(mains, main_buffers, main_sems)):
+            source = part.at[block(group, k, 1 - at.c)]
+            push(remote(source, buffers[1].at[slot], sems[0:2], slot, at.core()))
+            main_load(n, group, k).start()
+
+    def main_sum(n, group, k, more):
+        mine, crossed = main_buffers[n][:2]
+        slot = group * depth + k
+        main_load(n, group, k).wait()
+        arrive(crossed, main_sems[n][0:2], slot)
         terms = [(mine, (slot,)), (crossed, (slot,))] + more
         if slot < 4 * depth - 1:
             sum_rows(mine, (slot,), terms)
         else:
-            sum_rows(totals[n], (), terms)
+            sum_rows(main_totals[n], (), terms)
         return mine.at[slot]
 
-    for n in range(count):
-        for slot in range(2 * depth):
-            total = add(n, slot, [])
-            far_in = scratch[5 * n + 2]
-            push(remote(total, far_in.at[slot], sems[per * n + 2 :], slot, at.far()))
-    if shared:
-        mine, far_in, near_in, local = refs[-10:-6]
-        pltpu.make_async_copy(part.at[number(columns[2])], mine.at[0], local.at[0]).wait()
-        arrive(far_in, far_sems, 0)
-        sum_rows(mine, (0,), [(mine, (0,)), (far_in, (0,))])
-        push(remote(mine.at[0], near_in.at[0], near_sems, 0, at.near()))
-    for n in range(count):
-        far_in, near_in = scratch[5 * n + 2 : 5 * n + 4]
-        for k in range(depth):
-            arrive(far_in, sems[per * n + 2 :], k)
-            total = add(n, 2 * depth + k, [(far_in, (k,))])
-            push(remote(total, near_in.at[k], sems[per * n + 4 :], k, at.near()))
-    if shared:
-        mine, far_in, near_in, local = refs[-10:-6]
-        pltpu.make_async_copy(part.at[number(columns[3])], mine.at[1], local.at[1]).wait()
-        arrive(far_in, far_sems, 1)
-        arrive(near_in, near_sems, 0)
-        sum_rows(mine, (1,), [(mine, (1,)), (far_in, (1,)), (near_in, (0,))])
-        rows = arrived.shape[0] // (2 * depth)
-
-        def piece(ref, rank):
-            return ref.at[pl.ds(pl.multiple_of(rank * rows, rows), rows)]
-
-        own_rank = at.z * 2 + at.c
+    def main_far(k):
+        for n, (buffers, sems) in enumerate(zip(main_buffers, main_sems)):
+            for group in range(2):
+                slot = group * depth + k
+                total = main_sum(n, group, k, [])
+                push(remote(total, buffers[2].at[slot], sems[2:4], slot, at.far()))
+
+    def main_near(k):
+        for n, (buffers, sems) in enumerate(zip(main_buffers, main_sems)):
+            arrive(buffers[2], sems[2:4], k)
+            total = main_sum(n, 2, k, [(buffers[2], (k,))])
+            push(remote(total, buffers[3].at[k], sems[4:6], k, at.near()))
+
+    def main_own(k):
+        for n, (buffers, sems) in enumerate(zip(main_buffers, main_sems)):
+            arrive(buffers[2], sems[2:4], depth + k)
+            arrive(buffers[3], sems[4:6], k)
+            total = main_sum(n, 3, k, [(buffers[2], (depth + k,)), (buffers[3], (k,))])
+            if k < depth - 1:
+                push(remote(total, buffers[4].at[k], sems[6:8], k, at.chip(1 + k)))
+
+    def small_load(n, group):
+        return pltpu.make_async_copy(
+            smalls[n].at[at.c, number(columns(at.c)[group])],
+            small_buffers[n][0].at[group],
+            small_sems[n][8].at[group],
+        )
+
+    def small_cross():
+        for n, (part, buffers, sems) in enumerate(zip(smalls, small_buffers, small_sems)):
+            for group in range(4):
+                source = part.at[1 - at.c, number(columns(1 - at.c)[group])]
+                push(remote(source, buffers[1].at[group], sems[0:2], group, at.core()))
+                small_load(n, group).start()
+
+    def small_sum(n, group, more):
+        mine, crossed = small_buffers[n][:2]
+        small_load(n, group).wait()
+        arrive(crossed, small_sems[n][0:2], group)
+        for j in range(depth):
+            terms = [(mine, (group, j)), (crossed, (group, j))]
+            sum_rows(mine, (group, j), terms + [(ref, (i, j)) for ref, i in more])
+        return mine.at[group]
+
+    def small_far():
+        for n, (buffers, sems) in enumerate(zip(small_buffers, small_sems)):
+            for group in range(2):
+                total = small_sum(n, group, [])
+                push(remote(total, buffers[2].at[group], sems[2:4], group, at.far()))
+
+    def small_near():
+        for n, (buffers, sems) in enumerate(zip(small_buffers, small_sems)):
+            arrive(buffers[2], sems[2:4], 0)
+            total = small_sum(n, 2, [(buffers[2], 0)])
+            push(remote(total, buffers[3].at[0], sems[4:6], 0, at.near()))
+
+    def small_own():
+        for n, (buffers, sems) in enumerate(zip(small_buffers, small_sems)):
+            arrive(buffers[2], sems[2:4], 1)
+            arrive(buffers[3], sems[4:6], 0)
+            total = small_sum(n, 3, [(buffers[2], 1), (buffers[3], 0)])
+            for k in range(1, depth):
+                there = at.chip(k)
+                source = total.at[there[2]]
+                push(remote(source, buffers[4].at[k - 1], sems[6:8], k - 1, there))
+
+    def shared_load(n, i):
+        return pltpu.make_async_copy(
+            shareds[n].at[number(columns(at.c)[2 + i])], shared_buffers[n][0].at[i], shared_sems[n][0].at[i]
+        )
+
+    def shared_far():
+        for n, (part, buffers, sems) in enumerate(zip(shareds, shared_buffers, shared_sems)):
+            for i in range(2):
+                source = part.at[number(columns(at.c)[i])]
+                push(remote(source, buffers[1].at[i], sems[1:3], i, at.far()))
+                shared_load(n, i).start()
+
+    def shared_near():
+        for n, ((mine, far_in, near_in), sems) in enumerate(zip(shared_buffers, shared_sems)):
+            shared_load(n, 0).wait()
+            arrive(far_in, sems[1:3], 0)
+            sum_rows(mine, (0,), [(mine, (0,)), (far_in, (0,))])
+            push(remote(mine.at[0], near_in.at[0], sems[3:5], 0, at.near()))
+
+    def shared_own():
+        for n, ((mine, far_in, near_in), sems) in enumerate(zip(shared_buffers, shared_sems)):
+            shared_load(n, 1).wait()
+            arrive(far_in, sems[1:3], 1)
+            arrive(near_in, sems[3:5], 0)
+            sum_rows(mine, (1,), [(mine, (1,)), (far_in, (1,)), (near_in, (0,))])
+            for slot, there in enumerate(peers):
+                source = piece(mine.at[1], there[2] * 2 + there[3])
+                push(remote(source, piece(shared_outs[n], own_rank), sems[5:7], slot, there))
+            shared_kept(n).start()
+
+    def shared_kept(n):
+        mine = shared_buffers[n][0]
+        return pltpu.make_async_copy(
+            piece(mine.at[1], own_rank), piece(shared_outs[n], own_rank), shared_sems[n][0].at[2]
+        )
+
+    def extra_kept(n):
+        return pltpu.make_async_copy(
+            extras[n].at[own_rank], extra_outs[n].at[own_rank], extra_sems[n][2]
+        )
+
+    order = [(main_far, k) for k in range(2)] + [(main_near, 0)]
+    for k in range(2, depth):
+        order += [(main_far, k), (main_near, k - 1), (main_own, k - 2)]
+    order += [(main_near, depth - 1), (main_own, depth - 2), (main_own, depth - 1)]
+    groups = {main_far: (0, 1), main_near: (2,), main_own: (3,)}
+    shared_far()
+    small_cross()
+    for stage, k in order:
+        for group in groups[stage]:
+            main_cross(group, k)
+    for n in range(len(extras)):
         for slot, there in enumerate(peers):
-            source = piece(mine.at[1], there[2] * 2 + there[3])
-            push(remote(source, piece(arrived, own_rank), out_sems, slot, there))
-        kept = pltpu.make_async_copy(
-            piece(mine.at[1], own_rank), piece(arrived, own_rank), local.at[2]
-        )
-        kept.start()
-    for n in range(count):
-        far_in, near_in, z_in = scratch[5 * n + 2 : 5 * n + 5]
-        for k in range(depth):
-            arrive(far_in, sems[per * n + 2 :], depth + k)
-            arrive(near_in, sems[per * n + 4 :], k)
-            total = add(n, 3 * depth + k, [(far_in, (depth + k,)), (near_in, (k,))])
-            if k < depth - 1:
-                push(remote(total, z_in.at[k], sems[per * n + 6 :], k, at.chip(1 + k)))
-    for n in range(count):
-        z_in = scratch[5 * n + 4]
+            source = extras[n].at[there[2] * 2 + there[3]]
+            push(remote(source, extra_outs[n].at[own_rank], extra_sems[n][:2], slot, there))
+        extra_kept(n).start()
+    small_far()
+    for stage, k in order:
+        stage(k)
+        if (stage, k) == (main_near, 0):
+            shared_near()
+            small_near()
+        if (stage, k) == (main_own, 0):
+            shared_own()
+            small_own()
+    for n, (buffers, sems) in enumerate(zip(small_buffers, small_sems)):
         for k in range(depth - 1):
-            arrive(z_in, sems[per * n + 6 :], k)
-        sum_rows(totals[n], (), [(totals[n], ())] + [(z_in, (k,)) for k in range(depth - 1)])
-    if shared:
-        for slot, (k, core) in enumerate(ranks):
-            target = piece(arrived, at.along(depth - k) * 2 + lax.rem(at.c + core, 2))
-            remote(target, target, out_sems, slot, at.core()).wait_recv()
-        kept.wait()
+            arrive(buffers[4], sems[6:8], k)
+        terms = [(buffers[0], (3, at.z))] + [(buffers[4], (k,)) for k in range(depth - 1)]
+        sum_rows(small_totals[n], (), terms)
+    for n, (buffers, sems) in enumerate(zip(main_buffers, main_sems)):
+        for k in range(depth - 1):
+            arrive(buffers[4], sems[6:8], k)
+        terms = [(main_totals[n], ())] + [(buffers[4], (k,)) for k in range(depth - 1)]
+        sum_rows(main_totals[n], (), terms)
+    for slot, (k, core) in enumerate(ranks):
+        source = at.along(depth - k) * 2 + lax.rem(at.c + core, 2)
+        for n in range(len(shareds)):
+            target = piece(shared_outs[n], source)
+            remote(target, target, shared_sems[n][5:7], slot, at.core()).wait_recv()
+        for n in range(len(extras)):
+            target = extra_outs[n].at[source]
+            remote(target, target, extra_sems[n][:2], slot, at.core()).wait_recv()
+    for n in range(len(shareds)):
+        shared_kept(n).wait()
+        out, held = shared_totals[n], shared_outs[n]
+        count, rows = out.shape[:2]
+        heads = held.shape[1] // (count * HD)
+        for rank in range(2 * depth):
+            for i in range(count):
+                for j in range(heads):
+                    head = (rank % 2 * heads + j) * depth + rank // 2
+                    value = held[rank * rows : (rank + 1) * rows, (i * heads + j) * HD :][:, :HD]
+                    out[i, :, head * HD : (head + 1) * HD] = value.astype(out.dtype)
+    for n in range(len(extras)):
+        extra_kept(n).wait()
     for copy in started:
         copy.wait_send()
 
 
-def collect(depth, ident, *arrays, shared=None):
-    count = len(arrays)
+def collect(depth, ident, mains, smalls, shareds=(), extras=()):
+    dma = pltpu.SemaphoreType.DMA
+    peers = 2 * depth - 1
+
+    def by_core(a):
+        return a.reshape((4, depth, 2) + a.shape[1:]).transpose(2, 0, 1, 3, 4)
+
+    smalls = [by_core(a) for a in smalls]
     buffers, sems, shapes = [], [], []
-    for a in arrays:
+    for a in mains:
         for slots in (4 * depth, 4 * depth, 2 * depth, depth, depth - 1):
             buffers.append(pltpu.VMEM((slots,) + a.shape[1:], a.dtype))
         sems += pair(4 * depth) + pair(2 * depth) + pair(depth) + pair(depth - 1)
-        sems.append(pltpu.SemaphoreType.DMA((4 * depth,)))
+        sems.append(dma((4 * depth,)))
         shapes.append(jax.ShapeDtypeStruct(a.shape[1:], high_type))
-    specs = [pl.BlockSpec(memory_space=pltpu.VMEM)] * count
-    if shared is not None:
-        block = shared.shape[1:]
-        arrays += (shared,)
-        specs += in_hbm(1)
-        shapes.append(jax.ShapeDtypeStruct(block, shared.dtype))
-        sems += [pltpu.VMEM((slots,) + block, shared.dtype) for slots in (2, 2, 1)]
-        sems.append(pltpu.SemaphoreType.DMA((3,)))
-        sems += pair(2) + pair(1) + pair(2 * depth - 1)
+    for a in smalls:
+        for slots in ((4, depth), (4, depth), (2, depth), (1, depth), (depth - 1,)):
+            buffers.append(pltpu.VMEM(slots + a.shape[3:], a.dtype))
+        sems += pair(4) + pair(2) + pair(1) + pair(depth - 1) + [dma((4,))]
+        shapes.append(jax.ShapeDtypeStruct(a.shape[3:], high_type))
+    for a in shareds:
+        buffers += [pltpu.VMEM((slots,) + a.shape[1:], a.dtype) for slots in (2, 2, 1)]
+        buffers.append(pltpu.VMEM(a.shape[1:], a.dtype))
+        sems += [dma((3,))] + pair(2) + pair(1) + pair(peers)
+        shape = (3, a.shape[1] // (2 * depth), a.shape[2] // 3 * 2 * depth)
+        shapes.append(jax.ShapeDtypeStruct(shape, high_type))
+    for a in extras:
+        sems += pair(peers) + [dma]
+        shapes.append(jax.ShapeDtypeStruct(a.shape, a.dtype))
+    arrays = [*mains, *smalls, *shareds, *extras]
+    counts = (len(mains), len(smalls), len(shareds), len(extras))
+    in_vmem = [pl.BlockSpec(memory_space=pltpu.VMEM)] * (len(arrays) - len(extras))
     return pl.pallas_call(
-        functools.partial(collect_kernel, depth, count, shared is not None),
+        functools.partial(collect_kernel, depth, counts),
         out_shape=shapes,
         in_specs=in_hbm(len(arrays)),
-        out_specs=specs,
+        out_specs=in_vmem + in_hbm(len(extras)),
         scratch_shapes=buffers + sems,
         compiler_params=pltpu.CompilerParams(
             collective_id=ident, has_side_effects=True, vmem_limit_bytes=56 << 20
@@ -421,87 +584,154 @@
     )(*arrays)
 
 
-def gather_kernel(depth, x_ref, w_ref, s_ref, x_out, w_out, s_out, *sems):
+def gather_kernel(depth, x_ref, o_ref, w_ref, s_ref, x_out, o_out, w_out, s_out, *sems):
     at = Place(depth)
     ranks = [(k, core) for k in range(depth) for core in range(2) if k or core]
-
-    def peer(k, core):
-        return at.chip(k, lax.rem(at.c + core, 2))
-
-    meet([peer(k, core) for k, core in ranks] + [at.near(), at.far()])
+    peers = [at.chip(k, lax.rem(at.c + core, 2)) for k, core in ranks]
+    meet([at.near(), at.far()] + peers)
+    own, column = at.z * 2 + at.c, at.y * 2 + at.x
+    x_z, x_core, o_z, o_near, o_far, o_core, w_sems, s_sems, w_side, s_side = (
+        sems[2 * i : 2 * i + 2] for i in range(10)
+    )
     started, local = [], []
+    inner = lax.rem(at.z, depth - 1) != 0
+    onward = (at.z + 1, at.z + 1, at.z - 1, 3 * at.z - 3)
+    own_block = at.block(at.own_column, at.z, at.c)
 
     def push(copy):
         copy.start()
         started.append(copy)
 
-    def rank(z, c):
-        return z * 2 + c
-
-    own, column = rank(at.z, at.c), at.y * 2 + at.x
-    x_z, x_core, w_sems, s_sems, w_side, s_side = (sems[2 * i : 2 * i + 2] for i in range(6))
-    for slot, (k, core) in enumerate(ranks):
-        there = peer(k, core)
+    def arrive(target, pair_of, slot):
+        remote(target, target, pair_of, slot, at.core()).wait_recv()
+
+    def x_place(k):
+        return x_out.at[at.next_z(k) * 2 + at.c]
+
+    def o_place(k):
+        return o_out.at[at.block(at.own_column, at.next_z(k), at.c)]
+
+    def forward(source, target, pair_of, k):
+        z = at.next_z(k)
+        return pltpu.make_async_remote_copy(
+            src_ref=source,
+            dst_ref=target,
+            send_sem=pair_of[0].at[z if k else depth],
+            recv_sem=pair_of[1].at[z],
+            device_id=(at.y, at.x, onward[k], at.c),
+            device_id_type=MESH_ID,
+        )
+
+    for slot, there in enumerate(peers):
         push(remote(s_ref, s_out.at[column, own], s_sems, slot, there))
-        push(
-            remote(
-                w_ref.at[rank(there[2], there[3])], w_out.at[column, own], w_sems, slot, there
-            )
+        source = w_ref.at[there[2] * 2 + there[3]]
+        push(remote(source, w_out.at[column, own], w_sems, slot, there))
+    first = (at.y, at.x, at.next_z(1), at.c)
+    push(remote(o_ref, o_place(0), o_z, at.z, first))
+    push(remote(x_ref, x_place(0), x_z, at.z, first))
+
+    @pl.when(inner)
+    def _():
+        forward(o_ref, o_place(0), o_z, 0).start()
+        forward(x_ref, x_place(0), x_z, 0).start()
+
+    push(remote(x_ref, x_place(0), x_core, 0, at.core()))
+    push(remote(o_ref, o_place(0), o_near, 0, at.near()))
+    push(remote(o_ref, o_place(0), o_far, 0, at.far()))
+    push(remote(o_ref, o_place(0), o_core, 0, at.core()))
+    for i, (source, target) in enumerate(
+        (
+            (x_ref, x_place(0)),
+            (o_ref, o_place(0)),
+            (w_ref.at[own], w_out.at[column, own]),
+            (s_ref, s_out.at[column, own]),
         )
-    for k in range(1, depth):
-        push(remote(x_ref, x_out.at[own], x_z, k - 1, at.chip(k)))
-    push(remote(x_ref, x_out.at[own], x_core, 0, at.core()))
-    for i, (source, target) in enumerate(
-        ((x_ref, x_out.at[own]), (w_ref.at[own], w_out.at[column, own]), (s_ref, s_out.at[column, own]))
     ):
-        copy = pltpu.make_async_copy(source, target, sems[12].at[i])
+        copy = pltpu.make_async_copy(source, target, sems[20].at[i])
         copy.start()
         local.append(copy)
-
-    def arrive(target, pair_of, slot):
-        remote(target, target, pair_of, slot, at.core()).wait_recv()
-
-    for slot, (k, core) in enumerate(ranks):
-        source = rank(at.along(depth - k), lax.rem(at.c + core, 2))
-        arrive(s_out.at[column, source], s_sems, slot)
-        arrive(w_out.at[column, source], w_sems, slot)
-    for copy in local:
-        copy.wait()
     near_y, near_x = at.near_of(at.c)
     far_y, far_x = at.far_of(at.c)
     beside, across = near_y * 2 + near_x, far_y * 2 + far_x
-    for target, pair_of in ((s_out, s_side), (w_out, w_side)):
-        push(remote(target.at[column], target.at[column], pair_of, 0, at.near()))
-        push(remote(target.at[column], target.at[column], pair_of, 1, at.far()))
+    sides = ((s_out, s_side), (w_out, w_side))
     for k in range(1, depth):
-        source = rank(at.along(depth - k), at.c)
-        arrive(x_out.at[source], x_z, k - 1)
-        push(remote(x_out.at[source], x_out.at[source], x_core, k, at.core()))
-    for target, pair_of in ((s_out, s_side), (w_out, w_side)):
+        arrive(o_place(k), o_z, at.next_z(k))
+
+        @pl.when(inner)
+        def _(k=k):
+            forward(o_place(k), o_place(k), o_z, k).start()
+
+        push(remote(o_place(k), o_place(k), o_near, k, at.near()))
+        push(remote(o_place(k), o_place(k), o_far, k, at.far()))
+        push(remote(o_place(k), o_place(k), o_core, k, at.core()))
+        arrive(x_place(k), x_z, at.next_z(k))
+
+        @pl.when(inner)
+        def _(k=k):
+            forward(x_place(k), x_place(k), x_z, k).start()
+
+        push(remote(x_place(k), x_place(k), x_core, k, at.core()))
+        if k == 1:
+            for slot, (j, core) in enumerate(ranks):
+                source = at.along(depth - j) * 2 + lax.rem(at.c + core, 2)
+                arrive(s_out.at[column, source], s_sems, slot)
+                arrive(w_out.at[column, source], w_sems, slot)
+            for copy in local:
+                copy.wait()
+            for target, pair_of in sides:
+                push(remote(target.at[column], target.at[column], pair_of, 0, at.near()))
+                push(remote(target.at[column], target.at[column], pair_of, 1, at.far()))
+    for target, pair_of in sides:
         arrive(target.at[beside], pair_of, 0)
         push(remote(target.at[beside], target.at[beside], pair_of, 2, at.far()))
     for k in range(depth):
-        arrive(x_out.at[rank(at.along(depth - k), 1 - at.c)], x_core, k)
-    for target, pair_of in ((s_out, s_side), (w_out, w_side)):
+        target = o_out.at[at.block(at.near_of(at.c), at.next_z(k), at.c)]
+        arrive(target, o_near, k)
+        push(remote(target, target, o_far, depth + k, at.far()))
+        push(remote(target, target, o_core, depth + k, at.core()))
+    for j in range(2 * depth):
+        place = at.far_of(at.c) if j < depth else at.other_column
+        target = o_out.at[at.block(place, at.next_z(j % depth), at.c)]
+        arrive(target, o_far, j)
+        push(remote(target, target, o_core, 2 * depth + j, at.core()))
+    for target, pair_of in sides:
         arrive(target.at[across], pair_of, 1)
         arrive(target.at[3 - column], pair_of, 2)
+    for k in range(depth):
+        arrive(x_out.at[at.next_z(k) * 2 + 1 - at.c], x_core, k)
+    core = 1 - at.c
+    places = [at.own_column, at.near_of(core), at.far_of(core), at.other_column]
+    for j in range(4 * depth):
+        index = at.block(places[j // depth], at.next_z(j % depth), core)
+        arrive(o_out.at[index], o_core, j)
+
+    @pl.when(inner)
+    def _():
+        forward(x_ref, x_place(0), x_z, 0).wait_send()
+        forward(o_ref, o_place(0), o_z, 0).wait_send()
+        for k in range(1, depth):
+            forward(x_place(k), x_place(k), x_z, k).wait_send()
+            forward(o_place(k), o_place(k), o_z, k).wait_send()
+
     for copy in started:
         copy.wait_send()
 
 
-def gather(depth, ident, x, w, s):
+def gather(depth, ident, x, o, w, s):
     ranks = 2 * depth
-    sems = pair(depth - 1) + pair(depth) + pair(ranks - 1) * 2 + pair(3) * 2
-    sems.append(pltpu.SemaphoreType.DMA((3,)))
+    sems = pair(depth + 1) + pair(depth) + pair(depth + 1) + pair(depth) + pair(2 * depth)
+    sems += pair(4 * depth) + pair(ranks - 1) * 2 + pair(3) * 2
+    sems.append(pltpu.SemaphoreType.DMA((4,)))
     return pl.pallas_call(
         functools.partial(gather_kernel, depth),
         out_shape=[
             jax.ShapeDtypeStruct((ranks,) + x.shape, x.dtype),
+            jax.ShapeDtypeStruct((4 * ranks,) + o.shape, o.dtype),
             jax.ShapeDtypeStruct((4,) + w.shape, w.dtype),
             jax.ShapeDtypeStruct((4, ranks) + s.shape, s.dtype),
         ],
-        in_specs=in_hbm(3),
-        out_specs=in_hbm(3),
+        in_specs=in_hbm(4),
+        out_specs=in_hbm(4),
         scratch_shapes=sems,
         compiler_params=pltpu.CompilerParams(
             collective_id=ident, has_side_effects=True, vmem_limit_bytes=16 << 20
@@ -509,7 +739,7 @@
         cost_estimate=pl.CostEstimate(
             flops=0, bytes_accessed=64 * depth * x.size, transcendentals=0
         ),
-    )(x, w, s)
+    )(x, o, w, s)
 
 
 def exchange_kernel(depth, same, x_ref, out_ref, send_sems, recv_sems, local_sem):
@@ -687,6 +917,114 @@
         out_shape=jax.ShapeDtypeStruct((rows * ranks * span // 128, 128), high_type),
         compiler_params=pltpu.CompilerParams(vmem_limit_bytes=32 << 20),
     )(sliced)
+
+
+def experts_kernel(
+    local, tokens_ref, grads_ref, gates_ref, in_ref, down_ref, *outputs
+):
+    back_ref, mixed_ref, sums_ref, grad_in_ref, grad_down_ref, in_total, down_total = outputs
+    column = lax.axis_index("ey") * 2 + lax.axis_index("ex")
+    step = pl.program_id(0)
+    blocks, experts, rows = gates_ref.shape
+    span = down_ref.shape[1]
+    width = tokens_ref.shape[2]
+    units_of = (
+        lax.broadcasted_iota(jnp.int32, (experts, span), 1) // 128 + column * local
+        == lax.broadcasted_iota(jnp.int32, (experts, span), 0)
+    ).astype(low_type)
+
+    def terms(values, count):
+        result = []
+        for _ in range(count):
+            result.append(values.astype(low_type))
+            values = values - result[-1].astype(high_type)
+        return result
+
+    tokens = tokens_ref[...].reshape(blocks * rows, width)
+    grads = grads_ref[...].reshape(blocks * rows, width)
+    gates = jnp.concatenate([gates_ref[b] for b in range(blocks)], axis=1)
+    gates = jnp.concatenate(terms(gates, 3), axis=0)
+    wide = t_dot(gates, jnp.concatenate([units_of] * 3, axis=0))
+    both = dot(tokens, in_ref[...])
+    gate_part, up_part = both[:, :span], both[:, span:]
+    down_grad = dot(grads, down_ref[...])
+    sigma = 0.5 + 0.5 * jnp.tanh(0.5 * gate_part)
+    silu = gate_part * sigma
+    hidden = (silu * up_part).astype(low_type).astype(high_type)
+    weighted = (wide * hidden).astype(low_type)
+    inner = hidden * down_grad
+    high, rest = terms(inner, 2)
+    sums = dot_t(units_of, high) + dot_t(units_of, rest)
+    for b in range(blocks):
+        sums_ref[b] = sums[:, b * rows : (b + 1) * rows]
+    grad_hidden = wide * down_grad
+    grad_gate = grad_hidden * up_part * (sigma + silu * (1.0 - sigma))
+    grad_both = jnp.concatenate([grad_gate, grad_hidden * silu], axis=1).astype(low_type)
+    back_ref[...] = dot_t(grad_both, in_ref[...]).astype(low_type).reshape(back_ref.shape)
+    mixed_ref[...] = dot_t(weighted, down_ref[...]).astype(low_type).reshape(mixed_ref.shape)
+
+    @pl.when(step == 0)
+    def _():
+        in_total[...] = jnp.zeros_like(in_total)
+        down_total[...] = jnp.zeros_like(down_total)
+
+    in_total[...] += t_dot(tokens, grad_both)
+    down_total[...] += t_dot(grads, weighted)
+
+    @pl.when(step == pl.num_programs(0) - 1)
+    def _():
+        grad_in_ref[...] = in_total[...].astype(low_type)
+        grad_down_ref[...] = down_total[...].astype(low_type)
+
+
+def run_experts(local, tokens, grads, gates, weights_in, weights_down):
+    devices, rows, width = tokens.shape
+    experts = gates.shape[1]
+    blocks = 4
+    span = weights_down.shape[1]
+    once = pl.Buffered(1)
+
+    def by_step(shape):
+        return pl.BlockSpec((blocks,) + shape, lambda i: (i, 0, 0))
+
+    def whole(shape):
+        return pl.BlockSpec(shape, lambda i: (0, 0), pipeline_mode=once)
+
+    return pl.pallas_call(
+        functools.partial(experts_kernel, local),
+        grid=(devices // blocks,),
+        in_specs=[
+            by_step((rows, width)),
+            by_step((rows, width)),
+            by_step((experts, rows)),
+            whole((width, 2 * span)),
+            whole((width, span)),
+        ],
+        out_specs=[
+            by_step((rows, width)),
+            by_step((rows, width)),
+            by_step((experts, rows)),
+            whole((width, 2 * span)),
+            whole((width, span)),
+        ],
+        out_shape=[
+            jax.ShapeDtypeStruct((devices, rows, width), low_type),
+            jax.ShapeDtypeStruct((devices, rows, width), low_type),
+            jax.ShapeDtypeStruct((devices, experts, rows), high_type),
+            jax.ShapeDtypeStruct((width, 2 * span), low_type),
+            jax.ShapeDtypeStruct((width, span), low_type),
+        ],
+        scratch_shapes=[
+            pltpu.VMEM((width, 2 * span), high_type),
+            pltpu.VMEM((width, span), high_type),
+        ],
+        compiler_params=pltpu.CompilerParams(vmem_limit_bytes=60 << 20),
+        cost_estimate=pl.CostEstimate(
+            flops=18 * devices * rows * width * span,
+            bytes_accessed=8 * devices * rows * width,
+            transcendentals=devices * rows * span,
+        ),
+    )(tokens, grads, gates, weights_in, weights_down)
 
 
 def grid_shards(
@@ -743,7 +1081,10 @@
     small = jnp.pad(small, ((0, 0), (0, 128 - small.shape[1])))
     packed = attn_qkv.astype(low_type).transpose(1, 0, 2)
     packed = by_rank(packed).reshape(ranks, weight_rows, 3 * own_width)
-    seq_input, qkv_weight, small = gather(depth, 0, residual_in, packed, small)
+    seq_input, out_weight, qkv_weight, small = gather(
+        depth, 0, residual_in, attn_out.astype(low_type), packed, small
+    )
+    out_weight = out_weight.reshape(width, width)
     qkv_weight = qkv_weight.reshape(width, 3 * own_width)
     small = small.reshape(width, 128)
     gain_rows = small[:, :4].T.astype(high_type)
@@ -754,8 +1095,6 @@
     ]
     normed_in = seq_input.reshape(seq_rows, width).astype(high_type)
     normed_in = (normed_in * rms_scale(normed_in) * gain_rows[0]).astype(low_type)
-    out_weight = lax.all_gather(attn_out.astype(low_type), GRID, axis=0, tiled=True)
-
     sliced_in, sliced_down = pack(ranks, expert_in, expert_down)
 
     raw = dot(normed_in, qkv_weight)
@@ -807,39 +1146,28 @@
 
     grad_rows = cotangent.astype(high_type)
     grad_comb = live_rows * grad_rows
-    own_grads, normed_mid = lax.optimization_barrier((grad_comb.astype(low_type), normed_mid))
+    after = jnp.minimum(scales[0, 0], 0.0)
+    own_grads = (grad_comb + after).astype(low_type)
     grads = lax.all_gather(own_grads, GRID, axis=0, tiled=True)
     tokens, gates_all, weights_in, weights_down = spread(
         depth, 3, (normed_mid, gates.T), (sliced_in, sliced_down)
     )
-    weights_in, weights_down = weights_in.reshape(width, -1), weights_down.reshape(width, -1)
-    tokens = tokens.reshape(-1, width)
-    gates_all = lax.dynamic_slice_in_dim(gates_all, column * local_experts, local_experts, 1)
-    gates_all = gates_all.transpose(0, 2, 1).reshape(-1, local_experts)
-    wide = jnp.repeat(gates_all, part, axis=1)
-    both_parts = dot(tokens, weights_in)
-    gate_part, up_part = both_parts[:, :span], both_parts[:, span:]
-    down_grad = dot(grads, weights_down)
-    sigma = jax.nn.sigmoid(gate_part)
-    hidden = (gate_part * sigma * up_part).astype(low_type).astype(high_type)
-    gate_sums = jnp.sum((hidden * down_grad).reshape(-1, rows, local_experts, part), axis=3)
-    weighted = (wide * hidden).astype(low_type)
-    grad_hidden = wide * down_grad
-    grad_gate = grad_hidden * up_part * sigma * (1.0 + gate_part * (1.0 - sigma))
-    grad_up = grad_hidden * gate_part * sigma
-    grad_both = jnp.concatenate([grad_gate, grad_up], axis=1).astype(low_type)
-    grad_in = t_dot(tokens, grad_both).astype(low_type)
-    grad_both, grad_in = lax.optimization_barrier((grad_both, grad_in))
-    back = dot_t(grad_both, weights_in).astype(low_type)
-    placed = jnp.zeros((4 * ranks, experts, rows), high_type)
-    placed = lax.dynamic_update_slice(
-        placed, gate_sums.transpose(0, 2, 1), (0, column * local_experts, 0)
-    )
-    mixed = dot_t(weighted, weights_down).astype(low_type)
-    back, mixed = lax.optimization_barrier((back, mixed))
-    grad_mid_norm, grad_gates = collect(depth, 4, back.reshape(-1, rows, width), placed)
-    sliced = lax.all_to_all(grad_in.reshape(ranks, chunk_rows, 2 * span), SEQ, 0, 0, tiled=True)
-    grad_expert_in = unpack(local_experts, sliced).reshape(
+    back, mixed, gate_sums, grad_in, grad_down = run_experts(
+        local_experts,
+        tokens,
+        grads.reshape(tokens.shape),
+        gates_all,
+        weights_in.reshape(width, -1),
+        weights_down.reshape(width, -1),
+    )
+    grad_mid_norm, grad_gates, sliced_in = collect(
+        depth,
+        4,
+        [back],
+        [gate_sums],
+        extras=[grad_in.reshape(ranks, chunk_rows, 2 * span)],
+    )
+    grad_expert_in = unpack(local_experts, sliced_in).reshape(
         chunk_rows, local_experts, ranks, 2, part
     )
     grad_expert_in = grad_expert_in.transpose(0, 1, 3, 2, 4).reshape(expert_in.shape)
@@ -887,13 +1215,7 @@
 
     share = dot_t(grad_raw, qkv_weight).astype(low_type).reshape(ranks, rows, width)
     grad_norm_in = collect_column(depth, 8, share)
-    grad_norm_in, grads, attended = lax.optimization_barrier((grad_norm_in, grads, attended))
-    grad_down = t_dot(grads, weighted).astype(low_type)
-    sliced = lax.all_to_all(grad_down.reshape(ranks, chunk_rows, span), SEQ, 0, 0, tiled=True)
-    grad_expert_down = unpack(local_experts, sliced).reshape(
-        chunk_rows, ranks, local_experts, part
-    )
-    grad_expert_down = grad_expert_down.transpose(0, 2, 1, 3).reshape(expert_down.shape)
+
     scale_in = rms_scale(input_rows)
     grad_in_rows, grad_gain_in = rms_back(
         grad_norm_in, input_rows * scale_in, scale_in, gain_rows[0]
@@ -922,17 +1244,19 @@
     grad_small = jnp.pad(grad_small, ((0, 0), (0, 128 - grad_small.shape[1])))
     grad_out = t_dot(attended, grad_branch).astype(low_type)
     grad_qkv = t_dot(normed_in, grad_raw).astype(low_type)
-    combined, grad_out, grad_small, grad_qkv = collect(
+    combined, grad_out, grad_small, grad_qkv, sliced_down = collect(
         depth,
         5,
-        mixed.reshape(-1, rows, width),
-        grad_out.reshape(-1, weight_rows, width),
-        grad_small.reshape(-1, weight_rows, 128),
-        shared=grad_qkv.reshape(columns, -1, 3 * own_width),
-    )
+        [mixed, grad_out.reshape(-1, weight_rows, width)],
+        [grad_small.reshape(-1, weight_rows, 128)],
+        [grad_qkv.reshape(columns, -1, 3 * own_width)],
+        [grad_down.reshape(ranks, chunk_rows, span)],
+    )
+    grad_expert_down = unpack(local_experts, sliced_down).reshape(
+        chunk_rows, ranks, local_experts, part
+    )
+    grad_expert_down = grad_expert_down.transpose(0, 2, 1, 3).reshape(expert_down.shape)
     output = middle + live_rows * combined
-    grad_qkv = by_head(grad_qkv.reshape(ranks, weight_rows, 3, own_width))
-    grad_qkv = grad_qkv.transpose(1, 0, 2).astype(high_type)
     return (
         output,
         grad_input,

time: 1220 us -> 1000 us (0.82)
  matrix products: 166 us -> 53.5 us
  blocking collectives: 64 us -> 0 us
  other arithmetic: 69.2 us -> 28.3 us
    all_to_all x1 -> x0, blocking collectives: 64 us -> none  [grid_shards(): lax.all_to_all(grad_down.reshape(ranks, chunk_rows, span), SEQ, 0, 0, til...]
    pallas_call x2 -> x3, Pallas kernels: 362 us -> 407 us  [the longest x2 309 us: collect(): pl.pallas_call(functools.partial(collect_kernel, depth, counts), out_shap...]
    dot_general x5 -> x3, matrix products: 51.7 us -> 13 us  [dot_t(): lax.dot_general(left, right, (((1,), (1,)), ((), ())), preferred_element_...]
    dot_general x5 -> x3, matrix products: 46.6 us -> 9.23 us  [dot(): return jnp.dot(left, right, preferred_element_type=high_type)]
    dot_general x5 -> x3, matrix products: 47.7 us -> 10.9 us  [t_dot(): lax.dot_general(left, right, (((0,), (0,)), ((), ())), preferred_element_...]
    pallas_call x1, Pallas kernels: 245 us -> 215 us  [spread(): pl.pallas_call(functools.partial(spread_kernel, depth, len(arrays), len(e...]
    unnamed x2 -> x1, other arithmetic: 14.6 us -> 0.01 us
    unnamed x173 -> x121, local copies, waits for them, and re-layouts: 47.5 us -> 40.9 us
  transfers between devices with their start and end apart: 3 -> 1, of which waited for: 0 -> 0; matrix products, arithmetic and copies ran while one was open for 8% -> 3% of each run, Pallas kernels for 51% -> 24%
where the time goes in v3:
time: 1000 us; the launch traced here: 989 us
  Pallas kernels  835 us (84%)
  local copies, waits for them, and re-layouts  55.6 us (6%)
  matrix products  53.5 us (5%)
  other arithmetic  28.3 us (3%)
  between operations  16.6 us (2%)
    pallas_call x2, Pallas kernels, collect(): pl.pallas_call(functools.partial(collect_kernel, depth, counts), out_shap...  309 us
    pallas_call x1, Pallas kernels, spread(): pl.pallas_call(functools.partial(spread_kernel, depth, len(arrays), len(e...  215 us
    pallas_call x1, Pallas kernels, gather(): pl.pallas_call(functools.partial(gather_kernel, depth), out_shape=[jax.Sh...  101 us
    pallas_call x1, Pallas kernels, run_experts(): pl.pallas_call(functools.partial(experts_kernel, local), grid=(devices //...  98.2 us
    pallas_call x4, Pallas kernels, exchange(): pl.pallas_call(functools.partial(exchange_kernel, depth, same), out_shape...  49.3 us
    pallas_call x1, Pallas kernels, collect_column(): pl.pallas_call(functools.partial(column_kernel, depth), out_shape=jax.Sha...  40.9 us
    unnamed x121, local copies, waits for them, and re-layouts  40.9 us
  transfers between devices with their start and end apart: 1, of which 0 were waited for; matrix products, arithmetic and copies ran while one was open for 3% of the time, Pallas kernels for 24%

profile of v3, /device:TPU:0, one launch (start us, length us, event | category | flops | bytes accessed | tf_op | source)
XLA Modules:
  0.0 989.3 jit_solution(6945695060976977107)
XLA Ops:
  7.3 1.6 convert_bitcast_fusion
  10.6 100.5 %shard_map.161 = (bf16[8,128,2048]{2,1,0:T(8,128)(2,1)S(1)}, bf16[32,64,2048]{2,1,0:T(8,128)(2,1)S(1)}, bf16[4,8,64,768]{3,2,1,0:T(8,128)(2,1)S(1)}, bf16[4,8,64,128]{3,2,1,0:T(8,128)(2,1)S(1)}) custom-call(bf16[128,2048]{1,0:T(8,128)(2,1)S(1)} %copy-done.4, bf16[64,2048]{1,0:T(8,128)(2,1)S(1)} %convert_element_type.146.o_ref, ...), custom_call_target="tpu_custom_call" | custom-call | bytes 67108864 | tf_op jit(solution)/shard_map/pallas_call | solution.py:725
  111.2 3.2 copy-done
  114.4 2.0 copy-done.1
  116.4 1.7 copy-done.15
  118.5 3.2 multiply_reduce_fusion.1
  122.0 1.0 multiply_convert_fusion.1
  123.0 0.9 copy-done.16
  123.9 3.6 fusion.55
  127.7 1.5 copy-done.20
  129.3 5.8 shard_map.162
  136.9 1.0 fusion.22
  137.9 2.1 slice.172
  140.2 1.9 fusion.38
  142.1 1.9 fusion.34
  144.6 6.5 fusion.54
  151.2 4.1 fusion.15
  155.8 12.9 %shard_map.163 = bf16[8,128,256]{2,1,0:T(8,128)(2,1)S(1)} custom-call(bf16[8,128,256]{2,1,0:T(8,128)(2,1)S(1)} %copy.129.x_ref), custom_call_target="tpu_custom_call" | custom-call | bytes 8388608 | tf_op jit(solution)/shard_map/pallas_call | solution.py:769
  169.4 4.0 copy-done.5
  173.4 2.2 copy-done.6
  175.6 7.8 shard_map.164
  183.4 1.9 copy-done.8
  185.4 1.4 copy-done.11
  186.8 5.0 multiply_reduce_fusion.6
  192.7 215.3 %shard_map.165 = (bf16[32,128,2048]{2,1,0:T(8,128)(2,1)S(1)}, f32[32,16,128]{2,1,0:T(8,128)S(1)}, bf16[8,256,1024]{2,1,0:T(8,128)(2,1)S(1)}, bf16[8,256,512]{2,1,0:T(8,128)(2,1)S(1)}) custom-call(bf16[128,2048]{1,0:T(8,128)(2,1)S(1)} %multiply_convert_fusion.5.refs_0_, f32[16,128]{1,0:T(8,128)S(1)} %fusion.45.refs_1_, bf16[8,256,1024]{2,1,0:T(8,128)(2,1)S(1)} %copy-done.9, ...), custom_call_target="tpu_custom_call" | custom-call | bytes 136314880 | tf_op jit(solution)/shard_map/pallas_call | solution.py:272
  407.9 5.7 copy-done.13
  413.7 2.0 copy-done.14
  415.7 1.4 copy-done.18
  417.9 3.0 fusion.2
  420.9 98.2 %shard_map.166 = (bf16[32,128,2048]{2,1,0:T(8,128)(2,1)}, bf16[32,128,2048]{2,1,0:T(8,128)(2,1)}, f32[32,16,128]{2,1,0:T(8,128)}, bf16[2048,1024]{1,0:T(8,128)(2,1)}, bf16[2048,512]{1,0:T(8,128)(2,1)}) custom-call(bf16[32,128,2048]{2,1,0:T(8,128)(2,1)} %copy-done.13, bf16[32,128,2048]{2,1,0:T(8,128)(2,1)} %bitcast.262, f32[32,16,128]{2,1,0:T(8,128)} %copy-done.19, ...), custom_call_target="tpu_custom_call" | custom-call | flops 77309411328 | bytes 67108864 | tf_op jit(solution)/shard_map/pallas_call | solution.py:993
  519.2 1.7 copy.145
  520.9 133.4 %shard_map.167 = (f32[128,2048]{1,0:T(8,128)}, f32[16,128]{1,0:T(8,128)}, bf16[8,256,1024]{2,1,0:T(8,128)(2,1)}) custom-call(bf16[32,128,2048]{2,1,0:T(8,128)(2,1)} %get-tuple-element.42.refs_0_, f32[2,4,4,16,128]{4,3,2,1,0:T(8,128)} %bitcast.227, bf16[8,256,1024]{2,1,0:T(8,128)(2,1)} %bitcast.218), custom_call_target="tpu_custom_call" | custom-call | bytes 339738624 | tf_op jit(solution)/shard_map/pallas_call | solution.py:570
  655.7 1.8 multiply_reduce_fusion.2
  658.0 1.0 copy-done.22
  658.9 6.3 convolution_convert_fusion.3
  665.6 1.2 copy.144
  666.8 1.4 reshape.339.x_ref
  668.2 23.0 %shard_map.168 = bf16[8,128,256]{2,1,0:T(8,128)(2,1)S(1)} custom-call(bf16[8,128,256]{2,1,0:T(8,128)(2,1)S(1)} %reshape.339.x_ref), custom_call_target="tpu_custom_call" | custom-call | bytes 8388608 | tf_op jit(solution)/shard_map/pallas_call | solution.py:769
  691.8 5.0 multiply_reduce_fusion
  696.8 4.9 multiply_convert_fusion
  701.8 0.8 convolution_multiply_fusion.2
  702.8 1.5 convolution_multiply_fusion.1
  704.4 2.3 fusion.18
  707.0 5.8 convolution_convert_fusion
  713.4 1.2 copy-done.21
  715.7 7.6 shard_map.169
  723.3 2.4 multiply_convert_fusion.3
  726.1 4.9 convolution_convert_fusion.1
  731.1 4.9 convolution_convert_fusion.2
  736.0 40.9 %shard_map.170 = f32[128,2048]{1,0:T(8,128)S(1)} custom-call(bf16[8,128,2048]{2,1,0:T(8,128)(2,1)S(1)} %bitcast.198), custom_call_target="tpu_custom_call" | custom-call | bytes 67108864 | tf_op jit(solution)/shard_map/pallas_call | solution.py:826
  777.6 1.3 copy.131
  779.0 1.3 pad.9.clone
  780.3 1.1 copy.142
  781.3 175.1 %shard_map.171 = (f32[128,2048]{1,0:T(8,128)}, f32[64,2048]{1,0:T(8,128)}, f32[64,128]{1,0:T(8,128)}, f32[3,64,2048]{2,1,0:T(8,128)}, bf16[8,256,512]{2,1,0:T(8,128)(2,1)}) custom-call(bf16[32,128,2048]{2,1,0:T(8,128)(2,1)} %get-tuple-element.41.refs_0_, bf16[32,64,2048]{2,1,0:T(8,128)(2,1)} %bitcast.203, f32[2,4,4,64,128]{4,3,2,1,0:T(8,128)} %bitcast.212, ...), custom_call_target="tpu_custom_call" | custom-call | bytes 503316480 | tf_op jit(solution)/shard_map/pallas_call | solution.py:570
  956.4 0.8 slice.102
  957.3 0.8 slice_bitcast_fusion
  958.0 1.6 copy-done.10
  959.6 5.7 shard_map.173
  965.3 1.3 fusion.26
  966.6 1.1 multiply_add_fusion
  969.1 2.2 copy-done.7
  971.3 9.0 shard_map.172
  980.3 1.1 copy.156
  981.4 0.8 copy.157
  (172 shorter events, 13.8 us)
Async XLA Ops:
  7.2 3.2 copy-start.39
  7.2 3.3 copy-start.50
  7.2 3.3 copy-start.52
  7.2 3.4 copy-start.4
  7.2 413.7 %all-gather.2.cloned.1.call-start = ((), (), s32[]{:S(2)}) async-start(), calls=%async_computation | async-start | bytes 17301504 | tf_op jit(solution)/shard_map/all_gather | solution.py:1151
  111.2 3.2 copy-start
  114.4 2.0 copy-start.1
  116.4 1.7 copy-start.15
  118.5 3.5 copy-start.2
  122.0 1.9 copy-start.16
  123.9 13.1 %copy-start.33 = (bf16[128,2048]{1,0:T(8,128)(2,1)S(1)}, bf16[128,2048]{1,0:T(8,128)(2,1)}, u32[]{:S(2)}) copy-start(bf16[128,2048]{1,0:T(8,128)(2,1)} %param.11) | copy-start | bytes 1572868
  127.5 1.7 copy-start.20
  140.1 4.3 copy-start.46
  140.1 4.3 copy-start.48
  140.1 4.3 copy-start.42
  140.2 4.3 copy-start.44
  142.1 2.4 copy-start.31
  144.5 6.6 copy-start.28
  144.6 6.6 copy-start.34
  144.6 6.6 copy-start.40
  169.4 17.4 %copy-start.25 = (bf16[4,2,128,2,128]{2,4,0,3,1:T(8,128)(2,1)}, bf16[4,2,128,2,128]{2,4,0,3,1:T(8,128)(2,1)S(1)}, u32[]{:S(2)}) copy-start(bf16[4,2,128,2,128]{2,4,0,3,1:T(8,128)(2,1)S(1)} %copy.105) | copy-start | bytes 1572868
  169.4 4.0 copy-start.5
  173.4 2.2 copy-start.6
  175.6 11.1 %copy-start.51 = (s32[128,8]{0,1:T(8,128)S(1)}, s32[128,8]{0,1:T(8,128)}, u32[]{:S(2)}) copy-start(s32[128,8]{0,1:T(8,128)} %param.13) | copy-start | bytes 12292
  183.4 2.0 copy-start.8
  185.4 1.4 copy-start.11
  186.8 5.9 copy-start.9
  186.8 5.9 copy-start.12
  192.0 225.9 %copy-start.3 = (bf16[8,128,2048]{2,1,0:T(8,128)(2,1)S(1)}, bf16[8,128,2048]{2,1,0:T(8,128)(2,1)}, u32[]{:S(2)}) copy-start(bf16[8,128,2048]{2,1,0:T(8,128)(2,1)} %copy-done.1) | copy-start | bytes 12582916
  407.9 5.7 copy-start.13
  413.7 2.0 copy-start.14
  415.7 1.4 copy-start.18
  417.0 0.7 copy-start.19
  658.0 1.0 copy-start.22
  691.8 12.6 %slice-start = ((s8[8388608]{0:T(1024)(128)(4,1)}), s8[4194304]{0:T(1024)(128)(4,1)S(1)}, s32[]{:S(2)}) async-start(s8[8388608]{0:T(1024)(128)(4,1)} %bitcast.208), calls=%async_computation.1 | async-start | bytes 8388608
  696.8 5.0 copy-start.29
  696.8 7.5 slice-start.1
  701.8 1.0 copy-start.35
  704.4 2.5 copy-start.23
  704.4 2.5 copy-start.26
  706.9 5.8 copy-start.32
  706.9 5.8 copy-start.38
  712.8 1.9 copy-start.21
  712.8 1.9 copy-start.43
  712.8 1.9 copy-start.45
  712.8 1.9 copy-start.47
  712.8 1.9 copy-start.49
  714.7 1.0 copy-start.27
  723.3 2.8 copy-start.17
  726.1 4.9 copy-start.30
  726.1 4.9 copy-start.53
  781.3 184.0 %copy-start.24 = (f32[128,2048]{1,0:T(8,128)S(1)}, f32[128,2048]{1,0:T(8,128)}, u32[]{:S(2)}) copy-start(f32[128,2048]{1,0:T(8,128)} %copy-done.22) | copy-start | bytes 3145732
  958.0 1.6 copy-start.10
  959.6 7.0 copy-start.37
  969.1 2.2 copy-start.7
  971.3 9.0 copy-start.36
  971.3 10.1 %copy-start.41 = (f32[64,2048]{1,0:T(8,128)S(1)}, f32[64,2048]{1,0:T(8,128)}, u32[]{:S(2)}) copy-start(f32[64,2048]{1,0:T(8,128)} %get-tuple-element.149) | copy-start | bytes 1572868
Sparse Core Ops, SparseCore 0:
  138.1 191.1 all-gather.1

commit v4 on v3

--- a/solution.py
+++ b/solution.py
@@ -276,7 +276,7 @@
         out_specs=in_hbm(count),
         scratch_shapes=sems,
         compiler_params=pltpu.CompilerParams(
-            collective_id=ident, has_side_effects=True, vmem_limit_bytes=16 << 20
+            collective_id=ident, has_side_effects=True, vmem_limit_bytes=60 << 20
         ),
         cost_estimate=pl.CostEstimate(
             flops=0,
@@ -301,14 +301,16 @@
     lax.fori_loop(0, rows // tile, body, 0)
 
 
-def collect_kernel(depth, counts, *refs):
+def collect_kernel(depth, local, counts, *refs):
     rest = iter(refs)
 
     def take(count):
         return [next(rest) for _ in range(count)]
 
     mains, smalls, shareds, extras = (take(count) for count in counts)
+    halves = take(2 if local else 0)
     main_totals, small_totals, shared_totals, extra_outs = (take(count) for count in counts)
+    unpacked = take(1 if local else 0)
     main_buffers = [take(5) for _ in mains]
     small_buffers = [take(5) for _ in smalls]
     shared_buffers = [take(3) for _ in shareds]
@@ -350,12 +352,11 @@
             mains[n].at[block(group, k, at.c)], main_buffers[n][0].at[slot], main_sems[n][8].at[slot]
         )
 
-    def main_cross(group, k):
+    def main_cross(n, group, k):
         slot = group * depth + k
-        for n, (part, buffers, sems) in enumerate(zip(mains, main_buffers, main_sems)):
-            source = part.at[block(group, k, 1 - at.c)]
-            push(remote(source, buffers[1].at[slot], sems[0:2], slot, at.core()))
-            main_load(n, group, k).start()
+        source = mains[n].at[block(group, k, 1 - at.c)]
+        push(remote(source, main_buffers[n][1].at[slot], main_sems[n][0:2], slot, at.core()))
+        main_load(n, group, k).start()
 
     def main_sum(n, group, k, more):
         mine, crossed = main_buffers[n][:2]
@@ -369,26 +370,26 @@
             sum_rows(main_totals[n], (), terms)
         return mine.at[slot]
 
-    def main_far(k):
-        for n, (buffers, sems) in enumerate(zip(main_buffers, main_sems)):
-            for group in range(2):
-                slot = group * depth + k
-                total = main_sum(n, group, k, [])
-                push(remote(total, buffers[2].at[slot], sems[2:4], slot, at.far()))
-
-    def main_near(k):
-        for n, (buffers, sems) in enumerate(zip(main_buffers, main_sems)):
-            arrive(buffers[2], sems[2:4], k)
-            total = main_sum(n, 2, k, [(buffers[2], (k,))])
-            push(remote(total, buffers[3].at[k], sems[4:6], k, at.near()))
-
-    def main_own(k):
-        for n, (buffers, sems) in enumerate(zip(main_buffers, main_sems)):
-            arrive(buffers[2], sems[2:4], depth + k)
-            arrive(buffers[3], sems[4:6], k)
-            total = main_sum(n, 3, k, [(buffers[2], (depth + k,)), (buffers[3], (k,))])
-            if k < depth - 1:
-                push(remote(total, buffers[4].at[k], sems[6:8], k, at.chip(1 + k)))
+    def main_far(n, k):
+        buffers, sems = main_buffers[n], main_sems[n]
+        for group in range(2):
+            slot = group * depth + k
+            total = main_sum(n, group, k, [])
+            push(remote(total, buffers[2].at[slot], sems[2:4], slot, at.far()))
+
+    def main_near(n, k):
+        buffers, sems = main_buffers[n], main_sems[n]
+        arrive(buffers[2], sems[2:4], k)
+        total = main_sum(n, 2, k, [(buffers[2], (k,))])
+        push(remote(total, buffers[3].at[k], sems[4:6], k, at.near()))
+
+    def main_own(n, k):
+        buffers, sems = main_buffers[n], main_sems[n]
+        arrive(buffers[2], sems[2:4], depth + k)
+        arrive(buffers[3], sems[4:6], k)
+        total = main_sum(n, 3, k, [(buffers[2], (depth + k,)), (buffers[3], (k,))])
+        if k < depth - 1:
+            push(remote(total, buffers[4].at[k], sems[6:8], k, at.chip(1 + k)))
 
     def small_load(n, group):
         return pltpu.make_async_copy(
@@ -476,28 +477,37 @@
             extras[n].at[own_rank], extra_outs[n].at[own_rank], extra_sems[n][2]
         )
 
-    order = [(main_far, k) for k in range(2)] + [(main_near, 0)]
+    last = len(mains) - 1
+    stages = [(main_far, 0), (main_far, 1), (main_near, 0), (main_own, 0)]
     for k in range(2, depth):
-        order += [(main_far, k), (main_near, k - 1), (main_own, k - 2)]
-    order += [(main_near, depth - 1), (main_own, depth - 2), (main_own, depth - 1)]
+        stages += [(main_far, k), (main_near, k - 1), (main_own, k - 1)]
+    stages += [(main_near, depth - 1), (main_own, depth - 1)]
+    order = [(stage, n, k) for n in range(len(mains)) for stage, k in stages]
+    for n in range(last):
+        ahead = [(main_far, n + 1, k) for k in range(2)]
+        order = [step for step in order if step not in ahead]
+        at_end = order.index((main_near, n, depth - 1))
+        order[at_end:at_end] = ahead
     groups = {main_far: (0, 1), main_near: (2,), main_own: (3,)}
     shared_far()
     small_cross()
-    for stage, k in order:
+    for stage, n, k in order:
         for group in groups[stage]:
-            main_cross(group, k)
+            main_cross(n, group, k)
     for n in range(len(extras)):
         for slot, there in enumerate(peers):
             source = extras[n].at[there[2] * 2 + there[3]]
             push(remote(source, extra_outs[n].at[own_rank], extra_sems[n][:2], slot, there))
         extra_kept(n).start()
     small_far()
-    for stage, k in order:
-        stage(k)
-        if (stage, k) == (main_near, 0):
+    for stage, n, k in order:
+        stage(n, k)
+        if (stage, n, k) == (main_far, last, depth - 1) and local:
+            unpack_inside(local, *halves, *unpacked)
+        if (stage, n, k) == (main_near, 0, 0):
             shared_near()
             small_near()
-        if (stage, k) == (main_own, 0):
+        if (stage, n, k) == (main_own, 0, 0):
             shared_own()
             small_own()
     for n, (buffers, sems) in enumerate(zip(small_buffers, small_sems)):
@@ -535,7 +545,8 @@
         copy.wait_send()
 
 
-def collect(depth, ident, mains, smalls, shareds=(), extras=()):
+def collect(depth, ident, mains, smalls, shareds=(), extras=(), to_unpack=(0,)):
+    local, *halves = to_unpack
     dma = pltpu.SemaphoreType.DMA
     peers = 2 * depth - 1
 
@@ -566,25 +577,30 @@
         shapes.append(jax.ShapeDtypeStruct(a.shape, a.dtype))
     arrays = [*mains, *smalls, *shareds, *extras]
     counts = (len(mains), len(smalls), len(shareds), len(extras))
+    if halves:
+        lines = halves[0].size // 64
+        shapes.append(jax.ShapeDtypeStruct((lines, 128), high_type))
     in_vmem = [pl.BlockSpec(memory_space=pltpu.VMEM)] * (len(arrays) - len(extras))
     return pl.pallas_call(
-        functools.partial(collect_kernel, depth, counts),
+        functools.partial(collect_kernel, depth, local, counts),
         out_shape=shapes,
-        in_specs=in_hbm(len(arrays)),
-        out_specs=in_vmem + in_hbm(len(extras)),
+        in_specs=in_hbm(len(arrays) + len(halves)),
+        out_specs=in_vmem + in_hbm(len(extras) + len(halves) // 2),
         scratch_shapes=buffers + sems,
         compiler_params=pltpu.CompilerParams(
-            collective_id=ident, has_side_effects=True, vmem_limit_bytes=56 << 20
+            collective_id=ident, has_side_effects=True, vmem_limit_bytes=60 << 20
         ),
         cost_estimate=pl.CostEstimate(
             flops=0,
             bytes_accessed=sum(16 * a.size * a.dtype.itemsize for a in arrays),
             transcendentals=0,
         ),
-    )(*arrays)
-
-
-def gather_kernel(depth, x_ref, o_ref, w_ref, s_ref, x_out, o_out, w_out, s_out, *sems):
+    )(*arrays, *halves)
+
+
+def gather_kernel(depth, local_experts, x_ref, o_ref, w_ref, s_ref, in_ref, down_ref, *refs):
+    x_out, o_out, w_out, s_out = refs[:4]
+    packed, sems = refs[4:8], refs[8:]
     at = Place(depth)
     ranks = [(k, core) for k in range(depth) for core in range(2) if k or core]
     peers = [at.chip(k, lax.rem(at.c + core, 2)) for k, core in ranks]
@@ -654,6 +670,16 @@
     far_y, far_x = at.far_of(at.c)
     beside, across = near_y * 2 + near_x, far_y * 2 + far_x
     sides = ((s_out, s_side), (w_out, w_side))
+    pack(2 * depth, local_experts, in_ref, down_ref, *packed)
+    for slot, (j, core) in enumerate(ranks):
+        source = at.along(depth - j) * 2 + lax.rem(at.c + core, 2)
+        arrive(s_out.at[column, source], s_sems, slot)
+        arrive(w_out.at[column, source], w_sems, slot)
+    for copy in local:
+        copy.wait()
+    for target, pair_of in sides:
+        push(remote(target.at[column], target.at[column], pair_of, 0, at.near()))
+        push(remote(target.at[column], target.at[column], pair_of, 1, at.far()))
     for k in range(1, depth):
         arrive(o_place(k), o_z, at.next_z(k))
 
@@ -671,16 +697,6 @@
             forward(x_place(k), x_place(k), x_z, k).start()
 
         push(remote(x_place(k), x_place(k), x_core, k, at.core()))
-        if k == 1:
-            for slot, (j, core) in enumerate(ranks):
-                source = at.along(depth - j) * 2 + lax.rem(at.c + core, 2)
-                arrive(s_out.at[column, source], s_sems, slot)
-                arrive(w_out.at[column, source], w_sems, slot)
-            for copy in local:
-                copy.wait()
-            for target, pair_of in sides:
-                push(remote(target.at[column], target.at[column], pair_of, 0, at.near()))
-                push(remote(target.at[column], target.at[column], pair_of, 1, at.far()))
     for target, pair_of in sides:
         arrive(target.at[beside], pair_of, 0)
         push(remote(target.at[beside], target.at[beside], pair_of, 2, at.far()))
@@ -717,29 +733,32 @@
         copy.wait_send()
 
 
-def gather(depth, ident, x, o, w, s):
+def gather(depth, ident, x, o, w, s, expert_in, expert_down):
+    chunk, local = expert_in.shape[:2]
     ranks = 2 * depth
     sems = pair(depth + 1) + pair(depth) + pair(depth + 1) + pair(depth) + pair(2 * depth)
     sems += pair(4 * depth) + pair(ranks - 1) * 2 + pair(3) * 2
     sems.append(pltpu.SemaphoreType.DMA((4,)))
     return pl.pallas_call(
-        functools.partial(gather_kernel, depth),
+        functools.partial(gather_kernel, depth, local),
         out_shape=[
             jax.ShapeDtypeStruct((ranks,) + x.shape, x.dtype),
             jax.ShapeDtypeStruct((4 * ranks,) + o.shape, o.dtype),
             jax.ShapeDtypeStruct((4,) + w.shape, w.dtype),
             jax.ShapeDtypeStruct((4, ranks) + s.shape, s.dtype),
-        ],
-        in_specs=in_hbm(4),
-        out_specs=in_hbm(4),
+        ]
+        + [jax.ShapeDtypeStruct((ranks, chunk, local * 128), low_type)] * 2
+        + [jax.ShapeDtypeStruct((ranks, chunk, local * 64), low_type)] * 2,
+        in_specs=in_hbm(6),
+        out_specs=in_hbm(8),
         scratch_shapes=sems,
         compiler_params=pltpu.CompilerParams(
-            collective_id=ident, has_side_effects=True, vmem_limit_bytes=16 << 20
+            collective_id=ident, has_side_effects=True, vmem_limit_bytes=60 << 20
         ),
         cost_estimate=pl.CostEstimate(
             flops=0, bytes_accessed=64 * depth * x.size, transcendentals=0
         ),
-    )(x, o, w, s)
+    )(x, o, w, s, lines_in(expert_in), lines_down(expert_down))
 
 
 def exchange_kernel(depth, same, x_ref, out_ref, send_sems, recv_sems, local_sem):
@@ -781,44 +800,79 @@
     )(x)
 
 
-def column_kernel(depth, part, total, mine, crossed, z_in, z_out, *sems):
+def column_kernel(depth, part, total, mine, crossed, z_in, *sems):
     at = Place(depth)
     meet([at.core()] + [at.chip(k) for k in range(1, depth)])
     started = []
-
-    def push(copy):
-        copy.start()
-        started.append(copy)
+    inner = lax.rem(at.z, depth - 1) != 0
+    inside = lax.div(lax.rem(at.z, depth - 1) + 1, 2)
+    onto = (None, at.next_z(1), at.z + 1 - 2 * lax.div(at.z, 3), 1 + lax.rem(at.z, 2))
+    slots = (
+        None,
+        5 - lax.div(4 - at.z, 4),
+        4 * inside + (1 - inside) * at.next_z(2),
+        at.next_z(3),
+    )
 
     def local(k):
-        return pltpu.make_async_copy(
-            part.at[at.along(1 + k) * 2 + at.c], mine.at[k], sems[4].at[k]
+        return pltpu.make_async_copy(part.at[at.next_z(k) * 2 + at.c], mine.at[k], sems[4].at[k])
+
+    def cross(k):
+        source = part.at[at.next_z(k) * 2 + 1 - at.c]
+        return remote(source, crossed.at[k], sems[0:2], k, at.core())
+
+    def arrive(slot):
+        remote(z_in.at[slot], z_in.at[slot], sems[2:4], slot, at.core()).wait_recv()
+
+    def hand_on(k):
+        return pltpu.make_async_remote_copy(
+            src_ref=mine.at[k],
+            dst_ref=z_in.at[slots[k]],
+            send_sem=sems[2].at[k],
+            recv_sem=sems[3].at[slots[k]],
+            device_id=(at.y, at.x, onto[k], at.c),
+            device_id_type=MESH_ID,
         )
 
-    def arrive(buffer, pair_of, slot):
-        remote(buffer.at[slot], buffer.at[slot], pair_of, slot, at.core()).wait_recv()
-
-    for k in range(depth):
-        push(
-            remote(
-                part.at[at.along(1 + k) * 2 + 1 - at.c], crossed.at[k], sems[0:2], k, at.core()
-            )
-        )
+    order = tuple(range(depth - 1, -1, -1))
+    for k in order:
+        cross(k).start()
         local(k).start()
-    for k in range(depth):
+    for k in order:
         local(k).wait()
-        arrive(crossed, sems[0:2], k)
+        cross(k).wait_recv()
         terms = [(mine, (k,)), (crossed, (k,))]
-        if k < depth - 1:
-            sum_rows(z_out, (k,), terms)
-            push(remote(z_out.at[k], z_in.at[k], sems[2:4], k, at.chip(1 + k)))
-        else:
+        if k == 0:
             sum_rows(total, (), terms)
-    for k in range(depth - 1):
-        arrive(z_in, sems[2:4], k)
-    sum_rows(total, (), [(total, ())] + [(z_in, (k,)) for k in range(depth - 1)])
-    for copy in started:
-        copy.wait_send()
+            continue
+
+        @pl.when(inner)
+        def _(terms=terms, k=k):
+            arrive(at.next_z(k))
+            sum_rows(mine, (k,), terms + [(z_in, (at.next_z(k),))])
+
+        @pl.when(lax.rem(at.z, depth - 1) == 0)
+        def _(terms=terms, k=k):
+            sum_rows(mine, (k,), terms)
+
+        hand_on(k).start()
+
+    @pl.when(inner)
+    def _():
+        arrive(4)
+        arrive(5)
+        sum_rows(total, (), [(total, ()), (z_in, (4,)), (z_in, (5,))])
+
+    @pl.when(lax.rem(at.z, depth - 1) == 0)
+    def _():
+        slot = 5 - lax.div(at.z, 3)
+        arrive(slot)
+        sum_rows(total, (), [(total, ()), (z_in, (slot,))])
+
+    for k in order:
+        cross(k).wait_send()
+        if k:
+            hand_on(k).wait_send()
 
 
 def collect_column(depth, ident, part):
@@ -828,10 +882,9 @@
         out_shape=jax.ShapeDtypeStruct(block, high_type),
         in_specs=in_hbm(1),
         out_specs=pl.BlockSpec(memory_space=pltpu.VMEM),
-        scratch_shapes=[pltpu.VMEM((depth,) + block, part.dtype)] * 2
-        + [pltpu.VMEM((depth - 1,) + block, part.dtype)] * 2
+        scratch_shapes=[pltpu.VMEM((slots,) + block, part.dtype) for slots in (depth, depth, 6)]
         + pair(depth)
-        + pair(depth - 1)
+        + pair(6)
         + [pltpu.SemaphoreType.DMA((depth,))],
         compiler_params=pltpu.CompilerParams(
             collective_id=ident, has_side_effects=True, vmem_limit_bytes=32 << 20
@@ -853,83 +906,124 @@
     return values.reshape(rows, local, hidden // 128, 128).transpose(0, 2, 1, 3).reshape(-1, 128)
 
 
-def places(ranks, local):
+def lines_of(ranks, local):
+    half, of_in, of_down = local // 2, [], []
     for rank in range(ranks):
         for x in range(local):
             for k in range(2):
-                yield rank, (k * local + x) * 128, (x * ranks + rank) * 2 + k, None
-            yield rank, x * 128, None, rank * local + x
-
-
-def pack_kernel(ranks, local, step, in_ref, down_ref, in_out, down_out):
-    for rank, column, of_in, of_down in places(ranks, local):
-        if of_down is None:
-            value = in_ref[pl.ds(of_in, step, stride=2 * local * ranks), :]
-            in_out[rank, :, column : column + 128] = value.astype(low_type)
-        else:
-            value = down_ref[pl.ds(of_down, step, stride=local * ranks), :]
-            down_out[rank, :, column : column + 128] = value.astype(low_type)
-
-
-def pack(ranks, expert_in, expert_down):
-    rows, local = expert_in.shape[:2]
+                line = (x * ranks + rank) * 2 + k
+                columns = (k * half + x % half) * 128
+                of_in.append((rank, x // half, columns, line, 2 * local * ranks))
+            of_down.append((rank, x // half, x % half * 128, rank * local + x, local * ranks))
+    return of_in, of_down
+
+
+def pack_kernel(ranks, local, step, in_ref, down_ref, *outs):
+    of_in, of_down = lines_of(ranks, local)
+    for lines, ref, targets in ((of_in, in_ref, outs[:2]), (of_down, down_ref, outs[2:])):
+        for rank, half, column, line, stride in lines:
+            value = ref[pl.ds(line, step, stride=stride), :]
+            targets[half][rank, :, column : column + 128] = value.astype(low_type)
+
+
+def pack(ranks, local, in_ref, down_ref, *outs):
     step = 32
     lines = step * local * ranks
-    span = local * 128
-    return pl.pallas_call(
+
+    def slices(span):
+        return pl.BlockSpec((ranks, step, span), lambda i: (0, i, 0))
+
+    pltpu.emit_pipeline(
         functools.partial(pack_kernel, ranks, local, step),
-        grid=(rows // step,),
+        grid=(outs[0].shape[1] // step,),
         in_specs=[
             pl.BlockSpec((2 * lines, 128), lambda i: (i, 0)),
             pl.BlockSpec((lines, 128), lambda i: (i, 0)),
         ],
-        out_specs=[
-            pl.BlockSpec((ranks, step, 2 * span), lambda i: (0, i, 0)),
-            pl.BlockSpec((ranks, step, span), lambda i: (0, i, 0)),
-        ],
-        out_shape=[
-            jax.ShapeDtypeStruct((ranks, rows, 2 * span), low_type),
-            jax.ShapeDtypeStruct((ranks, rows, span), low_type),
-        ],
-        compiler_params=pltpu.CompilerParams(vmem_limit_bytes=32 << 20),
-    )(lines_in(expert_in), lines_down(expert_down))
-
-
-def unpack_kernel(ranks, local, step, in_ref, out_ref):
-    for rank, column, of_in, of_down in places(ranks, local):
-        down = in_ref.shape[2] == local * 128
-        if down == (of_in is None):
-            first = of_down if down else of_in
-            stride = (1 if down else 2) * local * ranks
-            value = in_ref[rank, :, column : column + 128].astype(high_type)
-            out_ref[pl.ds(first, step, stride=stride), :] = value
-
-
-def unpack(local, sliced):
-    ranks, rows, span = sliced.shape
+        out_specs=[slices(out.shape[2]) for out in outs],
+    )(in_ref, down_ref, *outs)
+
+
+def unpack_kernel(ranks, local, step, first_ref, second_ref, out_ref):
+    of_in, of_down = lines_of(ranks, local)
+    for rank, half, column, line, stride in (
+        of_in if first_ref.shape[2] == local * 128 else of_down
+    ):
+        value = (first_ref, second_ref)[half][rank, :, column : column + 128]
+        out_ref[pl.ds(line, step, stride=stride), :] = value.astype(high_type)
+
+
+def unpack_inside(local, first_ref, second_ref, out_ref):
+    ranks, rows, span = first_ref.shape
     step = 32
-    lines = step * ranks * span // 128
+    pltpu.emit_pipeline(
+        functools.partial(unpack_kernel, ranks, local, step),
+        grid=(rows // step,),
+        in_specs=[pl.BlockSpec((ranks, step, span), lambda i: (0, i, 0))] * 2,
+        out_specs=[pl.BlockSpec((step * ranks * span // 64, 128), lambda i: (i, 0))],
+    )(first_ref, second_ref, out_ref)
+
+
+def unpack(local, *halves):
+    ranks, rows, span = halves[0].shape
+    step = 32
+    lines = step * ranks * span // 64
     return pl.pallas_call(
         functools.partial(unpack_kernel, ranks, local, step),
         grid=(rows // step,),
-        in_specs=[pl.BlockSpec((ranks, step, span), lambda i: (0, i, 0))],
+        in_specs=[pl.BlockSpec((ranks, step, span), lambda i: (0, i, 0))] * 2,
         out_specs=pl.BlockSpec((lines, 128), lambda i: (i, 0)),
-        out_shape=jax.ShapeDtypeStruct((rows * ranks * span // 128, 128), high_type),
+        out_shape=jax.ShapeDtypeStruct((rows * ranks * span // 64, 128), high_type),
         compiler_params=pltpu.CompilerParams(vmem_limit_bytes=32 << 20),
-    )(sliced)
-
-
-def experts_kernel(
-    local, tokens_ref, grads_ref, gates_ref, in_ref, down_ref, *outputs
-):
-    back_ref, mixed_ref, sums_ref, grad_in_ref, grad_down_ref, in_total, down_total = outputs
+    )(*halves)
+
+
+def experts_kernel(first, depth, earlier, extra_count, *refs):
+    rest = iter(refs)
+
+    def take(count):
+        return [next(rest) for _ in range(count)]
+
+    tokens_ref, grads_ref, gates_ref, in_ref, down_ref = take(5)
+    added = take(3) if earlier else None
+    extra_refs = take(extra_count)
+    back_ref, mixed_ref, sums_ref, grad_in_ref, grad_down_ref = take(5)
+    extra_outs = take(extra_count)
+    in_total, down_total = take(2)
+    extra_sems = [take(3) for _ in extra_refs]
     column = lax.axis_index("ey") * 2 + lax.axis_index("ex")
-    step = pl.program_id(0)
+    step, steps = pl.program_id(0), pl.num_programs(0)
     blocks, experts, rows = gates_ref.shape
     span = down_ref.shape[1]
     width = tokens_ref.shape[2]
+    at = Place(depth)
+    ranks = [(k, core) for k in range(depth) for core in range(2) if k or core]
+    peers = [at.chip(k, lax.rem(at.c + core, 2)) for k, core in ranks]
+    own_rank = at.z * 2 + at.c
+
+    def extra_copies():
+        return [
+            remote(source.at[there[2] * 2 + there[3]], target.at[own_rank], sems, slot, there)
+            for source, target, sems in zip(extra_refs, extra_outs, extra_sems)
+            for slot, there in enumerate(peers)
+        ]
+
+    def kept():
+        return [
+            pltpu.make_async_copy(source.at[own_rank], target.at[own_rank], sems[2])
+            for source, target, sems in zip(extra_refs, extra_outs, extra_sems)
+        ]
+
+    @pl.when(step == 0)
+    def _():
+        meet(peers)
+        for copy in extra_copies() + kept():
+            copy.start()
+        in_total[...] = jnp.zeros_like(in_total)
+        down_total[...] = jnp.zeros_like(down_total)
+
     units_of = (
-        lax.broadcasted_iota(jnp.int32, (experts, span), 1) // 128 + column * local
+        lax.broadcasted_iota(jnp.int32, (experts, span), 1) // 128 + column * 4 + first
         == lax.broadcasted_iota(jnp.int32, (experts, span), 0)
     ).astype(low_type)
 
@@ -953,78 +1047,77 @@
     hidden = (silu * up_part).astype(low_type).astype(high_type)
     weighted = (wide * hidden).astype(low_type)
     inner = hidden * down_grad
-    high, rest = terms(inner, 2)
-    sums = dot_t(units_of, high) + dot_t(units_of, rest)
+    high, low = terms(inner, 2)
+    sums = dot_t(units_of, high) + dot_t(units_of, low)
     for b in range(blocks):
-        sums_ref[b] = sums[:, b * rows : (b + 1) * rows]
+        part = sums[:, b * rows : (b + 1) * rows]
+        sums_ref[b] = part + added[2][b] if earlier else part
     grad_hidden = wide * down_grad
     grad_gate = grad_hidden * up_part * (sigma + silu * (1.0 - sigma))
     grad_both = jnp.concatenate([grad_gate, grad_hidden * silu], axis=1).astype(low_type)
-    back_ref[...] = dot_t(grad_both, in_ref[...]).astype(low_type).reshape(back_ref.shape)
-    mixed_ref[...] = dot_t(weighted, down_ref[...]).astype(low_type).reshape(mixed_ref.shape)
-
-    @pl.when(step == 0)
-    def _():
-        in_total[...] = jnp.zeros_like(in_total)
-        down_total[...] = jnp.zeros_like(down_total)
-
+    back = dot_t(grad_both, in_ref[...]).reshape(back_ref.shape)
+    mixed = dot_t(weighted, down_ref[...]).reshape(mixed_ref.shape)
+    if earlier:
+        back = back + added[0][...].astype(high_type)
+        mixed = mixed + added[1][...].astype(high_type)
+    back_ref[...] = back.astype(low_type)
+    mixed_ref[...] = mixed.astype(low_type)
     in_total[...] += t_dot(tokens, grad_both)
     down_total[...] += t_dot(grads, weighted)
 
-    @pl.when(step == pl.num_programs(0) - 1)
+    @pl.when(step == steps - 1)
     def _():
         grad_in_ref[...] = in_total[...].astype(low_type)
         grad_down_ref[...] = down_total[...].astype(low_type)
-
-
-def run_experts(local, tokens, grads, gates, weights_in, weights_down):
+        for copy in kept() + extra_copies():
+            copy.wait()
+
+
+def run_experts(depth, ident, first, tokens, grads, gates, weights_in, weights_down, extras, earlier):
     devices, rows, width = tokens.shape
     experts = gates.shape[1]
     blocks = 4
-    span = weights_down.shape[1]
-    once = pl.Buffered(1)
+    span = weights_in.shape[1] // 2
 
     def by_step(shape):
         return pl.BlockSpec((blocks,) + shape, lambda i: (i, 0, 0))
 
     def whole(shape):
-        return pl.BlockSpec(shape, lambda i: (0, 0), pipeline_mode=once)
-
+        return pl.BlockSpec(shape, lambda i: (0, 0), pipeline_mode=pl.Buffered(1))
+
+    per_token = [by_step((rows, width)), by_step((rows, width)), by_step((experts, rows))]
+    sums = [jax.ShapeDtypeStruct((devices, rows, width), low_type)] * 2
+    sums.append(jax.ShapeDtypeStruct((devices, experts, rows), high_type))
     return pl.pallas_call(
-        functools.partial(experts_kernel, local),
+        functools.partial(experts_kernel, first, depth, bool(earlier), len(extras)),
         grid=(devices // blocks,),
-        in_specs=[
-            by_step((rows, width)),
-            by_step((rows, width)),
-            by_step((experts, rows)),
-            whole((width, 2 * span)),
-            whole((width, span)),
-        ],
-        out_specs=[
-            by_step((rows, width)),
-            by_step((rows, width)),
-            by_step((experts, rows)),
-            whole((width, 2 * span)),
-            whole((width, span)),
-        ],
-        out_shape=[
-            jax.ShapeDtypeStruct((devices, rows, width), low_type),
-            jax.ShapeDtypeStruct((devices, rows, width), low_type),
-            jax.ShapeDtypeStruct((devices, experts, rows), high_type),
+        in_specs=per_token
+        + [whole((width, 2 * span)), whole((width, span))]
+        + (per_token if earlier else [])
+        + in_hbm(len(extras)),
+        out_specs=per_token
+        + [whole((width, 2 * span)), whole((width, span))]
+        + in_hbm(len(extras)),
+        out_shape=sums
+        + [
             jax.ShapeDtypeStruct((width, 2 * span), low_type),
             jax.ShapeDtypeStruct((width, span), low_type),
-        ],
+        ]
+        + [jax.ShapeDtypeStruct(extra.shape, extra.dtype) for extra in extras],
         scratch_shapes=[
             pltpu.VMEM((width, 2 * span), high_type),
             pltpu.VMEM((width, span), high_type),
-        ],
-        compiler_params=pltpu.CompilerParams(vmem_limit_bytes=60 << 20),
+        ]
+        + (pair(2 * depth - 1) + [pltpu.SemaphoreType.DMA]) * len(extras),
+        compiler_params=pltpu.CompilerParams(
+            collective_id=ident, has_side_effects=True, vmem_limit_bytes=60 << 20
+        ),
         cost_estimate=pl.CostEstimate(
             flops=18 * devices * rows * width * span,
             bytes_accessed=8 * devices * rows * width,
             transcendentals=devices * rows * span,
         ),
-    )(tokens, grads, gates, weights_in, weights_down)
+    )(tokens, grads, gates, weights_in, weights_down, *earlier, *extras)
 
 
 def grid_shards(
@@ -1081,8 +1174,15 @@
     small = jnp.pad(small, ((0, 0), (0, 128 - small.shape[1])))
     packed = attn_qkv.astype(low_type).transpose(1, 0, 2)
     packed = by_rank(packed).reshape(ranks, weight_rows, 3 * own_width)
-    seq_input, out_weight, qkv_weight, small = gather(
-        depth, 0, residual_in, attn_out.astype(low_type), packed, small
+    seq_input, out_weight, qkv_weight, small, first_in, second_in, first_down, second_down = gather(
+        depth,
+        0,
+        residual_in,
+        attn_out.astype(low_type),
+        packed,
+        small,
+        expert_in,
+        expert_down,
     )
     out_weight = out_weight.reshape(width, width)
     qkv_weight = qkv_weight.reshape(width, 3 * own_width)
@@ -1095,8 +1195,6 @@
     ]
     normed_in = seq_input.reshape(seq_rows, width).astype(high_type)
     normed_in = (normed_in * rms_scale(normed_in) * gain_rows[0]).astype(low_type)
-    sliced_in, sliced_down = pack(ranks, expert_in, expert_down)
-
     raw = dot(normed_in, qkv_weight)
     query_raw, key_raw = raw[:, :own_width], raw[:, own_width : 2 * own_width]
     value_rows = raw[:, 2 * own_width :].astype(low_type)
@@ -1149,28 +1247,45 @@
     after = jnp.minimum(scales[0, 0], 0.0)
     own_grads = (grad_comb + after).astype(low_type)
     grads = lax.all_gather(own_grads, GRID, axis=0, tiled=True)
-    tokens, gates_all, weights_in, weights_down = spread(
-        depth, 3, (normed_mid, gates.T), (sliced_in, sliced_down)
-    )
-    back, mixed, gate_sums, grad_in, grad_down = run_experts(
-        local_experts,
+    tokens, gates_all, first_in, first_down = spread(
+        depth, 3, (normed_mid, gates.T), (first_in, first_down)
+    )
+    grads = grads.reshape(tokens.shape)
+
+    def flat(values):
+        return values.reshape(width, -1)
+
+    def by_slice(values):
+        return values.reshape(ranks, chunk_rows, -1)
+
+    *sums, grad_first, down_first, second_in, second_down = run_experts(
+        depth,
+        9,
+        0,
         tokens,
-        grads.reshape(tokens.shape),
+        grads,
         gates_all,
-        weights_in.reshape(width, -1),
-        weights_down.reshape(width, -1),
-    )
-    grad_mid_norm, grad_gates, sliced_in = collect(
+        flat(first_in),
+        flat(first_down),
+        (second_in, second_down),
+        (),
+    )
+    back, mixed, gate_sums, grad_second, down_second, grad_first, down_first = run_experts(
         depth,
-        4,
-        [back],
-        [gate_sums],
-        extras=[grad_in.reshape(ranks, chunk_rows, 2 * span)],
-    )
-    grad_expert_in = unpack(local_experts, sliced_in).reshape(
-        chunk_rows, local_experts, ranks, 2, part
-    )
-    grad_expert_in = grad_expert_in.transpose(0, 1, 3, 2, 4).reshape(expert_in.shape)
+        10,
+        local_experts // 2,
+        tokens,
+        grads,
+        gates_all,
+        flat(second_in),
+        flat(second_down),
+        (by_slice(grad_first), by_slice(down_first)),
+        tuple(sums),
+    )
+    grad_mid_norm, combined, grad_gates, grad_second = collect(
+        depth, 4, [back, mixed], [gate_sums], extras=[by_slice(grad_second)]
+    )
+    output = middle + live_rows * combined
 
     grad_gates = grad_gates.T
     grad_chosen = gates * (grad_gates - jnp.sum(gates * grad_gates, axis=1, keepdims=True))
@@ -1244,19 +1359,21 @@
     grad_small = jnp.pad(grad_small, ((0, 0), (0, 128 - grad_small.shape[1])))
     grad_out = t_dot(attended, grad_branch).astype(low_type)
     grad_qkv = t_dot(normed_in, grad_raw).astype(low_type)
-    combined, grad_out, grad_small, grad_qkv, sliced_down = collect(
+    grad_out, grad_small, grad_qkv, down_second, grad_expert_in = collect(
         depth,
         5,
-        [mixed, grad_out.reshape(-1, weight_rows, width)],
+        [grad_out.reshape(-1, weight_rows, width)],
         [grad_small.reshape(-1, weight_rows, 128)],
         [grad_qkv.reshape(columns, -1, 3 * own_width)],
-        [grad_down.reshape(ranks, chunk_rows, span)],
-    )
-    grad_expert_down = unpack(local_experts, sliced_down).reshape(
+        [by_slice(down_second)],
+        (local_experts, grad_first, grad_second),
+    )
+    grad_expert_in = grad_expert_in.reshape(chunk_rows, local_experts, ranks, 2, part)
+    grad_expert_in = grad_expert_in.transpose(0, 1, 3, 2, 4).reshape(expert_in.shape)
+    grad_expert_down = unpack(local_experts, down_first, down_second).reshape(
         chunk_rows, ranks, local_experts, part
     )
     grad_expert_down = grad_expert_down.transpose(0, 2, 1, 3).reshape(expert_down.shape)
-    output = middle + live_rows * combined
     return (
         output,
         grad_input,

time: 1000 us -> 890 us (0.89)
  Pallas kernels: 835 us -> 755 us
  local copies, waits for them, and re-layouts: 55.6 us -> 23.1 us
    pallas_call x1, Pallas kernels: 215 us -> 163 us  [spread(): pl.pallas_call(functools.partial(spread_kernel, depth, len(arrays), len(e...]
    unnamed x121 -> x98, local copies, waits for them, and re-layouts: 40.9 us -> 11 us
    pallas_call x5, Pallas kernels: 515 us -> 501 us  [the longest x2 245 us: collect(): pl.pallas_call(functools.partial(collect_kernel, depth, local, counts), o...]
  transfers between devices with their start and end apart: 1 -> 1, of which waited for: 0 -> 0; matrix products, arithmetic and copies ran while one was open for 3% -> 3% of each run, Pallas kernels for 24% -> 20%
where the time goes in v4:
time: 890 us; the launch traced here: 882 us
  Pallas kernels  755 us (85%)
  matrix products  52.8 us (6%)
  other arithmetic  33.6 us (4%)
  local copies, waits for them, and re-layouts  23.1 us (3%)
  between operations  16.8 us (2%)
    pallas_call x2, Pallas kernels, collect(): pl.pallas_call(functools.partial(collect_kernel, depth, local, counts), o...  245 us
    pallas_call x1, Pallas kernels, spread(): pl.pallas_call(functools.partial(spread_kernel, depth, len(arrays), len(e...  163 us
    pallas_call x2, Pallas kernels, run_experts(): pl.pallas_call(functools.partial(experts_kernel, first, depth, bool(earli...  155 us
    pallas_call x1, Pallas kernels, gather(): pl.pallas_call(functools.partial(gather_kernel, depth, local), out_shape=...  102 us
    pallas_call x1, Pallas kernels, collect_column(): pl.pallas_call(functools.partial(column_kernel, depth), out_shape=jax.Sha...  43.8 us
    pallas_call x4, Pallas kernels, exchange(): pl.pallas_call(functools.partial(exchange_kernel, depth, same), out_shape...  41.8 us
  transfers between devices with their start and end apart: 1, of which 0 were waited for; matrix products, arithmetic and copies ran while one was open for 3% of the time, Pallas kernels for 20%

profile of v4, /device:TPU:0, one launch (start us, length us, event | category | flops | bytes accessed | tf_op | source)
XLA Modules:
  0.0 881.5 jit_solution(4768324388378354994)
XLA Ops:
  7.2 1.6 convert_bitcast_fusion
  8.8 0.6 reshape.327
  9.4 0.6 copy.143
  10.0 1.2 reshape_reshape.12.w_ref
  11.2 0.7 convert_element_type.146.o_ref
  12.1 0.6 pad.8.s_ref
  12.7 101.7 %shard_map.161 = (bf16[8,128,2048]{2,1,0:T(8,128)(2,1)}, bf16[32,64,2048]{2,1,0:T(8,128)(2,1)}, bf16[4,8,64,768]{3,2,1,0:T(8,128)(2,1)}, bf16[4,8,64,128]{3,2,1,...) custom-call(bf16[128,2048]{1,0:T(8,128)(2,1)} %x_ref.1, ...), custom_call_target="tpu_custom_call" | custom-call | bytes 67108864 | tf_op jit(solution)/shard_map/pallas_call | solution.py:742
  114.4 1.1 slice_convert_fusion.1
  115.9 3.2 multiply_reduce_fusion.1
  119.3 1.0 multiply_convert_fusion.1
  120.3 0.9 copy-done.39
  121.2 3.6 fusion.55
  125.1 5.8 shard_map.162
  131.6 0.5 slice.118
  132.7 2.0 fusion.22
  134.8 0.9 slice.172
  135.8 2.0 fusion.38
  138.6 6.5 fusion.54
  145.2 4.1 fusion.15
  149.8 15.9 %shard_map.163 = bf16[8,128,256]{2,1,0:T(8,128)(2,1)S(1)} custom-call(bf16[8,128,256]{2,1,0:T(8,128)(2,1)S(1)} %copy.129.x_ref), custom_call_target="tpu_custom_call" | custom-call | bytes 8388608 | tf_op jit(solution)/shard_map/pallas_call | solution.py:788
  165.8 0.5 copy.107
  166.3 5.3 multiply_reduce_fusion.6
  171.8 0.6 select_reduce_fusion
  172.4 0.6 fusion.45.refs_1_
  173.1 162.8 %shard_map.164 = (bf16[32,128,2048]{2,1,0:T(8,128)(2,1)}, f32[32,16,128]{2,1,0:T(8,128)}, bf16[8,256,512]{2,1,0:T(8,128)(2,1)}, bf16[8,256,256]{2,1,0:T(8,128)(2,1)}) custom-call(bf16[128,2048]{1,0:T(8,128)(2,1)} %copy-done.10, f32[16,128]{1,0:T(8,128)} %fusion.45.refs_1_, bf16[8,256,512]{2,1,0:T(8,128)(2,1)} %get-tuple-element.47.refs_2_, ...), custom_call_target="tpu_custom_call" | custom-call | bytes 136314880 | tf_op jit(solution)/shard_map/pallas_call | solution.py:272
  336.1 5.2 fusion.2
  341.3 74.5 %shard_map.165 = (bf16[32,128,2048]{2,1,0:T(8,128)(2,1)}, bf16[32,128,2048]{2,1,0:T(8,128)(2,1)}, f32[32,16,128]{2,1,0:T(8,128)}, bf16[2048,512]{1,0:T(8,128)(2,...) custom-call(bf16[32,128,2048]{2,1,0:T(8,128)(2,1)} %get-tuple-element.49.refs_0_, ...), custom_call_target="tpu_custom_call" | custom-call | flops 38654705664 | bytes 67108864 | tf_op jit(solution)/shard_map/pallas_call | solution.py:1091
  415.8 80.1 %shard_map.166 = (bf16[32,128,2048]{2,1,0:T(8,128)(2,1)}, bf16[32,128,2048]{2,1,0:T(8,128)(2,1)}, f32[32,16,128]{2,1,0:T(8,128)}, bf16[2048,512]{1,0:T(8,128)(2,...) custom-call(bf16[32,128,2048]{2,1,0:T(8,128)(2,1)} %get-tuple-element.49.refs_0_, ...), custom_call_target="tpu_custom_call" | custom-call | flops 38654705664 | bytes 67108864 | tf_op jit(solution)/shard_map/pallas_call | solution.py:1091
  496.0 1.7 copy.145
  497.7 156.1 %shard_map.167 = (f32[128,2048]{1,0:T(8,128)}, f32[128,2048]{1,0:T(8,128)}, f32[16,128]{1,0:T(8,128)}, bf16[8,256,512]{2,1,0:T(8,128)(2,1)}) custom-call(bf16[32,128,2048]{2,1,0:T(8,128)(2,1)} %get-tuple-element.62.refs_0_, bf16[32,128,2048]{2,1,0:T(8,128)(2,1)} %get-tuple-element.63.refs_1_, f32[2,4,4,16,128]{4,3,2,1,0:T(8,128)} %bitcast.226, ...), custom_call_target="tpu_custom_call" | custom-call | bytes 574619648 | tf_op jit(solution)/shard_map/pallas_call | solution.py:584
  653.8 0.8 fusion.40
  654.6 0.7 fusion.42
  655.3 1.8 multiply_reduce_fusion.2
  657.1 1.5 convert_add_fusion
  658.6 6.7 convolution_convert_fusion.3
  665.7 0.4 copy.144
  666.4 12.2 %shard_map.168 = bf16[8,128,256]{2,1,0:T(8,128)(2,1)S(1)} custom-call(bf16[8,128,256]{2,1,0:T(8,128)(2,1)S(1)} %reshape.354.x_ref), custom_call_target="tpu_custom_call" | custom-call | bytes 8388608 | tf_op jit(solution)/shard_map/pallas_call | solution.py:788
  678.7 0.4 copy.114
  679.1 5.0 multiply_reduce_fusion
  684.2 5.0 multiply_convert_fusion
  689.2 1.5 convolution_multiply_fusion.1
  690.8 0.8 convolution_multiply_fusion.2
  691.6 2.3 fusion.18
  694.1 5.8 convolution_convert_fusion
  700.0 0.4 multiply_subtract_fusion.1
  700.6 1.6 copy-done.4
  702.2 0.7 fusion.30
  703.2 8.0 shard_map.169
  711.3 2.1 multiply_convert_fusion.3
  713.8 3.7 convolution_convert_fusion.1
  717.6 4.9 convolution_convert_fusion.2
  722.5 43.8 %shard_map.170 = f32[128,2048]{1,0:T(8,128)S(1)} custom-call(bf16[8,128,2048]{2,1,0:T(8,128)(2,1)S(1)} %bitcast.195), custom_call_target="tpu_custom_call" | custom-call | bytes 67108864 | tf_op jit(solution)/shard_map/pallas_call | solution.py:880
  766.3 0.4 fusion.27
  767.5 1.1 copy.142
  768.6 88.6 %shard_map.171 = (f32[64,2048]{1,0:T(8,128)}, f32[64,128]{1,0:T(8,128)}, f32[3,64,2048]{2,1,0:T(8,128)}, bf16[8,256,256]{2,1,0:T(8,128)(2,1)}, f32[16384,128]{1,0:T(8,128)}) custom-call(bf16[32,64,2048]{2,1,0:T(8,128)(2,1)} %bitcast.198, f32[2,4,4,64,128]{4,3,2,1,0:T(8,128)} %bitcast.211, bf16[4,512,768]{2,1,0:T(8,128)(2,1)} %bitcast.220, ...), custom_call_target="tpu_custom_call" | custom-call | bytes 218103808 | tf_op jit(solution)/shard_map/pallas_call | solution.py:584
  857.3 1.0 slice.102
  858.2 0.8 slice_bitcast_fusion
  859.0 0.7 copy.121
  859.7 0.7 copy.120
  860.3 2.8 fusion.25
  863.1 5.7 shard_map.172
  868.8 1.1 copy.157
  870.0 0.8 copy.158
  870.8 3.4 copy.159
  (147 shorter events, 5.8 us)
Async XLA Ops:
  7.2 4.1 copy-start.25
  7.2 4.8 copy-start.36
  7.2 4.8 copy-start.38
  7.2 334.1 %all-gather.2.cloned.1.call-start = ((), (), s32[]{:S(2)}) async-start(), calls=%async_computation | async-start | bytes 17301504 | tf_op jit(solution)/shard_map/all_gather | solution.py:1249
  115.9 3.5 copy-start.2
  119.3 1.9 copy-start.39
  124.8 13.2 %copy-start.3 = (f32[1024,768]{0,1:T(8,128)}, f32[1024,768]{0,1:T(8,128)S(1)}, u32[]{:S(2)}) copy-start(f32[1024,768]{0,1:T(8,128)S(1)} %fusion.55) | copy-start | bytes 9437188
  135.7 2.7 copy-start.32
  135.7 2.7 copy-start.34
  135.8 2.7 copy-start.28
  135.8 2.7 copy-start.30
  137.7 0.8 copy-start.17
  138.5 6.6 copy-start.13
  138.6 6.6 copy-start.20
  138.6 6.6 copy-start.26
  149.3 17.0 %copy-start.37 = (s32[128,8]{0,1:T(8,128)S(1)}, s32[128,8]{0,1:T(8,128)}, u32[]{:S(2)}) copy-start(s32[128,8]{0,1:T(8,128)} %param.13) | copy-start | bytes 12292
  149.3 17.0 %copy-start.6 = (bf16[128,2048]{1,0:T(8,128)(2,1)S(1)}, bf16[128,2048]{1,0:T(8,128)(2,1)}, u32[]{:S(2)}) copy-start(bf16[128,2048]{1,0:T(8,128)(2,1)} %x_ref.1) | copy-start | bytes 1572868
  166.3 5.5 copy-start.15
  171.8 1.3 copy-start.10
  497.7 159.5 %copy-start.19 = (bf16[128,2048]{1,0:T(8,128)(2,1)S(1)}, bf16[128,2048]{1,0:T(8,128)(2,1)}, u32[]{:S(2)}) copy-start(bf16[128,2048]{1,0:T(8,128)(2,1)} %param.11) | copy-start | bytes 1572868
  653.7 3.4 copy-start.23
  658.6 35.5 %copy-start.5 = (f32[128,2048]{1,0:T(8,128)}, f32[128,2048]{1,0:T(8,128)S(1)}, u32[]{:S(2)}) copy-start(f32[128,2048]{1,0:T(8,128)S(1)} %get-tuple-element.134) | copy-start | bytes 3145732
  679.1 12.4 %slice-start = ((s8[8388608]{0:T(1024)(128)(4,1)}), s8[4194304]{0:T(1024)(128)(4,1)S(1)}, s32[]{:S(2)}) async-start(s8[8388608]{0:T(1024)(128)(4,1)} %bitcast.203), calls=%async_computation.1 | async-start | bytes 8388608
  684.2 5.1 copy-start.21
  684.2 7.4 slice-start.1
  689.2 1.5 copy-start.14
  691.6 2.3 copy-start.11
  694.1 5.8 copy-start.18
  694.1 5.8 copy-start.24
  699.9 2.3 copy-start.4
  699.9 2.3 copy-start.29
  699.9 2.3 copy-start.31
  699.9 2.3 copy-start.33
  700.0 2.3 copy-start.35
  700.5 2.4 copy-start.8
  702.2 1.0 copy-start.9
  711.2 2.5 copy-start.40
  711.2 2.6 copy-start.41
  713.8 3.7 copy-start.16
  722.5 43.8 %copy-start.7 = (bf16[128,2048]{1,0:T(8,128)(2,1)S(1)}, bf16[128,2048]{1,0:T(8,128)(2,1)}, u32[]{:S(2)}) copy-start(bf16[128,2048]{1,0:T(8,128)(2,1)} %x_ref.1) | copy-start | bytes 1572868
  857.2 5.9 copy-start
  857.2 5.9 copy-start.1
  860.3 8.5 copy-start.22
  863.1 6.9 copy-start.27
  863.1 7.7 copy-start.12
Sparse Core Ops, SparseCore 0:
  134.9 184.9 all-gather.1

commit v5 on v4

--- a/solution.py
+++ b/solution.py
@@ -502,14 +502,14 @@
     small_far()
     for stage, n, k in order:
         stage(n, k)
-        if (stage, n, k) == (main_far, last, depth - 1) and local:
-            unpack_inside(local, *halves, *unpacked)
         if (stage, n, k) == (main_near, 0, 0):
             shared_near()
             small_near()
         if (stage, n, k) == (main_own, 0, 0):
             shared_own()
             small_own()
+    if local:
+        unpack_inside(local, *halves, *unpacked)
     for n, (buffers, sems) in enumerate(zip(small_buffers, small_sems)):
         for k in range(depth - 1):
             arrive(buffers[4], sems[6:8], k)
@@ -697,9 +697,10 @@
             forward(x_place(k), x_place(k), x_z, k).start()
 
         push(remote(x_place(k), x_place(k), x_core, k, at.core()))
-    for target, pair_of in sides:
-        arrive(target.at[beside], pair_of, 0)
-        push(remote(target.at[beside], target.at[beside], pair_of, 2, at.far()))
+        if k == 2:
+            for target, pair_of in sides:
+                arrive(target.at[beside], pair_of, 0)
+                push(remote(target.at[beside], target.at[beside], pair_of, 2, at.far()))
     for k in range(depth):
         target = o_out.at[at.block(at.near_of(at.c), at.next_z(k), at.c)]
         arrive(target, o_near, k)
@@ -1247,8 +1248,8 @@
     after = jnp.minimum(scales[0, 0], 0.0)
     own_grads = (grad_comb + after).astype(low_type)
     grads = lax.all_gather(own_grads, GRID, axis=0, tiled=True)
-    tokens, gates_all, first_in, first_down = spread(
-        depth, 3, (normed_mid, gates.T), (first_in, first_down)
+    tokens, gates_all, first_in, first_down, second_down = spread(
+        depth, 3, (normed_mid, gates.T), (first_in, first_down, second_down)
     )
     grads = grads.reshape(tokens.shape)
 
@@ -1258,7 +1259,7 @@
     def by_slice(values):
         return values.reshape(ranks, chunk_rows, -1)
 
-    *sums, grad_first, down_first, second_in, second_down = run_experts(
+    *sums, grad_first, down_first, second_in = run_experts(
         depth,
         9,
         0,
@@ -1267,10 +1268,10 @@
         gates_all,
         flat(first_in),
         flat(first_down),
-        (second_in, second_down),
+        (second_in,),
         (),
     )
-    back, mixed, gate_sums, grad_second, down_second, grad_first, down_first = run_experts(
+    back, mixed, gate_sums, grad_second, down_second, grad_first = run_experts(
         depth,
         10,
         local_experts // 2,
@@ -1279,7 +1280,7 @@
         gates_all,
         flat(second_in),
         flat(second_down),
-        (by_slice(grad_first), by_slice(down_first)),
+        (by_slice(grad_first),),
         tuple(sums),
     )
     grad_mid_norm, combined, grad_gates, grad_second = collect(
@@ -1359,13 +1360,13 @@
     grad_small = jnp.pad(grad_small, ((0, 0), (0, 128 - grad_small.shape[1])))
     grad_out = t_dot(attended, grad_branch).astype(low_type)
     grad_qkv = t_dot(normed_in, grad_raw).astype(low_type)
-    grad_out, grad_small, grad_qkv, down_second, grad_expert_in = collect(
+    grad_out, grad_small, grad_qkv, down_first, down_second, grad_expert_in = collect(
         depth,
         5,
         [grad_out.reshape(-1, weight_rows, width)],
         [grad_small.reshape(-1, weight_rows, 128)],
         [grad_qkv.reshape(columns, -1, 3 * own_width)],
-        [by_slice(down_second)],
+        [by_slice(down_first), by_slice(down_second)],
         (local_experts, grad_first, grad_second),
     )
     grad_expert_in = grad_expert_in.reshape(chunk_rows, local_experts, ranks, 2, part)

time: 890 us -> 872 us (0.980)
  Pallas kernels: 755 us -> 733 us
    pallas_call x2, Pallas kernels: 155 us -> 125 us  [run_experts(): pl.pallas_call(functools.partial(experts_kernel, first, depth, bool(earli...]
    pallas_call x1, Pallas kernels: 163 us -> 180 us  [spread(): pl.pallas_call(functools.partial(spread_kernel, depth, len(arrays), len(e...]
  transfers between devices with their start and end apart: 1 -> 1, of which waited for: 0 -> 0; matrix products, arithmetic and copies ran while one was open for 3% -> 3% of each run, Pallas kernels for 20% -> 23%
where the time goes in v5:
time: 872 us; the launch traced here: 859 us
  Pallas kernels  733 us (84%)
  matrix products  52.8 us (6%)
  other arithmetic  33.6 us (4%)
  local copies, waits for them, and re-layouts  23.1 us (3%)
  between operations  16.8 us (2%)
    pallas_call x2, Pallas kernels, collect(): pl.pallas_call(functools.partial(collect_kernel, depth, local, counts), o...  240 us
    pallas_call x1, Pallas kernels, spread(): pl.pallas_call(functools.partial(spread_kernel, depth, len(arrays), len(e...  180 us
    pallas_call x2, Pallas kernels, run_experts(): pl.pallas_call(functools.partial(experts_kernel, first, depth, bool(earli...  125 us
    pallas_call x1, Pallas kernels, gather(): pl.pallas_call(functools.partial(gather_kernel, depth, local), out_shape=...  96.6 us
    pallas_call x1, Pallas kernels, collect_column(): pl.pallas_call(functools.partial(column_kernel, depth), out_shape=jax.Sha...  43.8 us
    pallas_call x4, Pallas kernels, exchange(): pl.pallas_call(functools.partial(exchange_kernel, depth, same), out_shape...  41.5 us
  transfers between devices with their start and end apart: 1, of which 0 were waited for; matrix products, arithmetic and copies ran while one was open for 3% of the time, Pallas kernels for 23%

profile of v5, /device:TPU:0, one launch (start us, length us, event | category | flops | bytes accessed | tf_op | source)
XLA Modules:
  0.0 859.4 jit_solution(2476049375420739565)
XLA Ops:
  7.2 1.6 convert_bitcast_fusion
  8.8 0.6 reshape.327
  9.4 0.6 copy.143
  10.0 1.2 reshape_reshape.12.w_ref
  11.2 0.7 convert_element_type.146.o_ref
  12.1 0.6 pad.8.s_ref
  12.7 96.6 %shard_map.161 = (bf16[8,128,2048]{2,1,0:T(8,128)(2,1)}, bf16[32,64,2048]{2,1,0:T(8,128)(2,1)}, bf16[4,8,64,768]{3,2,1,0:T(8,128)(2,1)}, bf16[4,8,64,128]{3,2,1,...) custom-call(bf16[128,2048]{1,0:T(8,128)(2,1)} %x_ref.1, ...), custom_call_target="tpu_custom_call" | custom-call | bytes 67108864 | tf_op jit(solution)/shard_map/pallas_call | solution.py:743
  109.3 1.1 slice_convert_fusion.1
  110.8 3.2 multiply_reduce_fusion.1
  114.2 1.0 multiply_convert_fusion.1
  115.3 0.9 copy-done.39
  116.1 3.6 fusion.55
  120.0 5.8 shard_map.162
  126.4 0.5 slice.118
  127.6 2.0 fusion.22
  129.7 0.9 slice.172
  130.7 2.0 fusion.38
  133.5 6.5 fusion.54
  140.0 4.1 fusion.15
  144.6 16.1 %shard_map.163 = bf16[8,128,256]{2,1,0:T(8,128)(2,1)S(1)} custom-call(bf16[8,128,256]{2,1,0:T(8,128)(2,1)S(1)} %copy.129.x_ref), custom_call_target="tpu_custom_call" | custom-call | bytes 8388608 | tf_op jit(solution)/shard_map/pallas_call | solution.py:789
  160.8 0.5 copy.107
  161.4 5.2 multiply_reduce_fusion.6
  166.8 0.6 select_reduce_fusion
  167.4 0.6 fusion.45.refs_1_
  168.0 180.4 %shard_map.164 = (bf16[32,128,2048]{2,1,0:T(8,128)(2,1)}, f32[32,16,128]{2,1,0:T(8,128)}, bf16[8,256,512]{2,1,0:T(8,128)(2,1)}, bf16[8,256,256]{2,1,0:T(8,128)(2,1)}, bf16[8,256,256]{2,1,0:T(8,128)(2,1)}) custom-call(bf16[128,2048]{1,0:T(8,128)(2,1)} %copy-done.10, f32[16,128]{1,0:T(8,128)} %fusion.45.refs_1_, ...), custom_call_target="tpu_custom_call" | custom-call | bytes 136314880 | tf_op jit(solution)/shard_map/pallas_call | solution.py:272
  348.6 5.2 fusion.2
  353.9 63.1 %shard_map.165 = (bf16[32,128,2048]{2,1,0:T(8,128)(2,1)}, bf16[32,128,2048]{2,1,0:T(8,128)(2,1)}, f32[32,16,128]{2,1,0:T(8,128)}, bf16[2048,512]{1,0:T(8,128)(2,...) custom-call(bf16[32,128,2048]{2,1,0:T(8,128)(2,1)} %get-tuple-element.50.refs_0_, ...), custom_call_target="tpu_custom_call" | custom-call | flops 38654705664 | bytes 67108864 | tf_op jit(solution)/shard_map/pallas_call | solution.py:1092
  417.0 61.5 %shard_map.166 = (bf16[32,128,2048]{2,1,0:T(8,128)(2,1)}, bf16[32,128,2048]{2,1,0:T(8,128)(2,1)}, f32[32,16,128]{2,1,0:T(8,128)}, bf16[2048,512]{1,0:T(8,128)(2,...) custom-call(bf16[32,128,2048]{2,1,0:T(8,128)(2,1)} %get-tuple-element.50.refs_0_, ...), custom_call_target="tpu_custom_call" | custom-call | flops 38654705664 | bytes 67108864 | tf_op jit(solution)/shard_map/pallas_call | solution.py:1092
  478.5 1.7 copy.145
  480.1 150.2 %shard_map.167 = (f32[128,2048]{1,0:T(8,128)}, f32[128,2048]{1,0:T(8,128)}, f32[16,128]{1,0:T(8,128)}, bf16[8,256,512]{2,1,0:T(8,128)(2,1)}) custom-call(bf16[32,128,2048]{2,1,0:T(8,128)(2,1)} %get-tuple-element.61.refs_0_, bf16[32,128,2048]{2,1,0:T(8,128)(2,1)} %get-tuple-element.62.refs_1_, f32[2,4,4,16,128]{4,3,2,1,0:T(8,128)} %bitcast.226, ...), custom_call_target="tpu_custom_call" | custom-call | bytes 574619648 | tf_op jit(solution)/shard_map/pallas_call | solution.py:584
  630.3 0.8 fusion.40
  631.1 0.7 fusion.42
  631.9 1.8 multiply_reduce_fusion.2
  633.7 1.5 convert_add_fusion
  635.2 6.7 convolution_convert_fusion.3
  642.2 0.4 copy.144
  643.0 12.1 %shard_map.168 = bf16[8,128,256]{2,1,0:T(8,128)(2,1)S(1)} custom-call(bf16[8,128,256]{2,1,0:T(8,128)(2,1)S(1)} %reshape.353.x_ref), custom_call_target="tpu_custom_call" | custom-call | bytes 8388608 | tf_op jit(solution)/shard_map/pallas_call | solution.py:789
  655.3 0.4 copy.114
  655.7 5.0 multiply_reduce_fusion
  660.7 5.0 multiply_convert_fusion
  665.8 1.5 convolution_multiply_fusion.1
  667.3 0.8 convolution_multiply_fusion.2
  668.2 2.3 fusion.18
  670.7 5.8 convolution_convert_fusion
  676.5 0.4 multiply_subtract_fusion.1
  677.2 1.6 copy-done.4
  678.8 0.7 fusion.30
  679.8 7.6 shard_map.169
  687.4 2.1 multiply_convert_fusion.3
  690.0 3.7 convolution_convert_fusion.1
  693.7 4.9 convolution_convert_fusion.2
  698.6 43.8 %shard_map.170 = f32[128,2048]{1,0:T(8,128)S(1)} custom-call(bf16[8,128,2048]{2,1,0:T(8,128)(2,1)S(1)} %bitcast.195), custom_call_target="tpu_custom_call" | custom-call | bytes 67108864 | tf_op jit(solution)/shard_map/pallas_call | solution.py:881
  742.5 0.4 fusion.27
  743.7 1.1 copy.142
  744.8 90.2 %shard_map.171 = (f32[64,2048]{1,0:T(8,128)}, f32[64,128]{1,0:T(8,128)}, f32[3,64,2048]{2,1,0:T(8,128)}, bf16[8,256,256]{2,1,0:T(8,128)(2,1)}, bf16[8,256,256]{2,1,0:T(8,128)(2,1)}, /*index=5*/f32[16384,128]{1,0:T(8,128)}) custom-call(bf16[32,64,2048]{2,1,0:T(8,128)(2,1)} %bitcast.198, f32[2,4,4,64,128]{4,3,2,1,0:T(8,128)} %bitcast.211, ...), custom_call_target="tpu_custom_call" | custom-call | bytes 234881024 | tf_op jit(solution)/shard_map/pallas_call | solution.py:584
  835.1 1.0 slice.102
  836.1 0.8 slice_bitcast_fusion
  836.8 0.7 copy.121
  837.5 0.7 copy.120
  838.2 2.8 fusion.25
  841.0 5.7 shard_map.172
  846.7 1.1 copy.157
  847.8 0.8 copy.158
  848.6 3.4 copy.159
  (147 shorter events, 5.8 us)
Async XLA Ops:
  7.2 4.1 copy-start.25
  7.2 4.8 copy-start.36
  7.2 4.8 copy-start.38
  7.2 346.7 %all-gather.2.cloned.1.call-start = ((), (), s32[]{:S(2)}) async-start(), calls=%async_computation | async-start | bytes 17301504 | tf_op jit(solution)/shard_map/all_gather | solution.py:1250
  110.8 3.5 copy-start.2
  114.2 1.9 copy-start.39
  119.7 13.2 %copy-start.3 = (f32[1024,768]{0,1:T(8,128)}, f32[1024,768]{0,1:T(8,128)S(1)}, u32[]{:S(2)}) copy-start(f32[1024,768]{0,1:T(8,128)S(1)} %fusion.55) | copy-start | bytes 9437188
  130.6 2.7 copy-start.32
  130.6 2.7 copy-start.34
  130.6 2.7 copy-start.28
  130.7 2.7 copy-start.30
  132.6 0.8 copy-start.17
  133.4 6.6 copy-start.13
  133.5 6.6 copy-start.20
  133.5 6.6 copy-start.26
  144.2 17.2 %copy-start.37 = (s32[128,8]{0,1:T(8,128)S(1)}, s32[128,8]{0,1:T(8,128)}, u32[]{:S(2)}) copy-start(s32[128,8]{0,1:T(8,128)} %param.13) | copy-start | bytes 12292
  144.2 17.2 %copy-start.6 = (bf16[128,2048]{1,0:T(8,128)(2,1)S(1)}, bf16[128,2048]{1,0:T(8,128)(2,1)}, u32[]{:S(2)}) copy-start(bf16[128,2048]{1,0:T(8,128)(2,1)} %x_ref.1) | copy-start | bytes 1572868
  161.4 5.4 copy-start.15
  166.8 1.3 copy-start.10
  480.1 153.6 %copy-start.19 = (bf16[128,2048]{1,0:T(8,128)(2,1)S(1)}, bf16[128,2048]{1,0:T(8,128)(2,1)}, u32[]{:S(2)}) copy-start(bf16[128,2048]{1,0:T(8,128)(2,1)} %param.11) | copy-start | bytes 1572868
  630.3 3.4 copy-start.23
  635.2 35.5 %copy-start.5 = (f32[128,2048]{1,0:T(8,128)}, f32[128,2048]{1,0:T(8,128)S(1)}, u32[]{:S(2)}) copy-start(f32[128,2048]{1,0:T(8,128)S(1)} %get-tuple-element.134) | copy-start | bytes 3145732
  655.7 12.4 %slice-start = ((s8[8388608]{0:T(1024)(128)(4,1)}), s8[4194304]{0:T(1024)(128)(4,1)S(1)}, s32[]{:S(2)}) async-start(s8[8388608]{0:T(1024)(128)(4,1)} %bitcast.203), calls=%async_computation.1 | async-start | bytes 8388608
  660.7 5.1 copy-start.21
  660.7 7.4 slice-start.1
  665.8 1.5 copy-start.14
  668.1 2.4 copy-start.11
  670.7 5.8 copy-start.18
  670.7 5.8 copy-start.24
  676.5 2.3 copy-start.4
  676.5 2.3 copy-start.29
  676.5 2.3 copy-start.31
  676.5 2.3 copy-start.33
  676.5 2.3 copy-start.35
  677.1 2.4 copy-start.8
  678.8 1.0 copy-start.9
  687.4 2.5 copy-start.40
  687.4 2.6 copy-start.41
  690.0 3.7 copy-start.16
  698.6 43.8 %copy-start.7 = (bf16[128,2048]{1,0:T(8,128)(2,1)S(1)}, bf16[128,2048]{1,0:T(8,128)(2,1)}, u32[]{:S(2)}) copy-start(bf16[128,2048]{1,0:T(8,128)(2,1)} %x_ref.1) | copy-start | bytes 1572868
  835.1 5.9 copy-start
  835.1 5.9 copy-start.1
  838.2 8.5 copy-start.22
  841.0 6.9 copy-start.27
  841.0 7.7 copy-start.12
Sparse Core Ops, SparseCore 0:
  129.8 184.9 all-gather.1

commit v6 on v5

--- a/solution.py
+++ b/solution.py
@@ -642,6 +642,18 @@
         push(remote(s_ref, s_out.at[column, own], s_sems, slot, there))
         source = w_ref.at[there[2] * 2 + there[3]]
         push(remote(source, w_out.at[column, own], w_sems, slot, there))
+    def w_rank(j):
+        k, core = ([(0, 0)] + ranks)[j]
+        return at.along(depth - k) * 2 + lax.rem(at.c + core, 2)
+
+    all_ranks = 2 * depth
+
+    def w_aside(source, j):
+        target = w_out.at[column, w_rank(j)]
+        push(remote(source, target, w_side, j, at.near()))
+        push(remote(source, target, w_side, all_ranks + j, at.far()))
+
+    w_aside(w_ref.at[own], 0)
     first = (at.y, at.x, at.next_z(1), at.c)
     push(remote(o_ref, o_place(0), o_z, at.z, first))
     push(remote(x_ref, x_place(0), x_z, at.z, first))
@@ -669,17 +681,16 @@
     near_y, near_x = at.near_of(at.c)
     far_y, far_x = at.far_of(at.c)
     beside, across = near_y * 2 + near_x, far_y * 2 + far_x
-    sides = ((s_out, s_side), (w_out, w_side))
     pack(2 * depth, local_experts, in_ref, down_ref, *packed)
     for slot, (j, core) in enumerate(ranks):
         source = at.along(depth - j) * 2 + lax.rem(at.c + core, 2)
         arrive(s_out.at[column, source], s_sems, slot)
         arrive(w_out.at[column, source], w_sems, slot)
+        w_aside(w_out.at[column, source], 1 + slot)
     for copy in local:
         copy.wait()
-    for target, pair_of in sides:
-        push(remote(target.at[column], target.at[column], pair_of, 0, at.near()))
-        push(remote(target.at[column], target.at[column], pair_of, 1, at.far()))
+    push(remote(s_out.at[column], s_out.at[column], s_side, 0, at.near()))
+    push(remote(s_out.at[column], s_out.at[column], s_side, 1, at.far()))
     for k in range(1, depth):
         arrive(o_place(k), o_z, at.next_z(k))
 
@@ -698,9 +709,12 @@
 
         push(remote(x_place(k), x_place(k), x_core, k, at.core()))
         if k == 2:
-            for target, pair_of in sides:
-                arrive(target.at[beside], pair_of, 0)
-                push(remote(target.at[beside], target.at[beside], pair_of, 2, at.far()))
+            arrive(s_out.at[beside], s_side, 0)
+            push(remote(s_out.at[beside], s_out.at[beside], s_side, 2, at.far()))
+            for j in range(all_ranks):
+                target = w_out.at[beside, w_rank(j)]
+                arrive(target, w_side, j)
+                push(remote(target, target, w_side, 2 * all_ranks + j, at.far()))
     for k in range(depth):
         target = o_out.at[at.block(at.near_of(at.c), at.next_z(k), at.c)]
         arrive(target, o_near, k)
@@ -711,9 +725,11 @@
         target = o_out.at[at.block(place, at.next_z(j % depth), at.c)]
         arrive(target, o_far, j)
         push(remote(target, target, o_core, 2 * depth + j, at.core()))
-    for target, pair_of in sides:
-        arrive(target.at[across], pair_of, 1)
-        arrive(target.at[3 - column], pair_of, 2)
+    arrive(s_out.at[across], s_side, 1)
+    arrive(s_out.at[3 - column], s_side, 2)
+    for j in range(all_ranks):
+        arrive(w_out.at[across, w_rank(j)], w_side, all_ranks + j)
+        arrive(w_out.at[3 - column, w_rank(j)], w_side, 2 * all_ranks + j)
     for k in range(depth):
         arrive(x_out.at[at.next_z(k) * 2 + 1 - at.c], x_core, k)
     core = 1 - at.c
@@ -738,7 +754,7 @@
     chunk, local = expert_in.shape[:2]
     ranks = 2 * depth
     sems = pair(depth + 1) + pair(depth) + pair(depth + 1) + pair(depth) + pair(2 * depth)
-    sems += pair(4 * depth) + pair(ranks - 1) * 2 + pair(3) * 2
+    sems += pair(4 * depth) + pair(ranks - 1) * 2 + pair(3 * ranks) + pair(3)
     sems.append(pltpu.SemaphoreType.DMA((4,)))
     return pl.pallas_call(
         functools.partial(gather_kernel, depth, local),
@@ -1196,6 +1212,8 @@
     ]
     normed_in = seq_input.reshape(seq_rows, width).astype(high_type)
     normed_in = (normed_in * rms_scale(normed_in) * gain_rows[0]).astype(low_type)
+    normed_in = lax.optimization_barrier(normed_in)
+
     raw = dot(normed_in, qkv_weight)
     query_raw, key_raw = raw[:, :own_width], raw[:, own_width : 2 * own_width]
     value_rows = raw[:, 2 * own_width :].astype(low_type)

time: 872 us -> 863 us (0.990)
  no operation moved by 1% of the time
where the time goes in v6:
time: 863 us; the launch traced here: 852 us
  Pallas kernels  730 us (85%)
  matrix products  52.5 us (6%)
  other arithmetic  28.2 us (3%)
  local copies, waits for them, and re-layouts  24.3 us (3%)
  between operations  16.4 us (2%)
    pallas_call x2, Pallas kernels, collect(): pl.pallas_call(functools.partial(collect_kernel, depth, local, counts), o...  243 us
    pallas_call x1, Pallas kernels, spread(): pl.pallas_call(functools.partial(spread_kernel, depth, len(arrays), len(e...  180 us
    pallas_call x2, Pallas kernels, run_experts(): pl.pallas_call(functools.partial(experts_kernel, first, depth, bool(earli...  124 us
    pallas_call x1, Pallas kernels, gather(): pl.pallas_call(functools.partial(gather_kernel, depth, local), out_shape=...  92.2 us
    pallas_call x1, Pallas kernels, collect_column(): pl.pallas_call(functools.partial(column_kernel, depth), out_shape=jax.Sha...  43.8 us
    pallas_call x4, Pallas kernels, exchange(): pl.pallas_call(functools.partial(exchange_kernel, depth, same), out_shape...  41.9 us
  transfers between devices with their start and end apart: 1, of which 0 were waited for; matrix products, arithmetic and copies ran while one was open for 3% of the time, Pallas kernels for 23%

profile of v6, /device:TPU:0, one launch (start us, length us, event | category | flops | bytes accessed | tf_op | source)
XLA Modules:
  0.0 851.9 jit_solution(9734676652070688105)
XLA Ops:
  7.2 1.6 convert_bitcast_fusion
  8.8 0.6 reshape.316
  9.4 0.6 copy.143
  10.0 1.2 reshape_reshape.12.w_ref
  11.2 0.7 convert_element_type.140.o_ref
  12.1 0.6 pad.8.s_ref
  12.7 92.2 %shard_map.161 = (bf16[8,128,2048]{2,1,0:T(8,128)(2,1)}, bf16[32,64,2048]{2,1,0:T(8,128)(2,1)}, bf16[4,8,64,768]{3,2,1,0:T(8,128)(2,1)}, bf16[4,8,64,128]{3,2,1,...) custom-call(bf16[128,2048]{1,0:T(8,128)(2,1)} %x_ref.1, ...), custom_call_target="tpu_custom_call" | custom-call | bytes 67108864 | tf_op jit(solution)/shard_map/pallas_call | solution.py:759
  105.0 1.1 slice_convert_fusion.1
  106.4 3.2 multiply_reduce_fusion.1
  109.9 1.0 fusion.2
  110.9 0.8 copy-done.34
  111.8 3.6 fusion.54
  115.6 5.8 shard_map.162
  122.2 0.5 slice.118
  123.3 2.0 fusion.22
  125.4 0.9 slice.172
  126.4 2.2 fusion.38
  129.3 6.5 fusion.53
  135.9 4.1 fusion.15
  140.5 15.9 %shard_map.163 = bf16[8,128,256]{2,1,0:T(8,128)(2,1)S(1)} custom-call(bf16[8,128,256]{2,1,0:T(8,128)(2,1)S(1)} %copy.129.x_ref), custom_call_target="tpu_custom_call" | custom-call | bytes 8388608 | tf_op jit(solution)/shard_map/pallas_call | solution.py:805
  156.6 0.5 copy.107
  157.1 5.4 multiply_reduce_fusion.6
  162.7 0.6 select_reduce_fusion
  163.3 0.6 fusion.45.refs_1_
  164.0 179.8 %shard_map.164 = (bf16[32,128,2048]{2,1,0:T(8,128)(2,1)}, f32[32,16,128]{2,1,0:T(8,128)}, bf16[8,256,512]{2,1,0:T(8,128)(2,1)}, bf16[8,256,256]{2,1,0:T(8,128)(2,1)}, bf16[8,256,256]{2,1,0:T(8,128)(2,1)}) custom-call(bf16[128,2048]{1,0:T(8,128)(2,1)} %copy-done.13, f32[16,128]{1,0:T(8,128)} %fusion.45.refs_1_, ...), custom_call_target="tpu_custom_call" | custom-call | bytes 136314880 | tf_op jit(solution)/shard_map/pallas_call | solution.py:272
  344.0 62.9 %shard_map.165 = (bf16[32,128,2048]{2,1,0:T(8,128)(2,1)}, bf16[32,128,2048]{2,1,0:T(8,128)(2,1)}, f32[32,16,128]{2,1,0:T(8,128)}, bf16[2048,512]{1,0:T(8,128)(2,...) custom-call(bf16[32,128,2048]{2,1,0:T(8,128)(2,1)} %get-tuple-element.50.refs_0_, ...), custom_call_target="tpu_custom_call" | custom-call | flops 38654705664 | bytes 67108864 | tf_op jit(solution)/shard_map/pallas_call | solution.py:1108
  406.9 61.5 %shard_map.166 = (bf16[32,128,2048]{2,1,0:T(8,128)(2,1)}, bf16[32,128,2048]{2,1,0:T(8,128)(2,1)}, f32[32,16,128]{2,1,0:T(8,128)}, bf16[2048,512]{1,0:T(8,128)(2,...) custom-call(bf16[32,128,2048]{2,1,0:T(8,128)(2,1)} %get-tuple-element.50.refs_0_, ...), custom_call_target="tpu_custom_call" | custom-call | flops 38654705664 | bytes 67108864 | tf_op jit(solution)/shard_map/pallas_call | solution.py:1108
  468.4 1.7 copy.145
  470.1 152.1 %shard_map.167 = (f32[128,2048]{1,0:T(8,128)}, f32[128,2048]{1,0:T(8,128)}, f32[16,128]{1,0:T(8,128)}, bf16[8,256,512]{2,1,0:T(8,128)(2,1)}) custom-call(bf16[32,128,2048]{2,1,0:T(8,128)(2,1)} %get-tuple-element.61.refs_0_, bf16[32,128,2048]{2,1,0:T(8,128)(2,1)} %get-tuple-element.62.refs_1_, f32[2,4,4,16,128]{4,3,2,1,0:T(8,128)} %bitcast.224, ...), custom_call_target="tpu_custom_call" | custom-call | bytes 574619648 | tf_op jit(solution)/shard_map/pallas_call | solution.py:584
  622.2 0.8 fusion.40
  623.0 0.7 fusion.42
  623.7 1.8 multiply_reduce_fusion.2
  625.6 1.4 convert_add_fusion
  627.0 1.0 copy-done.4
  628.0 6.3 convolution_convert_fusion.3
  634.7 0.4 copy.144
  635.5 12.1 %shard_map.168 = bf16[8,128,256]{2,1,0:T(8,128)(2,1)S(1)} custom-call(bf16[8,128,256]{2,1,0:T(8,128)(2,1)S(1)} %reshape.342.x_ref), custom_call_target="tpu_custom_call" | custom-call | bytes 8388608 | tf_op jit(solution)/shard_map/pallas_call | solution.py:805
  647.7 0.4 copy.114
  648.2 4.8 multiply_reduce_fusion
  653.1 4.8 multiply_convert_fusion
  657.9 1.5 convolution_multiply_fusion.1
  659.4 0.8 convolution_multiply_fusion.2
  660.2 2.3 fusion.18
  663.1 1.7 copy-done.3
  664.8 0.7 fusion.30
  665.8 8.0 shard_map.169
  673.9 2.1 multiply_convert_fusion.2
  676.0 0.6 copy-done.18
  676.7 4.9 convolution_convert_fusion.2
  681.7 3.7 convolution_convert_fusion.1
  685.6 5.8 convolution_convert_fusion
  691.4 43.8 %shard_map.170 = f32[128,2048]{1,0:T(8,128)S(1)} custom-call(bf16[8,128,2048]{2,1,0:T(8,128)(2,1)S(1)} %bitcast.194), custom_call_target="tpu_custom_call" | custom-call | bytes 67108864 | tf_op jit(solution)/shard_map/pallas_call | solution.py:897
  735.2 0.4 fusion.27
  736.2 1.1 copy.142
  737.3 90.6 %shard_map.171 = (f32[64,2048]{1,0:T(8,128)}, f32[64,128]{1,0:T(8,128)}, f32[3,64,2048]{2,1,0:T(8,128)}, bf16[8,256,256]{2,1,0:T(8,128)(2,1)}, bf16[8,256,256]{2,1,0:T(8,128)(2,1)}, /*index=5*/f32[16384,128]{1,0:T(8,128)}) custom-call(bf16[32,64,2048]{2,1,0:T(8,128)(2,1)} %bitcast.197, f32[2,4,4,64,128]{4,3,2,1,0:T(8,128)} %bitcast.210, ...), custom_call_target="tpu_custom_call" | custom-call | bytes 234881024 | tf_op jit(solution)/shard_map/pallas_call | solution.py:584
  827.9 1.0 slice.102
  828.9 0.8 slice_bitcast_fusion
  829.7 0.7 copy.121
  830.3 0.7 copy.120
  831.0 2.8 fusion.25
  833.8 5.7 shard_map.172
  839.5 1.1 copy.157
  840.6 0.8 copy.158
  841.4 3.4 copy.159
  (136 shorter events, 5.5 us)
Async XLA Ops:
  7.2 4.1 copy-start.25
  7.2 4.8 copy-start.31
  7.2 4.8 copy-start.33
  7.2 336.8 %all-gather.2.cloned.1.call-start = ((), (), s32[]{:S(2)}) async-start(), calls=%async_computation | async-start | bytes 17301504 | tf_op jit(solution)/shard_map/all_gather | solution.py:1268
  106.4 3.5 copy-start.6
  106.4 4.5 copy-start.29
  109.9 1.9 copy-start.34
  110.9 4.5 copy-start.17
  115.4 13.4 %copy-start.2 = (f32[1024,768]{0,1:T(8,128)}, f32[1024,768]{0,1:T(8,128)S(1)}, u32[]{:S(2)}) copy-start(f32[1024,768]{0,1:T(8,128)S(1)} %fusion.54) | copy-start | bytes 9437188
  129.3 6.6 copy-start.20
  129.3 6.6 copy-start.26
  140.0 17.0 %copy-start.32 = (s32[128,8]{0,1:T(8,128)S(1)}, s32[128,8]{0,1:T(8,128)}, u32[]{:S(2)}) copy-start(s32[128,8]{0,1:T(8,128)} %param.13) | copy-start | bytes 12292
  140.0 17.1 %copy-start.7 = (bf16[128,2048]{1,0:T(8,128)(2,1)S(1)}, bf16[128,2048]{1,0:T(8,128)(2,1)}, u32[]{:S(2)}) copy-start(bf16[128,2048]{1,0:T(8,128)(2,1)} %x_ref.1) | copy-start | bytes 1572868
  157.1 5.5 copy-start.9
  157.1 5.6 copy-start.16
  162.7 1.3 copy-start.13
  470.1 155.5 %copy-start.19 = (bf16[128,2048]{1,0:T(8,128)(2,1)S(1)}, bf16[128,2048]{1,0:T(8,128)(2,1)}, u32[]{:S(2)}) copy-start(bf16[128,2048]{1,0:T(8,128)(2,1)} %param.11) | copy-start | bytes 1572868
  622.2 3.4 copy-start.23
  627.0 1.0 copy-start.4
  634.3 13.9 %copy-start.27 = (bf16[1024,256]{0,1:T(8,128)(2,1)S(1)}, bf16[1024,256]{0,1:T(8,128)(2,1)}, u32[]{:S(2)}) copy-start(bf16[1024,256]{0,1:T(8,128)(2,1)} %slice.172) | copy-start | bytes 1572868
  648.2 12.0 %slice-start = ((s8[8388608]{0:T(1024)(128)(4,1)}), s8[4194304]{0:T(1024)(128)(4,1)S(1)}, s32[]{:S(2)}) async-start(s8[8388608]{0:T(1024)(128)(4,1)} %bitcast.202), calls=%async_computation.1 | async-start | bytes 8388608
  653.1 4.8 copy-start.21
  653.1 7.1 slice-start.1
  660.2 2.4 copy-start.24
  662.5 2.3 copy-start.3
  663.0 2.5 copy-start.11
  664.8 1.0 copy-start.12
  673.8 2.8 copy-start.18
  673.8 2.9 copy-start.36
  676.7 4.9 copy-start.35
  681.7 3.7 copy-start.14
  681.7 3.9 copy-start.5
  681.7 3.9 copy-start.10
  691.4 43.8 %copy-start.8 = (bf16[128,2048]{1,0:T(8,128)(2,1)S(1)}, bf16[128,2048]{1,0:T(8,128)(2,1)}, u32[]{:S(2)}) copy-start(bf16[128,2048]{1,0:T(8,128)(2,1)} %x_ref.1) | copy-start | bytes 1572868
  691.4 43.8 %copy-start.30 = (f32[1,2048]{1,0:T(1,128)S(1)}, f32[1,2048]{1,0:T(1,128)}, u32[]{:S(2)}) copy-start(f32[1,2048]{1,0:T(1,128)} %copy-done.29) | copy-start | bytes 24580
  827.9 5.9 copy-start
  827.9 5.9 copy-start.1
  831.0 8.5 %copy-start.22 = (f32[3,64,2048]{2,1,0:T(8,128)S(1)}, f32[3,64,2048]{2,1,0:T(8,128)}, u32[]{:S(2)}) copy-start(f32[3,64,2048]{2,1,0:T(8,128)} %get-tuple-element.172) | copy-start | bytes 4718596
  833.8 6.9 copy-start.28
  833.8 7.7 copy-start.15
Sparse Core Ops, SparseCore 0:
  125.5 185.6 all-gather.1

commit v7 on v6

--- a/solution.py
+++ b/solution.py
@@ -191,37 +191,55 @@
         for n in range(count):
             forward(n, sources[n], 0).start()
 
-    for k in others:
-        index = at.block(at.own_column, at.next_z(k), at.c)
-        for n in range(count):
-            arrive(n, index, z_kind, at.next_z(k))
-
-        @pl.when(inner)
-        def _(index=index, k=k):
-            for n in range(count):
-                forward(n, targets[n].at[index], k).start()
-
-        for n in range(count):
-            push(n, targets[n].at[index], index, near_kind, k, at.near())
-            push(n, targets[n].at[index], index, far_kind, k, at.far())
-            push(n, targets[n].at[index], index, core_kind, k, at.core())
     own_rank = at.z * 2 + at.c
-    for n in range(extra):
-        for slot, there in enumerate(peers):
-            copy = remote(
+
+    def extra_copies():
+        return [
+            remote(
                 extra_sources[n].at[there[2] * 2 + there[3]],
                 extra_targets[n].at[own_rank],
                 extra_sems[3 * n :],
                 slot,
                 there,
             )
+            for n in range(extra)
+            for slot, there in enumerate(peers)
+        ]
+
+    def extra_kept():
+        return [
+            pltpu.make_async_copy(
+                extra_sources[n].at[own_rank], extra_targets[n].at[own_rank], extra_sems[3 * n + 2]
+            )
+            for n in range(extra)
+        ]
+
+    def start_extras():
+        for copy in extra_copies() + extra_kept():
             copy.start()
-            started.append(copy)
-        copy = pltpu.make_async_copy(
-            extra_sources[n].at[own_rank], extra_targets[n].at[own_rank], extra_sems[3 * n + 2]
-        )
-        copy.start()
-        local.append(copy)
+
+    @pl.when(lax.rem(at.z, depth - 1) == 0)
+    def _():
+        start_extras()
+
+    for k in others:
+        index = at.block(at.own_column, at.next_z(k), at.c)
+        for n in range(count):
+            arrive(n, index, z_kind, at.next_z(k))
+
+        @pl.when(inner)
+        def _(index=index, k=k):
+            for n in range(count):
+                forward(n, targets[n].at[index], k).start()
+
+        for n in range(count):
+            push(n, targets[n].at[index], index, near_kind, k, at.near())
+            push(n, targets[n].at[index], index, far_kind, k, at.far())
+            push(n, targets[n].at[index], index, core_kind, k, at.core())
+    @pl.when(inner)
+    def _():
+        start_extras()
+
     for k in range(depth):
         index = at.block(at.near_of(at.c), at.next_z(k), at.c)
         for n in range(count):
@@ -253,9 +271,9 @@
                 index = at.block(at.own_column, at.next_z(k), at.c)
                 forward(n, targets[n].at[index], k).wait_send()
 
-    for copy in started:
+    for copy in extra_copies() + started:
         copy.wait_send()
-    for copy in local:
+    for copy in extra_kept() + local:
         copy.wait()
 
 

time: 863 us -> 862 us (level)
  no operation moved by 1% of the time
where the time goes in v7:
time: 862 us; the launch traced here: 850 us
  Pallas kernels  729 us (85%)
  matrix products  52.5 us (6%)
  other arithmetic  28.2 us (3%)
  local copies, waits for them, and re-layouts  24.3 us (3%)
  between operations  16.4 us (2%)
    pallas_call x2, Pallas kernels, collect(): pl.pallas_call(functools.partial(collect_kernel, depth, local, counts), o...  241 us
    pallas_call x1, Pallas kernels, spread(): pl.pallas_call(functools.partial(spread_kernel, depth, len(arrays), len(e...  177 us
    pallas_call x2, Pallas kernels, run_experts(): pl.pallas_call(functools.partial(experts_kernel, first, depth, bool(earli...  127 us
    pallas_call x1, Pallas kernels, gather(): pl.pallas_call(functools.partial(gather_kernel, depth, local), out_shape=...  92.2 us
    pallas_call x1, Pallas kernels, collect_column(): pl.pallas_call(functools.partial(column_kernel, depth), out_shape=jax.Sha...  43.8 us
    pallas_call x4, Pallas kernels, exchange(): pl.pallas_call(functools.partial(exchange_kernel, depth, same), out_shape...  41.8 us
  transfers between devices with their start and end apart: 1, of which 0 were waited for; matrix products, arithmetic and copies ran while one was open for 3% of the time, Pallas kernels for 23%

profile of v7, /device:TPU:0, one launch (start us, length us, event | category | flops | bytes accessed | tf_op | source)
XLA Modules:
  0.0 850.1 jit_solution(13689781001648779632)
XLA Ops:
  7.2 1.6 convert_bitcast_fusion
  8.8 0.6 reshape.316
  9.4 0.6 copy.143
  10.0 1.2 reshape_reshape.12.w_ref
  11.2 0.7 convert_element_type.140.o_ref
  12.1 0.6 pad.8.s_ref
  12.7 92.2 %shard_map.161 = (bf16[8,128,2048]{2,1,0:T(8,128)(2,1)}, bf16[32,64,2048]{2,1,0:T(8,128)(2,1)}, bf16[4,8,64,768]{3,2,1,0:T(8,128)(2,1)}, bf16[4,8,64,128]{3,2,1,...) custom-call(bf16[128,2048]{1,0:T(8,128)(2,1)} %x_ref.1, ...), custom_call_target="tpu_custom_call" | custom-call | bytes 67108864 | tf_op jit(solution)/shard_map/pallas_call | solution.py:777
  105.0 1.1 slice_convert_fusion.1
  106.4 3.2 multiply_reduce_fusion.1
  109.9 1.0 fusion.2
  110.9 0.8 copy-done.34
  111.8 3.6 fusion.54
  115.6 5.8 shard_map.162
  122.2 0.5 slice.118
  123.3 2.0 fusion.22
  125.4 0.9 slice.172
  126.4 2.2 fusion.38
  129.3 6.5 fusion.53
  135.9 4.1 fusion.15
  140.5 15.9 %shard_map.163 = bf16[8,128,256]{2,1,0:T(8,128)(2,1)S(1)} custom-call(bf16[8,128,256]{2,1,0:T(8,128)(2,1)S(1)} %copy.129.x_ref), custom_call_target="tpu_custom_call" | custom-call | bytes 8388608 | tf_op jit(solution)/shard_map/pallas_call | solution.py:823
  156.6 0.5 copy.107
  157.1 5.4 multiply_reduce_fusion.6
  162.7 0.6 select_reduce_fusion
  163.3 0.6 fusion.45.refs_1_
  164.0 177.1 %shard_map.164 = (bf16[32,128,2048]{2,1,0:T(8,128)(2,1)}, f32[32,16,128]{2,1,0:T(8,128)}, bf16[8,256,512]{2,1,0:T(8,128)(2,1)}, bf16[8,256,256]{2,1,0:T(8,128)(2,1)}, bf16[8,256,256]{2,1,0:T(8,128)(2,1)}) custom-call(bf16[128,2048]{1,0:T(8,128)(2,1)} %copy-done.13, f32[16,128]{1,0:T(8,128)} %fusion.45.refs_1_, ...), custom_call_target="tpu_custom_call" | custom-call | bytes 136314880 | tf_op jit(solution)/shard_map/pallas_call | solution.py:290
  341.3 64.0 %shard_map.165 = (bf16[32,128,2048]{2,1,0:T(8,128)(2,1)}, bf16[32,128,2048]{2,1,0:T(8,128)(2,1)}, f32[32,16,128]{2,1,0:T(8,128)}, bf16[2048,512]{1,0:T(8,128)(2,...) custom-call(bf16[32,128,2048]{2,1,0:T(8,128)(2,1)} %get-tuple-element.50.refs_0_, ...), custom_call_target="tpu_custom_call" | custom-call | flops 38654705664 | bytes 67108864 | tf_op jit(solution)/shard_map/pallas_call | solution.py:1126
  405.3 62.9 %shard_map.166 = (bf16[32,128,2048]{2,1,0:T(8,128)(2,1)}, bf16[32,128,2048]{2,1,0:T(8,128)(2,1)}, f32[32,16,128]{2,1,0:T(8,128)}, bf16[2048,512]{1,0:T(8,128)(2,...) custom-call(bf16[32,128,2048]{2,1,0:T(8,128)(2,1)} %get-tuple-element.50.refs_0_, ...), custom_call_target="tpu_custom_call" | custom-call | flops 38654705664 | bytes 67108864 | tf_op jit(solution)/shard_map/pallas_call | solution.py:1126
  468.1 1.7 copy.145
  469.8 150.8 %shard_map.167 = (f32[128,2048]{1,0:T(8,128)}, f32[128,2048]{1,0:T(8,128)}, f32[16,128]{1,0:T(8,128)}, bf16[8,256,512]{2,1,0:T(8,128)(2,1)}) custom-call(bf16[32,128,2048]{2,1,0:T(8,128)(2,1)} %get-tuple-element.61.refs_0_, bf16[32,128,2048]{2,1,0:T(8,128)(2,1)} %get-tuple-element.62.refs_1_, f32[2,4,4,16,128]{4,3,2,1,0:T(8,128)} %bitcast.224, ...), custom_call_target="tpu_custom_call" | custom-call | bytes 574619648 | tf_op jit(solution)/shard_map/pallas_call | solution.py:602
  620.6 0.8 fusion.40
  621.4 0.7 fusion.42
  622.2 1.8 multiply_reduce_fusion.2
  624.0 1.4 convert_add_fusion
  625.5 1.0 copy-done.4
  626.4 6.3 convolution_convert_fusion.3
  633.1 0.4 copy.144
  633.9 12.1 %shard_map.168 = bf16[8,128,256]{2,1,0:T(8,128)(2,1)S(1)} custom-call(bf16[8,128,256]{2,1,0:T(8,128)(2,1)S(1)} %reshape.342.x_ref), custom_call_target="tpu_custom_call" | custom-call | bytes 8388608 | tf_op jit(solution)/shard_map/pallas_call | solution.py:823
  646.2 0.4 copy.114
  646.6 4.8 multiply_reduce_fusion
  651.5 4.8 multiply_convert_fusion
  656.3 1.5 convolution_multiply_fusion.1
  657.8 0.8 convolution_multiply_fusion.2
  658.6 2.3 fusion.18
  661.5 1.7 copy-done.3
  663.2 0.7 fusion.30
  664.2 7.9 shard_map.169
  672.2 2.1 multiply_convert_fusion.2
  674.3 0.6 copy-done.18
  675.0 4.9 convolution_convert_fusion.2
  680.0 3.7 convolution_convert_fusion.1
  683.9 5.8 convolution_convert_fusion
  689.7 43.8 %shard_map.170 = f32[128,2048]{1,0:T(8,128)S(1)} custom-call(bf16[8,128,2048]{2,1,0:T(8,128)(2,1)S(1)} %bitcast.194), custom_call_target="tpu_custom_call" | custom-call | bytes 67108864 | tf_op jit(solution)/shard_map/pallas_call | solution.py:915
  733.5 0.4 fusion.27
  734.5 1.1 copy.142
  735.6 90.5 %shard_map.171 = (f32[64,2048]{1,0:T(8,128)}, f32[64,128]{1,0:T(8,128)}, f32[3,64,2048]{2,1,0:T(8,128)}, bf16[8,256,256]{2,1,0:T(8,128)(2,1)}, bf16[8,256,256]{2,1,0:T(8,128)(2,1)}, /*index=5*/f32[16384,128]{1,0:T(8,128)}) custom-call(bf16[32,64,2048]{2,1,0:T(8,128)(2,1)} %bitcast.197, f32[2,4,4,64,128]{4,3,2,1,0:T(8,128)} %bitcast.210, ...), custom_call_target="tpu_custom_call" | custom-call | bytes 234881024 | tf_op jit(solution)/shard_map/pallas_call | solution.py:602
  826.1 1.0 slice.102
  827.1 0.8 slice_bitcast_fusion
  827.9 0.7 copy.121
  828.5 0.7 copy.120
  829.2 2.8 fusion.25
  832.0 5.7 shard_map.172
  837.7 1.1 copy.157
  838.9 0.8 copy.158
  839.7 3.4 copy.159
  (136 shorter events, 5.5 us)
Async XLA Ops:
  7.2 4.1 copy-start.25
  7.2 4.8 copy-start.31
  7.2 4.8 copy-start.33
  7.2 334.1 %all-gather.2.cloned.1.call-start = ((), (), s32[]{:S(2)}) async-start(), calls=%async_computation | async-start | bytes 17301504 | tf_op jit(solution)/shard_map/all_gather | solution.py:1286
  106.4 3.5 copy-start.6
  106.4 4.5 copy-start.29
  109.9 1.9 copy-start.34
  110.9 4.5 copy-start.17
  115.4 13.4 %copy-start.2 = (f32[1024,768]{0,1:T(8,128)}, f32[1024,768]{0,1:T(8,128)S(1)}, u32[]{:S(2)}) copy-start(f32[1024,768]{0,1:T(8,128)S(1)} %fusion.54) | copy-start | bytes 9437188
  129.3 6.6 copy-start.20
  129.3 6.6 copy-start.26
  140.0 17.0 %copy-start.32 = (s32[128,8]{0,1:T(8,128)S(1)}, s32[128,8]{0,1:T(8,128)}, u32[]{:S(2)}) copy-start(s32[128,8]{0,1:T(8,128)} %param.13) | copy-start | bytes 12292
  140.0 17.1 %copy-start.7 = (bf16[128,2048]{1,0:T(8,128)(2,1)S(1)}, bf16[128,2048]{1,0:T(8,128)(2,1)}, u32[]{:S(2)}) copy-start(bf16[128,2048]{1,0:T(8,128)(2,1)} %x_ref.1) | copy-start | bytes 1572868
  157.1 5.5 copy-start.9
  157.1 5.6 copy-start.16
  162.7 1.3 copy-start.13
  469.8 154.2 %copy-start.19 = (bf16[128,2048]{1,0:T(8,128)(2,1)S(1)}, bf16[128,2048]{1,0:T(8,128)(2,1)}, u32[]{:S(2)}) copy-start(bf16[128,2048]{1,0:T(8,128)(2,1)} %param.11) | copy-start | bytes 1572868
  620.6 3.4 copy-start.23
  625.5 1.0 copy-start.4
  632.7 13.8 %copy-start.27 = (bf16[1024,256]{0,1:T(8,128)(2,1)S(1)}, bf16[1024,256]{0,1:T(8,128)(2,1)}, u32[]{:S(2)}) copy-start(bf16[1024,256]{0,1:T(8,128)(2,1)} %slice.172) | copy-start | bytes 1572868
  646.6 12.0 %slice-start = ((s8[8388608]{0:T(1024)(128)(4,1)}), s8[4194304]{0:T(1024)(128)(4,1)S(1)}, s32[]{:S(2)}) async-start(s8[8388608]{0:T(1024)(128)(4,1)} %bitcast.202), calls=%async_computation.1 | async-start | bytes 8388608
  651.5 4.8 copy-start.21
  651.5 7.1 slice-start.1
  658.6 2.3 copy-start.24
  660.9 2.3 copy-start.3
  661.4 2.5 copy-start.11
  663.2 1.0 copy-start.12
  672.1 2.8 copy-start.18
  672.1 2.9 copy-start.36
  675.0 4.9 copy-start.35
  680.0 3.7 copy-start.14
  680.0 3.9 copy-start.5
  680.0 3.9 copy-start.10
  689.7 43.8 %copy-start.8 = (bf16[128,2048]{1,0:T(8,128)(2,1)S(1)}, bf16[128,2048]{1,0:T(8,128)(2,1)}, u32[]{:S(2)}) copy-start(bf16[128,2048]{1,0:T(8,128)(2,1)} %x_ref.1) | copy-start | bytes 1572868
  689.7 43.8 %copy-start.30 = (f32[1,2048]{1,0:T(1,128)S(1)}, f32[1,2048]{1,0:T(1,128)}, u32[]{:S(2)}) copy-start(f32[1,2048]{1,0:T(1,128)} %copy-done.29) | copy-start | bytes 24580
  826.1 5.9 copy-start
  826.1 5.9 copy-start.1
  829.2 8.5 %copy-start.22 = (f32[3,64,2048]{2,1,0:T(8,128)S(1)}, f32[3,64,2048]{2,1,0:T(8,128)}, u32[]{:S(2)}) copy-start(f32[3,64,2048]{2,1,0:T(8,128)} %get-tuple-element.172) | copy-start | bytes 4718596
  832.0 6.9 copy-start.28
  832.0 7.7 copy-start.15
Sparse Core Ops, SparseCore 0:
  125.5 194.7 all-gather.1
